TPU v7x, 128 devices: a whole 4x4x4 slice. The times are simulated.
128 devices in a mesh: dp: 16 (over y, x_lo, core), fsdp: 8 (over z, x_hi).
Axes of the slice: x: 4 (x_hi: 2, x_lo: 2; x = x_hi * 2 + x_lo), y: 4, z: 4, core: 2. Of those that a mesh axis runs over, the one named last changes fastest.
Arguments:
- q_policy: bfloat16 [32768, 2560], P(('dp', 'fsdp')), may hold values from -288 to 288
- kv_policy: bfloat16 [32768, 1024], P(('dp', 'fsdp')), may hold values from -72 to 72
- q_reference: bfloat16 [32768, 2560], P(('dp', 'fsdp')), may hold values from -288 to 288
- kv_reference: bfloat16 [32768, 1024], P(('dp', 'fsdp')), may hold values from -6 to 6
- target: bfloat16 [32768, 2560], P(('dp', 'fsdp')), may hold values from -4 to 4
- send_slot: int32 [128, 256], P(('dp', 'fsdp')), may hold values from 0 to 255, each once within a row
- lengths: int32 [128, 2], P(('dp', 'fsdp')), may hold values from 1 to 192, 256 in all within a row
- rewards: float32 [256], P(('dp', 'fsdp')), may hold values from -6 to 6
- group_ids: int32 [256], P(('dp', 'fsdp')), may hold values from 0 to 31, as said below
- policy_weight: bfloat16 [2560, 2560], P('fsdp'), may hold values from -6 to 6
- ema_weight: float32 [2560, 2560], P('fsdp'), may hold values from -6 to 6
Outputs:
- update: float32 [2560, 2560], P('fsdp')
- new_weights: bfloat16 [2560, 2560], P('fsdp')
- ema_next: float32 [2560, 2560], P('fsdp')
Inputs may be any that keep to these rules, and one draw needn't show every extreme that they name: `send_slot`: each row is a permutation of 0 to 255. Each device's 2 lengths sum to 256. `group_ids`: each prompt names exactly 8 rollouts.
All inputs are finite; a program needn't handle non-finite values.
Results may differ from a plain program's by a relative error of at most 0.02.
Values may be sent and summed in bfloat16 or wider, within the bound.
No kernel may reach another device: no remote copies, remote signals or barrier semaphores. Data moves between devices by JAX's collectives and lax.ppermute only.
A program may use at most 128 MiB of HBM per device.

v0:
```python
import math

import jax
import jax.numpy as jnp
from jax import lax
from jax.sharding import PartitionSpec as P

HEADS = 20
KV_HEADS = 4
HEAD_DIM = 128
D_OUT = 2560
GROUP = 8
Q_WIDTH = 2560


kl_weight = 0.1
step_size = 0.02
ema_decay = 0.95
std_floor = 0.6
norm_epsilon = 1e-06


def row_layout(lengths_local, row_count):
    places = jnp.arange(row_count, dtype=jnp.int32)
    bounds = jnp.cumsum(lengths_local)
    segment = jnp.sum((places[:, None] >= bounds[None, :]).astype(jnp.int32), axis=1)
    choose = segment[:, None] == jnp.arange(lengths_local.shape[0], dtype=jnp.int32)[None, :]
    return (segment, choose)


def attend(queries, keys_values, segment):
    row_count = queries.shape[0]
    group_size = HEADS // KV_HEADS
    group_width = group_size * HEAD_DIM
    split_at = KV_HEADS * HEAD_DIM
    places = jnp.arange(row_count, dtype=jnp.int32)
    allowed = (places[None, :] <= places[:, None]) & (segment[None, :] == segment[:, None])

    def one_group(head):
        grouped = lax.dynamic_slice_in_dim(queries, head * group_width, group_width, 1)
        grouped = grouped.reshape(row_count, group_size, HEAD_DIM)
        key_rows = lax.dynamic_slice_in_dim(keys_values, head * HEAD_DIM, HEAD_DIM, 1)
        value_rows = lax.dynamic_slice_in_dim(keys_values, split_at + head * HEAD_DIM, HEAD_DIM, 1)
        scores = jnp.einsum(
            "qgd,kd->gqk", grouped, key_rows, preferred_element_type=jnp.float32
        ) / math.sqrt(HEAD_DIM)
        masked = jnp.where(allowed[None, :, :], scores, -1e30)
        row_peak = jnp.max(masked, axis=-1, keepdims=True)
        weights = jnp.where(allowed[None, :, :], jnp.exp(masked - row_peak), 0.0)
        totals = jnp.sum(weights, axis=-1, keepdims=True)
        shares = (weights / totals).astype(jnp.bfloat16)
        mixture = jnp.einsum("gqk,kd->qgd", shares, value_rows, preferred_element_type=jnp.float32)
        return mixture.reshape(row_count, group_width).astype(jnp.bfloat16)

    blocks = lax.map(one_group, jnp.arange(KV_HEADS, dtype=jnp.int32))
    return blocks.transpose(1, 0, 2).reshape(row_count, HEADS * HEAD_DIM)


def advantage_from(rewards, member, first, second):
    center = first / GROUP
    spread = jnp.maximum(jnp.sqrt(jnp.maximum(second / GROUP - center * center, 0.0)), std_floor)
    shifted = rewards - jnp.dot(member, center, precision=lax.Precision.HIGHEST)
    return shifted / jnp.dot(member, spread, precision=lax.Precision.HIGHEST)


def normalize(rows):
    scale = jnp.sqrt(jnp.mean(rows * rows, axis=1, keepdims=True) + norm_epsilon)
    return (rows / scale, scale)


def token_gradient(y_policy, y_reference, target_rows, choose, lengths_local, advantage_local):
    row_length = jnp.sum(jnp.where(choose, lengths_local[None, :], 0), axis=1).astype(jnp.float32)
    row_advantage = jnp.sum(jnp.where(choose, advantage_local[None, :], 0.0), axis=1)
    h_policy, norm_policy = normalize(y_policy)
    h_reference, norm_reference = normalize(y_reference)
    target_float = target_rows.astype(jnp.float32)
    gap_policy = h_policy - target_float
    gap_reference = h_reference - target_float
    log_factor = 1.0 / (4.0 * math.sqrt(target_rows.shape[1]))
    log_policy = -jnp.sum(gap_policy * gap_policy, axis=1) * log_factor
    log_reference = -jnp.sum(gap_reference * gap_reference, axis=1) * log_factor
    weight_rows = (
        row_advantage - kl_weight * (1.0 - jnp.exp(log_reference - log_policy))
    ) / row_length
    along = jnp.mean(gap_policy * h_policy, axis=1, keepdims=True)
    grad = weight_rows[:, None] * (gap_policy - h_policy * along) / norm_policy
    return grad.astype(jnp.bfloat16)


def fold_rows(source, row_piece):
    return jnp.dot(source, row_piece, preferred_element_type=jnp.float32)


def local(
    q_policy,
    kv_policy,
    q_reference,
    kv_reference,
    target,
    send_slot,
    lengths,
    rewards,
    group_ids,
    policy_weight,
    ema_weight,
):
    row_count = q_policy.shape[0]
    places = jnp.arange(row_count, dtype=jnp.int32)
    inverse = jnp.zeros((row_count,), jnp.int32).at[send_slot[0]].set(places)
    query_policy, pairs_policy, query_reference, pairs_reference, target_rows = (
        lax.all_to_all(q_policy[inverse], "dp", split_axis=0, concat_axis=0, tiled=True),
        lax.all_to_all(kv_policy[inverse], "dp", split_axis=0, concat_axis=0, tiled=True),
        lax.all_to_all(q_reference[inverse], "dp", split_axis=0, concat_axis=0, tiled=True),
        lax.all_to_all(kv_reference[inverse], "dp", split_axis=0, concat_axis=0, tiled=True),
        lax.all_to_all(target[inverse], "dp", split_axis=0, concat_axis=0, tiled=True),
    )
    total_groups = rewards.shape[0] * lax.axis_size("dp") * lax.axis_size("fsdp") // GROUP
    member = (group_ids[:, None] == jnp.arange(total_groups, dtype=jnp.int32)[None, :]).astype(
        jnp.float32
    )
    first, second = lax.psum(
        (
            jnp.dot(rewards, member, precision=lax.Precision.HIGHEST),
            jnp.dot(rewards * rewards, member, precision=lax.Precision.HIGHEST),
        ),
        ("dp", "fsdp"),
    )
    advantage_local = advantage_from(rewards, member, first, second)
    lengths_local = lengths[0]
    segment, choose = row_layout(lengths_local, row_count)
    out_policy = attend(query_policy, pairs_policy, segment)
    out_reference = attend(query_reference, pairs_reference, segment)
    ema_half = ema_weight.astype(jnp.bfloat16)
    y_policy = fold_rows(out_policy, lax.all_gather(policy_weight, "fsdp", axis=0, tiled=True))
    y_reference = fold_rows(out_reference, lax.all_gather(ema_half, "fsdp", axis=0, tiled=True))
    grad_rows = token_gradient(
        y_policy, y_reference, target_rows, choose, lengths_local, advantage_local
    )
    grad_share = lax.psum_scatter(
        lax.dot_general(
            out_policy, grad_rows, (((0,), (0,)), ((), ())), preferred_element_type=jnp.float32
        ).astype(jnp.bfloat16),
        "fsdp",
        scatter_dimension=0,
        tiled=True,
    )
    grad_total = lax.psum(grad_share, "dp").astype(jnp.float32)
    square_sum = lax.psum(jnp.sum(grad_total * grad_total), "fsdp")
    update = grad_total / jnp.sqrt(square_sum / (Q_WIDTH * D_OUT) + norm_epsilon)
    moved = policy_weight.astype(jnp.float32) - step_size * update
    return (update, moved.astype(jnp.bfloat16), ema_decay * ema_weight + (1.0 - ema_decay) * moved)


def solution(mesh):
    in_specs = (
        P(("dp", "fsdp"), None),
        P(("dp", "fsdp"), None),
        P(("dp", "fsdp"), None),
        P(("dp", "fsdp"), None),
        P(("dp", "fsdp"), None),
        P(("dp", "fsdp"), None),
        P(("dp", "fsdp"), None),
        P(("dp", "fsdp")),
        P(("dp", "fsdp")),
        P("fsdp", None),
        P("fsdp", None),
    )
    out_specs = (P("fsdp", None), P("fsdp", None), P("fsdp", None))
    return jax.shard_map(local, mesh=mesh, in_specs=in_specs, out_specs=out_specs, check_vma=False)
```

profile of v0, /device:TPU:0, one launch (start us, length us, event | category | flops | bytes accessed | tf_op | source)
XLA Modules:
  0.0 688.1 jit_solution(1774460681990765302)
XLA Ops:
  8.0 3.3 convert_element_type.86
  15.3 5.7 all-to-all-start
  23.0 12.4 %all-to-all-done = bf16[16,16,1024]{2,1,0:T(8,128)(2,1)S(1)} async-done(((bf16[16,16,1024]{2,1,0:T(8,128)(2,1)}), bf16[16,16,1024]{2,1,0:T(8,128)(2,1)S(1)}, u32[]{:S(2)}, u32[]{:S(2)}) %all-to-all-start) | async-done | bytes 524320 | tf_op jit(solution)/shard_map/all_to_all | solution.py:112
  35.4 3.6 all-to-all-start.2
  39.0 2.5 gather_fusion.1
  41.5 13.5 %all-to-all-done.2 = bf16[16,16,1024]{2,1,0:T(8,128)(2,1)S(1)} async-done(((bf16[16,16,1024]{2,1,0:T(8,128)(2,1)}), bf16[16,16,1024]{2,1,0:T(8,128)(2,1)S(1)}, u32[]{:S(2)}, u32[]{:S(2)}) %all-to-all-start.2) | async-done | bytes 524320 | tf_op jit(solution)/shard_map/all_to_all | solution.py:114
  55.1 4.5 all-to-all-start.1
  60.0 149.8 %all-reduce = (f32[32]{0:T(128)S(1)}, f32[32]{0:T(128)S(1)}) all-reduce(f32[32]{0:T(128)S(1)} %convolution_bitcast_fusion.1, f32[32]{0:T(128)S(1)} %convolution_bitcast_fusion.3), channel_id=1, replica_groups=mesh['dp'=16,'fsdp'=8] {'dp','fsdp'}, use_global_device_ids=true, to_apply=%region_8.9 | all-reduce | flops 64 | bytes 512 | tf_op jit(solution)/shard_map/psum | solution.py:121
  210.0 2.5 gather_fusion.3
  212.5 2.5 gather_fusion.4
  215.7 4.4 all-to-all-start.3
  221.2 29.9 %while.26 = (s32[]{:T(128)}, bf16[4,256,640]{1,2,0:T(8,128)(2,1)}, s32[4]{0:T(128)S(1)}, bf16[256,1024]{1,0:T(8,128)(2,1)S(1)}, bf16[256,2560]{1,0:T(8,128)(2,1)...) while((s32[]{:T(128)}, bf16[4,256,640]{1,2,0:T(8,128)(2,1)}, ...), condition=%wide.region_6.7_spmd.clone, body=%wide.region_3.6_spmd.clone.sunk | while | flops 170426624 | bytes 6634279 | solution.py:55
  251.1 5.6 all-to-all-start.4
  257.1 27.0 %while.27 = (s32[]{:T(128)}, bf16[4,256,640]{1,2,0:T(8,128)(2,1)S(1)}, s32[4]{0:T(128)S(1)}, bf16[256,1024]{1,0:T(8,128)(2,1)S(1)}, bf16[256,2560]{1,0:T(8,128)(...) while((s32[]{:T(128)}, ...), condition=%wide.region_13.14_spmd.clone, body=%wide.region_10.13_spmd.clone.sunk | while | flops 170426624 | bytes 6633771 | solution.py:55
  284.2 10.2 %multiply_reduce_fusion.2 = (f32[256]{0:T(256)S(1)}, f32[256,2560]{1,0:T(8,128)}) fusion(bf16[256,2560]{0,1:T(8,128)(2,1)} %bitcast.9, bf16[2560,2560]{1,0:T(8,128)(2,1)} %all-gather.5.cloned.1.call-done), kind=kOutput, calls=%fused_computation.71 | convolution fusion | flops 3356753664 | bytes 17040384 | tf_op jit(solution)/shard_map/dot_general | solution.py:91
  294.4 49.9 %all-gather.3.cloned.1.call-done = bf16[2560,2560]{1,0:T(8,128)(2,1)} async-done(((bf16[320,2560]{1,0:T(8,128)(2,1)}), bf16[2560,2560]{1,0:T(8,128)(2,1)}) %all-gather.3.cloned.1.call-update) | async-done | bytes 13107216 | tf_op jit(solution)/shard_map/all_gather | solution.py:135
  344.4 9.8 %multiply_reduce_fusion.3 = (f32[256]{0:T(256)S(1)}, f32[256,2560]{1,0:T(8,128)}) fusion(bf16[256,2560]{0,1:T(8,128)(2,1)S(1)} %bitcast.153, bf16[2560,2560]{1,0:T(8,128)(2,1)} %all-gather.3.cloned.1.call-done), kind=kOutput, calls=%fused_computation.72 | convolution fusion | flops 3356753664 | bytes 17040384 | tf_op jit(solution)/shard_map/dot_general | solution.py:91
  354.2 4.3 multiply_reduce_fusion.1
  358.5 10.2 %convolution_convert_fusion.2 = bf16[2560,2560]{1,0:T(8,128)(2,1)} fusion(bf16[256,2560]{0,1:T(8,128)(2,1)} %bitcast.9, bf16[256,2560]{1,0:T(8,128)(2,1)} %bitcast.27, f32[256]{0:T(256)S(1)} %get-tuple-element.253, f32[256]{0:T(256)S(1)} %get-tuple-element.252, f32[256]{0:T(256)S(1)} %add_sqrt_fusion, f32[256,2560]{1,0:T(8,128)S(1)} %copy-done.10), kind=kOutput, calls=%fused_computation.58 | convolution fusion | flops 3367239680 | bytes 18353152 | tf_op jit(solution)/shard_map/dot_general | solution.py:140
  368.9 155.0 %reduce-scatter.2.cloned.1.call-done = bf16[320,2560]{1,0:T(8,128)(2,1)} async-done(((bf16[2560,2560]{1,0:T(8,128)(2,1)}), bf16[320,2560]{1,0:T(8,128)(2,1)}) %reduce-scatter.2.cloned.1.call-update) | async-done | bytes 1638416 | tf_op jit(solution)/shard_map/reduce_scatter | solution.py:139
  523.9 121.8 %all-reduce.3.cloned.1.call-done = bf16[320,2560]{1,0:T(8,128)(2,1)} async-done(((bf16[320,2560]{1,0:T(8,128)(2,1)}), bf16[320,2560]{1,0:T(8,128)(2,1)}) %all-reduce.3.cloned.1.call-update) | async-done | bytes 1638416 | tf_op jit(solution)/shard_map/psum | solution.py:147
  645.7 3.0 fusion.52
  648.7 25.3 %psum.31 = f32[]{:T(128)} all-reduce(f32[]{:T(128)} %fusion.52), channel_id=1, replica_groups=mesh['dp'=16,'fsdp'=8] {'fsdp'}, use_global_device_ids=true, to_apply=%region_23.24 | all-reduce | flops 1 | bytes 8 | tf_op jit(solution)/shard_map/psum | solution.py:148
  674.8 4.5 multiply_add_fusion
  (131 shorter events, 58.0 us)
Async XLA Ops:
  7.2 31.9 %copy-start = (bf16[256,2560]{1,0:T(8,128)(2,1)S(1)}, bf16[256,2560]{1,0:T(8,128)(2,1)}, u32[]{:S(2)}) copy-start(bf16[256,2560]{1,0:T(8,128)(2,1)} %param.15) | copy-start | bytes 3932164
  7.2 277.0 %all-gather.5.cloned.1.call-start = ((), (), s32[]{:S(2)}) async-start(), calls=%async_computation.7 | async-start | bytes 14745600 | tf_op jit(solution)/shard_map/all_gather | solution.py:134
  7.9 336.4 %all-gather.3.cloned.1.call-start = ((), (), s32[]{:S(2)}) async-start(), calls=%async_computation.6 | async-start | bytes 14745600 | tf_op jit(solution)/shard_map/all_gather | solution.py:135
  11.2 2.1 copy-start.4
  15.3 5.7 copy-start.5
  15.3 20.1 %all-to-all-start = ((bf16[16,16,1024]{2,1,0:T(8,128)(2,1)}), bf16[16,16,1024]{2,1,0:T(8,128)(2,1)S(1)}, u32[]{:S(2)}, u32[]{:S(2)}) async-start(bf16[16,16,1024]{2,1,0:T(8,128)(2,1)} %bitcast.2), calls=%async_computation | async-start | bytes 1048576 | tf_op jit(solution)/shard_map/all_to_all | solution.py:112
  35.4 6.1 copy-start.6
  35.4 19.6 %all-to-all-start.2 = ((bf16[16,16,1024]{2,1,0:T(8,128)(2,1)}), bf16[16,16,1024]{2,1,0:T(8,128)(2,1)S(1)}, u32[]{:S(2)}, u32[]{:S(2)}) async-start(bf16[16,16,1024]{2,1,0:T(8,128)(2,1)} %bitcast.18), calls=%async_computation.2 | async-start | bytes 1048576 | tf_op jit(solution)/shard_map/all_to_all | solution.py:114
  55.1 4.6 copy-start.14
  55.1 4.6 copy-start.15
  55.1 154.8 %copy-start.13 = (s32[1,2]{1,0:T(1,128)S(1)}, s32[1,2]{1,0:T(1,128)}, u32[]{:S(2)}) copy-start(s32[1,2]{1,0:T(1,128)} %param.21) | copy-start | bytes 28
  55.1 154.9 %copy-start.2 = (bf16[256,2560]{1,0:T(8,128)(2,1)S(1)}, bf16[256,2560]{1,0:T(8,128)(2,1)}, u32[]{:S(2)}) copy-start(bf16[256,2560]{1,0:T(8,128)(2,1)} %param.17) | copy-start | bytes 3932164
  55.1 160.6 %all-to-all-start.1 = ((bf16[16,16,2560]{2,1,0:T(8,128)(2,1)}), bf16[16,16,2560]{2,1,0:T(8,128)(2,1)}, u32[]{:S(2)}, u32[]{:S(2)}) async-start(bf16[16,16,2560]{2,1,0:T(8,128)(2,1)} %bitcast.155), calls=%async_computation.1 | async-start | bytes 2621440 | tf_op jit(solution)/shard_map/all_to_all | solution.py:111
  210.0 2.5 copy-start.3
  215.7 35.5 %all-to-all-start.3 = ((bf16[16,16,2560]{2,1,0:T(8,128)(2,1)}), bf16[16,16,2560]{2,1,0:T(8,128)(2,1)}, u32[]{:S(2)}, u32[]{:S(2)}) async-start(bf16[16,16,2560]{2,1,0:T(8,128)(2,1)} %bitcast.20), calls=%async_computation.3 | async-start | bytes 2621440 | tf_op jit(solution)/shard_map/all_to_all | solution.py:113
  220.1 1.2 copy-start.7
  251.1 103.0 %all-to-all-start.4 = ((bf16[16,16,2560]{2,1,0:T(8,128)(2,1)}), bf16[16,16,2560]{2,1,0:T(8,128)(2,1)}, u32[]{:S(2)}, u32[]{:S(2)}) async-start(bf16[16,16,2560]{2,1,0:T(8,128)(2,1)} %bitcast.154), calls=%async_computation.4 | async-start | bytes 2621440 | tf_op jit(solution)/shard_map/all_to_all | solution.py:115
  256.8 267.1 %reduce-scatter.2.cloned.1.call-start = ((), (), s32[]{:S(2)}) async-start(), calls=%async_computation.8 | async-start | bytes 14745600 | tf_op jit(solution)/shard_map/reduce_scatter | solution.py:139
  354.2 4.4 copy-start.10
  368.8 276.9 %all-reduce.3.cloned.1.call-start = ((), (), s32[]{:S(2)}) async-start(), calls=%async_computation.9 | async-start | bytes 3276800 | tf_op jit(solution)/shard_map/psum | solution.py:147
  523.9 150.9 %copy-start.8 = (bf16[320,2560]{1,0:T(8,128)(2,1)S(1)}, bf16[320,2560]{1,0:T(8,128)(2,1)}, u32[]{:S(2)}) copy-start(bf16[320,2560]{1,0:T(8,128)(2,1)} %param.24) | copy-start | bytes 4915204
  645.7 29.1 %copy-start.11 = (bf16[320,2560]{1,0:T(8,128)(2,1)S(1)}, bf16[320,2560]{1,0:T(8,128)(2,1)}, u32[]{:S(2)}) copy-start(bf16[320,2560]{1,0:T(8,128)(2,1)} %all-reduce.3.cloned.1.call-done) | copy-start | bytes 4915204
  679.3 2.2 copy-start.9
  679.3 2.3 copy-start.1
  (1 other events, 0.7 us)
Sparse Core Ops, SparseCore 0:
  10.3 163.0 all-gather.4
  176.3 168.0 all-gather.2
  368.9 154.8 reduce-scatter.1
  526.3 119.4 all-reduce.2
where the time goes:
time: 690 us; the launch traced here: 688 us
  waiting for transfers between devices  353 us (51%)
  blocking collectives  175 us (25%)
  matrix products  57.4 us (8%)
  local copies, waits for them, and re-layouts  34.3 us (5%)
  starting transfers between devices  24.2 us (4%)
  other arithmetic  18.1 us (3%)
  between operations  14.7 us (2%)
  loops' own time  10.8 us (2%)
    reduce_scatter x1, waiting for transfers between devices, local(): lax.psum_scatter(lax.dot_general(out_policy, grad_rows, (((0,), (0,)), ((...  155 us
    psum x1, blocking collectives, local(): lax.psum((jnp.dot(rewards, member, precision=lax.Precision.HIGHEST), jnp....  150 us
    psum x1, waiting for transfers between devices, local(): grad_total = lax.psum(grad_share, 'dp').astype(jnp.float32)  122 us
    all_gather x1, waiting for transfers between devices, local(): lax.all_gather(ema_half, 'fsdp', axis=0, tiled=True)  49.9 us
    psum x1, blocking collectives, local(): square_sum = lax.psum(jnp.sum(grad_total * grad_total), 'fsdp')  25.3 us
    dot_general x2, matrix products, fold_rows(): return jnp.dot(source, row_piece, preferred_element_type=jnp.float32)  20 us
  transfers between devices with their start and end apart: 9, of which 5 were waited for; matrix products, arithmetic and copies ran while one was open for 12% of the time, Pallas kernels for 0%

commit v1 on v0

v1 whole, which is shorter than its diff:
```python
import functools
import math

import jax
import jax.numpy as jnp
from jax import lax
from jax.experimental import pallas as pl
from jax.experimental.pallas import tpu as pltpu
from jax.sharding import Mesh
from jax.sharding import PartitionSpec as P

HEADS = 20
KV_HEADS = 4
HEAD_DIM = 128
D_OUT = 2560
GROUP = 8
Q_WIDTH = 2560
ROWS = 256
SPAN = 16
SHARD = 320
HALF = 1280
CHUNK = 256
PIECE = 640

kl_weight = 0.1
step_size = 0.02
ema_decay = 0.95
std_floor = 0.6
norm_epsilon = 1e-06

bf16 = jnp.bfloat16
f32 = jnp.float32
VMEM = pltpu.VMEM
SMEM = pltpu.SMEM
BIG = pltpu.CompilerParams(vmem_limit_bytes=56 * 1024 * 1024)

DP = ("y", "xl", "c")
FSDP = ("z", "xh")
EVERY = DP + FSDP


def ring(step):
    return [(i, (i + step) % 4) for i in range(4)]


FLIP = [(0, 1), (1, 0)]
ACROSS = [(2, 1), (1, 2), (0, 3), (3, 0)]


def whole(shape=None):
    return pl.BlockSpec(memory_space=VMEM)


def scalars():
    return pl.BlockSpec(memory_space=SMEM)


def in_place():
    return pl.BlockSpec(memory_space=pl.ANY)


def dot(a, b):
    return jnp.dot(a, b, preferred_element_type=f32)


def one_hot_rows(slots_ref):
    return (lax.broadcasted_iota(jnp.int32, (ROWS, ROWS), 0) == slots_ref[...]).astype(bf16)


def pack_policy_kernel(slots_ref, q_ref, kv_ref, out_ref):
    pick = one_hot_rows(slots_ref)
    out_ref[:, :Q_WIDTH] = dot(pick, q_ref[...]).astype(bf16)
    out_ref[:, Q_WIDTH:] = dot(pick, kv_ref[...]).astype(bf16)


def pack_reference_kernel(slots_ref, q_ref, kv_ref, target_ref, facts_ref, out_ref):
    pick = one_hot_rows(slots_ref)
    rows = dot(pick, target_ref[...]).astype(bf16)
    for pair in range(ROWS // (2 * SPAN)):
        top = pair * 2 * SPAN
        first, second = rows[top : top + SPAN], rows[top + SPAN : top + 2 * SPAN]
        out_ref[top : top + SPAN, :HALF] = first[:, :HALF]
        out_ref[top : top + SPAN, HALF:D_OUT] = second[:, :HALF]
        out_ref[top + SPAN : top + 2 * SPAN, :HALF] = first[:, HALF:]
        out_ref[top + SPAN : top + 2 * SPAN, HALF:D_OUT] = second[:, HALF:]
    out_ref[:, D_OUT : D_OUT + Q_WIDTH] = dot(pick, q_ref[...]).astype(bf16)
    out_ref[:, D_OUT + Q_WIDTH : D_OUT + Q_WIDTH + 1024] = dot(pick, kv_ref[...]).astype(bf16)
    facts = facts_ref[...]
    high = facts.astype(bf16).astype(f32)
    middle = (facts - high).astype(bf16).astype(f32)
    low = facts - high - middle
    lane = lax.broadcasted_iota(jnp.int32, facts.shape, 1)
    coded = jnp.where(lane < 8, high, jnp.where(lane < 16, middle, low)).astype(bf16)
    for block in range(ROWS // SPAN):
        out_ref[block * SPAN : (block + 1) * SPAN, D_OUT + Q_WIDTH + 1024 :] = coded


def attention_kernel(lengths_ref, q_ref, k_ref, v_ref, out_ref):
    row = lax.broadcasted_iota(jnp.int32, (ROWS, ROWS), 0)
    column = lax.broadcasted_iota(jnp.int32, (ROWS, ROWS), 1)
    bound = lengths_ref[0, 0]
    allowed = (column <= row) & ((column >= bound) | (row < bound))
    keys, values = k_ref[...], v_ref[...]
    for head in range(HEADS // KV_HEADS):
        lanes = slice(head * HEAD_DIM, (head + 1) * HEAD_DIM)
        scores = lax.dot_general(
            q_ref[:, lanes], keys, (((1,), (1,)), ((), ())), preferred_element_type=f32
        ) * (1.0 / math.sqrt(HEAD_DIM))
        scores = jnp.where(allowed, scores, -1e30)
        weights = jnp.exp(scores - jnp.max(scores, axis=1, keepdims=True))
        shares = (weights / jnp.sum(weights, axis=1, keepdims=True)).astype(bf16)
        out_ref[:, lanes] = dot(shares, values).astype(bf16)


def attend(rows, lengths, q_at, k_at, v_at):
    width = Q_WIDTH // KV_HEADS
    return pl.pallas_call(
        attention_kernel,
        grid=(KV_HEADS,),
        in_specs=[
            scalars(),
            pl.BlockSpec((ROWS, width), lambda g: (0, q_at // width + g)),
            pl.BlockSpec((ROWS, HEAD_DIM), lambda g: (0, k_at // HEAD_DIM + g)),
            pl.BlockSpec((ROWS, HEAD_DIM), lambda g: (0, v_at // HEAD_DIM + g)),
        ],
        out_specs=pl.BlockSpec((ROWS, width), lambda g: (0, g)),
        out_shape=jax.ShapeDtypeStruct((ROWS, Q_WIDTH), bf16),
        compiler_params=BIG,
        cost_estimate=pl.CostEstimate(
            flops=4 * HEADS * ROWS * ROWS * HEAD_DIM, bytes_accessed=4 << 20, transcendentals=HEADS * ROWS * ROWS
        ),
    )(lengths, rows, rows, rows)


def advantage_kernel(place_ref, facts_ref, out_ref):
    coded = facts_ref[...].astype(f32)
    facts = coded + pltpu.roll(coded, 128 - 8, 1) + pltpu.roll(coded, 128 - 16, 1)
    row = lax.broadcasted_iota(jnp.int32, (ROWS, 128), 0)
    lane = lax.broadcasted_iota(jnp.int32, (ROWS, 128), 1)
    ids = pltpu.roll(facts, 128 - 2, 1)
    counted = (row % SPAN < 8) & (lane < 2)
    own = place_ref[0] * 4 + place_ref[1] * 2 + place_ref[2]
    other = place_ref[0] * 4 + place_ref[1] * 2 + 1 - place_ref[2]

    def fact(device, at):
        return jnp.sum(jnp.where((row == device * SPAN) & (lane == at), facts, 0.0))

    for j in range(4):
        device, mine = (own, other)[j // 2], j % 2
        reward, group = fact(device, mine), fact(device, 2 + mine)
        held = jnp.where(counted & (ids == group), facts, 0.0)
        center = jnp.sum(held, keepdims=True) / GROUP
        second = jnp.sum(held * held, keepdims=True) / GROUP
        spread = jnp.maximum(jnp.sqrt(jnp.maximum(second - center * center, 0.0)), std_floor)
        out_ref[j : j + 1, :] = jnp.broadcast_to((reward - center) / spread, (1, 128))
        out_ref[4 + j : 5 + j, :] = jnp.full((1, 128), fact(device, 4 + mine), f32)


def project_kernel(
    place_ref, own_p, other_p, own_r, other_r, target_ref,
    w0, sm, sp, s2p, s2e, o0, om, op, o2p, o2e,
    y_ref, stats_ref, rows_p, rows_r, weight_p, weight_r, sems,
):
    c, z, xh = place_ref[2], place_ref[3], place_ref[4]

    def load(source, first, weight, dz, side, sem):
        shard = lax.rem(z + 4 + dz, 4) * 2 + side
        at = pl.multiple_of(shard * SHARD, 64)
        return pltpu.make_async_copy(
            source.at[pl.ds(first, SHARD), :], weight.at[pl.ds(at, SHARD), :], sem
        )

    here, there = xh, 1 - xh
    copies_p = [
        pltpu.make_async_copy(own_p, rows_p.at[pl.ds(0, ROWS), :], sems.at[0]),
        pltpu.make_async_copy(other_p, rows_p.at[pl.ds(ROWS, ROWS), :], sems.at[0]),
    ]
    copies_r = [
        pltpu.make_async_copy(own_r, rows_r.at[pl.ds(0, ROWS), :], sems.at[1]),
        pltpu.make_async_copy(other_r, rows_r.at[pl.ds(ROWS, ROWS), :], sems.at[1]),
    ]
    for block, dz, side in ((w0, 0, here), (sm, -1, here), (sp, 1, here), (o0, 0, there), (om, -1, there), (op, 1, there)):
        copies_p.append(load(block, 0, weight_p, dz, side, sems.at[0]))
        copies_r.append(load(block, SHARD, weight_r, dz, side, sems.at[1]))
    for block, side in ((s2p, here), (o2p, there)):
        copies_p.append(load(block, 0, weight_p, 2, side, sems.at[0]))
    for block, side in ((s2e, here), (o2e, there)):
        copies_r.append(load(block, 0, weight_r, 2, side, sems.at[1]))
    for copy in copies_p + copies_r:
        copy.start()

    def lanes_of(value):
        total = value[:, :128]
        for k in range(1, value.shape[1] // 128):
            total = total + value[:, k * 128 : (k + 1) * 128]
        return total

    def run(rows, weight, keep):
        def step(j, sums):
            squares, products = sums
            at = pl.multiple_of(j * CHUNK, CHUNK)
            y = dot(rows[...], weight[:, pl.ds(at, CHUNK)])
            if keep:
                y_ref[:, pl.ds(at, CHUNK)] = y
            mine = target_ref[:, pl.ds(pl.multiple_of(c * HALF + at, 128), CHUNK)]
            theirs = target_ref[:, pl.ds(pl.multiple_of((1 - c) * HALF + at, 128), CHUNK)]
            target = jnp.concatenate([mine, theirs], axis=0).astype(f32)
            return squares + lanes_of(y * y), products + lanes_of(y * target)

        zero = jnp.zeros((2 * ROWS, 128), f32)
        squares, products = lax.fori_loop(0, HALF // CHUNK, step, (zero, zero))
        return jnp.sum(squares, axis=1, keepdims=True), jnp.sum(products, axis=1, keepdims=True)

    for copy in copies_p:
        copy.wait()
    policy_squares, policy_products = run(rows_p, weight_p, True)
    for copy in copies_r:
        copy.wait()
    reference_squares, reference_products = run(rows_r, weight_r, False)
    lane = lax.broadcasted_iota(jnp.int32, (2 * ROWS, 128), 1)
    stats_ref[...] = jnp.where(
        lane == 0,
        policy_squares,
        jnp.where(lane == 1, policy_products, jnp.where(lane == 2, reference_squares, reference_products)),
    )


def project(place, outs, target, weights):
    return pl.pallas_call(
        project_kernel,
        in_specs=[scalars()]
        + [in_place()] * 4
        + [pl.BlockSpec((ROWS, D_OUT), lambda i: (0, 0))]
        + [in_place()] * len(weights),
        grid=(1,),
        out_specs=[
            pl.BlockSpec((2 * ROWS, HALF), lambda i: (0, 0)),
            pl.BlockSpec((2 * ROWS, 128), lambda i: (0, 0)),
        ],
        out_shape=[
            jax.ShapeDtypeStruct((2 * ROWS, HALF), f32),
            jax.ShapeDtypeStruct((2 * ROWS, 128), f32),
        ],
        scratch_shapes=[
            VMEM((2 * ROWS, Q_WIDTH), bf16),
            VMEM((2 * ROWS, Q_WIDTH), bf16),
            VMEM((Q_WIDTH, HALF), bf16),
            VMEM((Q_WIDTH, HALF), bf16),
            pltpu.SemaphoreType.DMA((2,)),
        ],
        compiler_params=BIG,
        cost_estimate=pl.CostEstimate(
            flops=8 * ROWS * Q_WIDTH * HALF, bytes_accessed=24 << 20, transcendentals=0
        ),
    )(place, *outs, target, *weights)


def gradient_kernel(
    place_ref, own_ref, other_ref, y_ref, stats_ref, more_ref, target_ref, facts_ref,
    a0, a1, a2, a3, b0, b1, b2, b3, rows, grad, terms,
):
    y_at, c, z = place_ref[0], place_ref[2], place_ref[3]
    rows[:ROWS, :] = own_ref[...]
    rows[ROWS:, :] = other_ref[...]
    row = lax.broadcasted_iota(jnp.int32, (ROWS, 1), 0)
    for side in range(2):
        here = slice(side * ROWS, (side + 1) * ROWS)
        there = slice((1 - side) * ROWS, (2 - side) * ROWS)
        stats = stats_ref[here, :] + more_ref[there, :]
        policy_squares, policy_products = stats[:, 0:1], stats[:, 1:2]
        reference_squares, reference_products = stats[:, 2:3], stats[:, 3:4]
        one, two = 2 * side, 2 * side + 1
        early = row.astype(f32) < facts_ref[4 + one : 5 + one, 0:1]
        length = jnp.where(early, facts_ref[4 + one : 5 + one, 0:1], facts_ref[4 + two : 5 + two, 0:1])
        advantage = jnp.where(early, facts_ref[one : one + 1, 0:1], facts_ref[two : two + 1, 0:1])
        policy_norm = jnp.sqrt(policy_squares / D_OUT + norm_epsilon)
        reference_norm = jnp.sqrt(reference_squares / D_OUT + norm_epsilon)
        policy_self = policy_squares / (policy_norm * policy_norm)
        policy_cross = policy_products / policy_norm
        reference_self = reference_squares / (reference_norm * reference_norm)
        reference_cross = reference_products / reference_norm
        gain = ((policy_self - reference_self) - 2.0 * (policy_cross - reference_cross)) * (
            1.0 / (4.0 * math.sqrt(D_OUT))
        )
        weight = (advantage - kl_weight * (1.0 - jnp.exp(gain))) / length
        along = (policy_self - policy_cross) / D_OUT
        scale = weight / policy_norm
        slope = scale * (1.0 - along) / policy_norm
        side_lanes = c if side == 0 else 1 - c
        target = target_ref[:, pl.ds(pl.multiple_of(side_lanes * HALF, 128), HALF)].astype(f32)
        grad[here, :] = (y_ref[here, :] * slope - target * scale).astype(bf16)

    def term(first, lanes):
        return lax.dot_general(
            rows[:, pl.ds(first, PIECE)], grad[:, lanes], (((0,), (0,)), ((), ())), preferred_element_type=f32
        ).astype(bf16)

    for d, out in enumerate((a0, a1, a2, a3)):
        out[...] = term(pl.multiple_of(lax.rem(z + d, 4) * PIECE, 128), slice(0, PIECE))
    for k in range(4):
        terms[...] = term(k * PIECE, slice(PIECE, HALF)).reshape(2, 4, 80, PIECE)
        for d, out in enumerate((b0, b1, b2, b3)):
            out[2 * k : 2 * k + 2] = terms[:, lax.rem(y_at + d, 4)]


def gradient(place, own, other, y, stats, more, target, facts):
    block = lambda *shape: pl.BlockSpec(shape, lambda i: (0,) * len(shape))
    return pl.pallas_call(
        gradient_kernel,
        grid=(1,),
        in_specs=[
            scalars(),
            block(ROWS, Q_WIDTH),
            block(ROWS, Q_WIDTH),
            block(2 * ROWS, HALF),
            block(2 * ROWS, 128),
            block(2 * ROWS, 128),
            block(ROWS, D_OUT),
            block(8, 128),
        ],
        out_specs=[block(PIECE, PIECE)] * 4 + [block(8, 80, PIECE)] * 4,
        out_shape=[jax.ShapeDtypeStruct((PIECE, PIECE), bf16)] * 4
        + [jax.ShapeDtypeStruct((8, 80, PIECE), bf16)] * 4,
        scratch_shapes=[
            VMEM((2 * ROWS, Q_WIDTH), bf16),
            VMEM((2 * ROWS, HALF), bf16),
            VMEM((2, 4, 80, PIECE), bf16),
        ],
        compiler_params=BIG,
        cost_estimate=pl.CostEstimate(
            flops=4 * ROWS * Q_WIDTH * HALF, bytes_accessed=16 << 20, transcendentals=0
        ),
    )(place, own, other, y, stats, more, target, facts)


def total_of(refs, index):
    total = refs[0][index].astype(f32)
    for ref in refs[1:]:
        total = total + ref[index].astype(f32)
    return total


def sum_kernel(axis, place_at, place_ref, *refs):
    parts, outs = refs[:4], refs[4:]
    own = place_ref[place_at]
    for d, out in enumerate(outs):
        at = lax.rem(own + d, 4)
        index = (slice(None), at) if axis == 1 else (at,)
        out[...] = total_of(parts, index).astype(bf16)


def sum_blocks(place, parts, axis, place_at):
    shape = (2, 80, PIECE)
    return pl.pallas_call(
        functools.partial(sum_kernel, axis, place_at),
        in_specs=[scalars()] + [whole()] * 4,
        out_specs=[whole()] * 4,
        out_shape=[jax.ShapeDtypeStruct(shape, bf16)] * 4,
        compiler_params=BIG,
        cost_estimate=pl.CostEstimate(flops=4 << 20, bytes_accessed=5 << 20, transcendentals=0),
    )(place, *parts)


def last_sum_kernel(place_ref, *refs):
    first, second, keep, send = refs[:4], refs[4:8], refs[8], refs[9]
    xh = place_ref[4]
    for out, at in ((keep, xh), (send, 1 - xh)):
        out[:, :PIECE] = total_of(first, (at,)).astype(bf16)
        out[:, PIECE:] = total_of(second, (at,)).astype(bf16)


def last_sum(place, first, second):
    return pl.pallas_call(
        last_sum_kernel,
        in_specs=[scalars()] + [whole()] * 8,
        out_specs=[whole()] * 2,
        out_shape=[jax.ShapeDtypeStruct((80, HALF), bf16)] * 2,
        compiler_params=BIG,
    )(place, *first, *second)


def step_kernel(
    place_ref, square_ref, mine_ref, theirs_ref, weight_ref, ema_ref, update_ref, moved_ref, next_ref
):
    scale = lax.rsqrt(square_ref[0:1, 0:1] / (Q_WIDTH * D_OUT) + norm_epsilon)
    c = place_ref[2]
    for half in range(2):
        lanes = slice(half * HALF, (half + 1) * HALF)
        grad = jnp.where(c == half, mine_ref[0].astype(f32), theirs_ref[0].astype(f32))
        update = grad * scale
        moved = weight_ref[:, lanes].astype(f32) - step_size * update
        update_ref[:, lanes] = update
        moved_ref[:, lanes] = moved.astype(bf16)
        next_ref[:, lanes] = ema_decay * ema_ref[:, lanes] + (1.0 - ema_decay) * moved


def take_step(place, square_sum, mine, theirs, policy_weight, ema_weight):
    wide = lambda: pl.BlockSpec((80, D_OUT), lambda i, place: (i, 0))
    turned = lambda: pl.BlockSpec((1, 80, HALF), lambda i, place: (lax.rem(i + 4 - place[0], 4), 0, 0))
    return pl.pallas_call(
        step_kernel,
        grid_spec=pltpu.PrefetchScalarGridSpec(
            num_scalar_prefetch=1,
            grid=(4,),
            in_specs=[pl.BlockSpec((8, 128), lambda i, place: (0, 0)), turned(), turned(), wide(), wide()],
            out_specs=[wide()] * 3,
        ),
        out_shape=[
            jax.ShapeDtypeStruct((SHARD, D_OUT), f32),
            jax.ShapeDtypeStruct((SHARD, D_OUT), bf16),
            jax.ShapeDtypeStruct((SHARD, D_OUT), f32),
        ],
        compiler_params=BIG,
    )(place, square_sum, mine, theirs, policy_weight, ema_weight)


def local(
    q_policy,
    kv_policy,
    q_reference,
    kv_reference,
    target,
    send_slot,
    lengths,
    rewards,
    group_ids,
    policy_weight,
    ema_weight,
):
    place = jnp.stack([lax.axis_index(name) for name in EVERY]).astype(jnp.int32)
    c = place[2]
    send = lax.ppermute

    def half(weight):
        return lax.dynamic_slice_in_dim(weight, c * HALF, HALF, 1).astype(bf16)

    w0 = jnp.concatenate([half(policy_weight), half(ema_weight)], axis=0)
    sm = send(w0, "z", ring(1))
    sp = send(w0, "z", ring(-1))
    o0 = send(w0, ("xl", "xh"), ACROSS)

    facts = jnp.concatenate(
        [rewards, group_ids.astype(f32), lengths[0].astype(f32), jnp.zeros((2,), f32)]
    )[None, :]
    facts = jnp.concatenate([facts, send(facts, "xh", FLIP)], axis=0)
    facts = jnp.concatenate([facts] + [send(facts, "z", ring(d)) for d in (1, 2, 3)], axis=0)
    facts = jnp.pad(jnp.tile(facts, (2, 3)), ((0, 0), (0, 128 - 24)))

    rows_policy = pl.pallas_call(
        pack_policy_kernel,
        in_specs=[whole()] * 3,
        out_specs=whole(),
        out_shape=jax.ShapeDtypeStruct((ROWS, Q_WIDTH + 1024), bf16),
        compiler_params=BIG,
    )(send_slot, q_policy, kv_policy)
    rows_policy = lax.all_to_all(rows_policy, DP, split_axis=0, concat_axis=0, tiled=True)

    s2p = send(sm[:SHARD], "z", ring(1))
    s2e = send(sp[SHARD:], "z", ring(-1))
    om = send(sm, ("xl", "xh"), ACROSS)
    op = send(o0, "z", ring(-1))

    rows_reference = pl.pallas_call(
        pack_reference_kernel,
        in_specs=[whole()] * 5,
        out_specs=whole(),
        out_shape=jax.ShapeDtypeStruct((ROWS, D_OUT + Q_WIDTH + 1024 + 128), bf16),
        compiler_params=BIG,
    )(send_slot, q_reference, kv_reference, target, facts)
    rows_reference = lax.all_to_all(rows_reference, DP, split_axis=0, concat_axis=0, tiled=True)

    out_policy = attend(rows_policy, lengths, 0, Q_WIDTH, Q_WIDTH + 512)
    other_policy = send(out_policy, "c", FLIP)

    o2p = send(s2p, ("xl", "xh"), ACROSS)
    o2e = send(om[SHARD:], "z", ring(1))

    out_reference = attend(rows_reference, lengths, D_OUT, D_OUT + Q_WIDTH, D_OUT + Q_WIDTH + 512)
    other_reference = send(out_reference, "c", FLIP)
    advantages = pl.pallas_call(
        advantage_kernel,
        grid=(1,),
        in_specs=[scalars(), pl.BlockSpec((ROWS, 128), lambda i: (0, (D_OUT + Q_WIDTH + 1024) // 128))],
        out_specs=pl.BlockSpec((8, 128), lambda i: (0, 0)),
        out_shape=jax.ShapeDtypeStruct((8, 128), f32),
        compiler_params=BIG,
    )(place, rows_reference)

    y_policy, stats = project(
        place,
        (out_policy, other_policy, out_reference, other_reference),
        rows_reference,
        (w0, sm, sp, s2p, s2e, o0, om, op, o2p, o2e),
    )
    more = send(stats, "c", FLIP)
    pieces = gradient(place, out_policy, other_policy, y_policy, stats, more, rows_reference, advantages)

    first, second = pieces[:4], pieces[4:]
    first = [first[0]] + [send(first[d], "z", ring(d)) for d in (1, 2, 3)]
    second = [second[0]] + [send(second[d], "y", ring(d)) for d in (1, 2, 3)]
    first = sum_blocks(place, [piece.reshape(2, 4, 80, PIECE) for piece in first], 1, 0)
    second = sum_blocks(place, [piece.reshape(4, 2, 80, PIECE) for piece in second], 0, 3)
    first = [first[0]] + [send(first[d], "y", ring(d)) for d in (1, 2, 3)]
    second = [second[0]] + [send(second[d], "z", ring(d)) for d in (1, 2, 3)]
    kept, given = last_sum(place, first, second)

    def add(one, two):
        return (one.astype(f32) + two.astype(f32)).astype(bf16)

    block = add(kept, send(given, ("xl", "xh"), ACROSS))
    block = add(block, send(block, "xl", FLIP))

    mine = jnp.stack([block] + [send(block, "y", ring(-d)) for d in (1, 2, 3)])
    theirs = send(mine, "c", FLIP)
    square = jnp.sum(jnp.square(mine.astype(f32)), axis=(1, 2)) + jnp.sum(
        jnp.square(theirs.astype(f32)), axis=(1, 2)
    )
    square = (square[0] + square[2]) + (square[1] + square[3])
    square = jnp.broadcast_to(square, (8, 128))
    square = square + send(square, ("xl", "xh"), ACROSS)
    square = (square + send(square, "z", ring(2))) + (send(square, "z", ring(1)) + send(square, "z", ring(3)))
    return tuple(take_step(place, square, mine, theirs, policy_weight, ema_weight))


def solution(mesh):
    names = Mesh(mesh.devices.reshape(4, 2, 2, 4, 2), EVERY)
    rows, whole_rows = P(EVERY, None), P(EVERY)
    in_specs = (rows,) * 7 + (whole_rows,) * 2 + (P(FSDP, None),) * 2
    out_specs = (P(FSDP, None),) * 3
    return jax.shard_map(local, mesh=names, in_specs=in_specs, out_specs=out_specs, check_vma=False)
```

time: 690 us -> 309 us (0.45)
  waiting for transfers between devices: 353 us -> 153 us
  blocking collectives: 175 us -> 0 us
  Pallas kernels: 0 us -> 65.3 us
  matrix products: 57.4 us -> 0 us
  starting transfers between devices: 24.2 us -> 66.1 us
  local copies, waits for them, and re-layouts: 34.3 us -> 17.2 us
  other arithmetic: 18.1 us -> 3.85 us
  between operations: 14.7 us -> 3.59 us
  loops' own time: 10.8 us -> 0 us
    psum x2 -> x0, blocking collectives: 175 us -> none  [the longest x1 150 us: local(): lax.psum((jnp.dot(rewards, member, precision=lax.Precision.HIGHEST), jnp....]
    reduce_scatter x1 -> x0, waiting for transfers between devices: 155 us -> none  [local(): lax.psum_scatter(lax.dot_general(out_policy, grad_rows, (((0,), (0,)), ((...]
    ppermute x0 -> x38, waiting for transfers between devices: none -> 153 us  [the longest x1 33.7 us: local(): sm = send(w0, 'z', ring(1))]
    psum x1 -> x0, waiting for transfers between devices: 122 us -> none  [local(): grad_total = lax.psum(grad_share, 'dp').astype(jnp.float32)]
    pallas_call x0 -> x11, Pallas kernels: none -> 65.3 us  [the longest x1 15.1 us: project(): pl.pallas_call(project_kernel, in_specs=[scalars()] + [in_place()] * 4 +...]
    ppermute x0 -> x38, starting transfers between devices: none -> 56.1 us  [the longest x3 6.57 us: local(): send(facts, 'z', ring(d))]
    all_gather x2 -> x0, waiting for transfers between devices: 49.9 us -> none  [the longest x1 49.9 us: local(): lax.all_gather(ema_half, 'fsdp', axis=0, tiled=True)]
    dot_general x15 -> x0, matrix products: 43.7 us -> none  [the longest x2 20 us: fold_rows(): return jnp.dot(source, row_piece, preferred_element_type=jnp.float32)]
  transfers between devices with their start and end apart: 9 -> 40, of which waited for: 5 -> 22; matrix products, arithmetic and copies ran while one was open for 12% -> 3% of each run, Pallas kernels for 0% -> 9%
where the time goes in v1:
time: 309 us
  waiting for transfers between devices  153 us (50%)
  starting transfers between devices  66.1 us (21%)
  Pallas kernels  65.3 us (21%)
  local copies, waits for them, and re-layouts  17.2 us (6%)
  other arithmetic  3.85 us (1%)
  between operations  3.59 us (1%)
    ppermute x1, waiting for transfers between devices, local(): sm = send(w0, 'z', ring(1))  33.7 us
    ppermute x3, waiting for transfers between devices, local(): second = [second[0]] + [send(second[d], 'y', ring(d)) for d in (1, 2, 3)]  28.4 us
    ppermute x1, waiting for transfers between devices, local(): facts = jnp.concatenate([facts, send(facts, 'xh', FLIP)], axis=0)  19.6 us
    ppermute x1, waiting for transfers between devices, local(): o2p = send(s2p, ('xl', 'xh'), ACROSS)  16.6 us
    pallas_call x1, Pallas kernels, project(): pl.pallas_call(project_kernel, in_specs=[scalars()] + [in_place()] * 4 +...  15.1 us
    ppermute x1, waiting for transfers between devices, local(): om = send(sm, ('xl', 'xh'), ACROSS)  13.8 us
    pallas_call x2, Pallas kernels, attend(): pl.pallas_call(attention_kernel, grid=(KV_HEADS,), in_specs=[scalars(), p...  13.7 us
    pallas_call x1, Pallas kernels, gradient(): pl.pallas_call(gradient_kernel, grid=(1,), in_specs=[scalars(), block(ROW...  10.2 us
  transfers between devices with their start and end apart: 40, of which 22 were waited for; matrix products, arithmetic and copies ran while one was open for 3% of the time, Pallas kernels for 9%

profile of v1, /device:TPU:0, one launch (start us, length us, event | category | flops | bytes accessed | tf_op | source)
XLA Modules:
  0.0 308.7 jit_solution(3929822047365589150)
XLA Ops:
  0.6 3.3 %shard_map.130 = bf16[256,3584]{1,0:T(8,128)(2,1)} custom-call(s32[1,256]{1,0:T(1,128)} %slots_ref.3, bf16[256,2560]{1,0:T(8,128)(2,1)} %q_ref.2, bf16[256,1024]{1,0:T(8,128)(2,1)} %kv_ref.2), custom_call_target="tpu_custom_call" | custom-call | tf_op jit(solution)/shard_map/pallas_call | solution.py:449
  4.0 5.7 %all-to-all-start = ((bf16[16,16,3584]{2,1,0:T(8,128)(2,1)}), bf16[16,16,3584]{2,1,0:T(8,128)(2,1)S(1)}, u32[]{:S(2)}, u32[]{:S(2)}) async-start(bf16[16,16,3584]{2,1,0:T(8,128)(2,1)} %bitcast.38), calls=%async_computation | async-start | bytes 3670016 | tf_op jit(solution)/shard_map/all_to_all | solution.py:456
  15.3 19.6 %collective-permute-done.1 = f32[1,8]{1,0:T(1,128)S(1)} collective-permute-done((f32[1,8]{1,0:T(1,128)S(1)}, f32[1,8]{1,0:T(1,128)S(1)}, u32[]{:S(2)}, u32[]{:S(2)}) %collective-permute-start.1) | collective-permute-done | bytes 64 | tf_op jit(solution)/shard_map/ppermute | solution.py:445
  36.9 3.6 %collective-permute-start.3 = (f32[2,8]{1,0:T(2,128)S(1)}, f32[2,8]{1,0:T(2,128)S(1)}, u32[]{:S(2)}, u32[]{:S(2)}) collective-permute-start(f32[2,8]{1,0:T(2,128)S(1)} %pad_maximum_fusion.2), channel_id=1, source_target_pairs={{0,4},{2,6},{4,0},{6,2},{1,5},{3,7},{5,1},{7,3},{8,12},{10,14},{12... | collective-permute-start | bytes 200 | tf_op jit(solution)/shard_map/ppermute | solution.py:446
  45.0 4.5 %shard_map.132 = bf16[256,6272]{1,0:T(8,128)(2,1)} custom-call(s32[1,256]{1,0:T(1,128)} %slots_ref.3, bf16[256,2560]{1,0:T(8,128)(2,1)} %q_ref.3, bf16[256,1024]{1,0:T(8,128)(2,1)} %kv_ref.3, bf16[256,2560]{1,0:T(8,128)(2,1)} %target_ref.1, f32[16,128]{1,0:T(8,128)} %pad.4.facts_ref), custom_call_target="tpu_custom_call" | custom-call | tf_op jit(solution)/shard_map/pallas_call | solution.py:463
  50.7 4.3 %all-to-all-start.1 = ((bf16[16,16,6272]{2,1,0:T(8,128)(2,1)}), bf16[16,16,6272]{2,1,0:T(8,128)(2,1)S(1)}, u32[]{:S(2)}, u32[]{:S(2)}) async-start(bf16[16,16,6272]{2,1,0:T(8,128)(2,1)} %bitcast.37), calls=%async_computation.1 | async-start | bytes 6422528 | tf_op jit(solution)/shard_map/all_to_all | solution.py:470
  62.3 33.7 %collective-permute-done.6.sm = bf16[640,1280]{1,0:T(8,128)(2,1)} collective-permute-done((bf16[640,1280]{1,0:T(8,128)(2,1)S(1)}, bf16[640,1280]{1,0:T(8,128)(2,1)}, u32[]{:S(2)}, u32[]{:S(2)}) %collective-permute-start.6) | collective-permute-done | bytes 1638432 | tf_op jit(solution)/shard_map/ppermute | solution.py:438
  105.1 6.8 %shard_map.131.own_p.own_ref = bf16[256,2560]{1,0:T(8,128)(2,1)} custom-call(s32[1,2]{1,0:T(1,128)} %lengths_ref.3, bf16[256,3584]{1,0:T(8,128)(2,1)} %bitcast.34, bf16[256,3584]{1,0:T(8,128)(2,1)} %bitcast.35, bf16[256,3584]{1,0:T(8,128)(2,1)} %bitcast.36), custom_call_target="tpu_custom_call" | custom-call | flops 671088640 | bytes 4194304 | tf_op jit(solution)/shard_map/pallas_call | solution.py:117
  113.6 6.8 %shard_map.133.own_r = bf16[256,2560]{1,0:T(8,128)(2,1)} custom-call(s32[1,2]{1,0:T(1,128)} %lengths_ref.3, bf16[256,6272]{1,0:T(8,128)(2,1)} %bitcast.28, bf16[256,6272]{1,0:T(8,128)(2,1)} %bitcast.29, bf16[256,6272]{1,0:T(8,128)(2,1)} %bitcast.30), custom_call_target="tpu_custom_call" | custom-call | flops 671088640 | bytes 4194304 | tf_op jit(solution)/shard_map/pallas_call | solution.py:117
  121.1 13.8 %collective-permute-done.11.om = bf16[640,1280]{1,0:T(8,128)(2,1)} collective-permute-done((bf16[640,1280]{1,0:T(8,128)(2,1)}, bf16[640,1280]{1,0:T(8,128)(2,1)}, u32[]{:S(2)}, u32[]{:S(2)}) %collective-permute-start.11) | collective-permute-done | bytes 1638432 | tf_op jit(solution)/shard_map/ppermute | solution.py:460
  138.7 16.6 %collective-permute-done.13.o2p = bf16[320,1280]{1,0:T(8,128)(2,1)S(1)} collective-permute-done((bf16[320,1280]{1,0:T(8,128)(2,1)}, bf16[320,1280]{1,0:T(8,128)(2,1)S(1)}, u32[]{:S(2)}, u32[]{:S(2)}) %collective-permute-start.13) | collective-permute-done | bytes 819232 | tf_op jit(solution)/shard_map/ppermute | solution.py:475
  158.7 15.1 %shard_map.134 = (f32[512,1280]{1,0:T(8,128)}, f32[512,128]{1,0:T(8,128)}) custom-call(s32[5]{0:T(128)} %stack.38.place_ref, bf16[256,2560]{1,0:T(8,128)(2,1)} %shard_map.131.own_p.own_ref, bf16[256,2560]{1,0:T(8,128)(2,1)} %collective-permute-done.other_p.other_ref, bf16[256,2560]{1,0:T(8,128)(2,1)} %shard_map.133.own_r, bf16[256,2560]{1,0:T(8,128)(2,1)} %copy-done.21, ...), custom_call_target="tpu_custom_call" | custom-call | flops 6710886400 | bytes 25165824 | tf_op jit(solution)/shard_map/pallas_call | solution.py:229
  177.1 10.2 %shard_map.136 = (bf16[640,640]{1,0:T(8,128)(2,1)}, bf16[640,640]{1,0:T(8,128)(2,1)}, bf16[640,640]{1,0:T(8,128)(2,1)}, bf16[640,640]{1,0:T(8,128)(2,1)}, bf16[8...) custom-call(s32[5]{0:T(128)} %stack.38.place_ref, ...), custom_call_target="tpu_custom_call" | custom-call | flops 3355443200 | bytes 16777216 | tf_op jit(solution)/shard_map/pallas_call | solution.py:308
  193.0 4.0 %collective-permute-start.17 = (bf16[640,640]{1,0:T(8,128)(2,1)}, bf16[640,640]{1,0:T(8,128)(2,1)S(1)}, u32[]{:S(2)}, u32[]{:S(2)}) collective-permute-start(bf16[640,640]{1,0:T(8,128)(2,1)} %get-tuple-element.27), channel_id=1, source_target_pairs={{0,4},{2,6},{4,0},{6,2},{1,5},{3,7},{5,1},{7,3},{8,12},{10,14},{12... | collective-permute-start | bytes 2457608 | tf_op jit(solution)/shard_map/ppermute | solution.py:499
  197.0 12.5 %collective-permute-done.22 = bf16[8,80,640]{2,1,0:T(8,128)(2,1)S(1)} collective-permute-done((bf16[8,80,640]{2,1,0:T(8,128)(2,1)}, bf16[8,80,640]{2,1,0:T(8,128)(2,1)S(1)}, u32[]{:S(2)}, u32[]{:S(2)}) %collective-permute-start.22) | collective-permute-done | bytes 819232 | tf_op jit(solution)/shard_map/ppermute | solution.py:500
  212.0 15.9 %collective-permute-done.23 = bf16[8,80,640]{2,1,0:T(8,128)(2,1)S(1)} collective-permute-done((bf16[8,80,640]{2,1,0:T(8,128)(2,1)}, bf16[8,80,640]{2,1,0:T(8,128)(2,1)S(1)}, u32[]{:S(2)}, u32[]{:S(2)}) %collective-permute-start.23) | collective-permute-done | bytes 819232 | tf_op jit(solution)/shard_map/ppermute | solution.py:500
  232.1 4.0 %collective-permute-start.26 = (bf16[2,80,640]{2,1,0:T(8,128)(2,1)}, bf16[2,80,640]{2,1,0:T(8,128)(2,1)S(1)}, u32[]{:S(2)}, u32[]{:S(2)}) collective-permute-start(bf16[2,80,640]{2,1,0:T(8,128)(2,1)} %get-tuple-element.39), channel_id=1, source_target_pairs={{0,4},{2,6},{4,0},{6,2},{1,5},{3,7},{5,1},{7,3},{8,12},{10,14},{12... | collective-permute-start | bytes 614408 | tf_op jit(solution)/shard_map/ppermute | solution.py:504
  245.7 3.5 %collective-permute-done.19.refs_1_ = bf16[2,80,640]{2,1,0:T(8,128)(2,1)S(1)} collective-permute-done((bf16[2,80,640]{2,1,0:T(8,128)(2,1)}, bf16[2,80,640]{2,1,0:T(8,128)(2,1)S(1)}, u32[]{:S(2)}, u32[]{:S(2)}) %collective-permute-start.19) | collective-permute-done | bytes 204832 | tf_op jit(solution)/shard_map/ppermute | solution.py:503
  249.2 4.0 %collective-permute-done.20.refs_2_ = bf16[2,80,640]{2,1,0:T(8,128)(2,1)S(1)} collective-permute-done((bf16[2,80,640]{2,1,0:T(8,128)(2,1)}, bf16[2,80,640]{2,1,0:T(8,128)(2,1)S(1)}, u32[]{:S(2)}, u32[]{:S(2)}) %collective-permute-start.20) | collective-permute-done | bytes 204832 | tf_op jit(solution)/shard_map/ppermute | solution.py:503
  257.7 5.8 %collective-permute-done.28 = bf16[80,1280]{1,0:T(8,128)(2,1)S(1)} collective-permute-done((bf16[80,1280]{1,0:T(8,128)(2,1)}, bf16[80,1280]{1,0:T(8,128)(2,1)S(1)}, u32[]{:S(2)}, u32[]{:S(2)}) %collective-permute-start.28) | collective-permute-done | bytes 204832 | tf_op jit(solution)/shard_map/ppermute | solution.py:510
  264.6 5.7 %collective-permute-done.29 = bf16[80,1280]{1,0:T(8,128)(2,1)S(1)} collective-permute-done((bf16[80,1280]{1,0:T(8,128)(2,1)S(1)}, bf16[80,1280]{1,0:T(8,128)(2,1)S(1)}, u32[]{:S(2)}, u32[]{:S(2)}) %collective-permute-start.29) | collective-permute-done | bytes 204832 | tf_op jit(solution)/shard_map/ppermute | solution.py:511
  275.0 5.1 %collective-permute-done.30 = bf16[80,1280]{1,0:T(8,128)(2,1)S(1)} collective-permute-done((bf16[80,1280]{1,0:T(8,128)(2,1)S(1)}, bf16[80,1280]{1,0:T(8,128)(2,1)S(1)}, u32[]{:S(2)}, u32[]{:S(2)}) %collective-permute-start.30) | collective-permute-done | bytes 204832 | tf_op jit(solution)/shard_map/ppermute | solution.py:513
  291.1 3.6 %collective-permute-done.34 = f32[8,128]{1,0:T(8,128)S(1)} collective-permute-done((f32[8,128]{1,0:T(8,128)S(1)}, f32[8,128]{1,0:T(8,128)S(1)}, u32[]{:S(2)}, u32[]{:S(2)}) %collective-permute-start.34) | collective-permute-done | bytes 4128 | tf_op jit(solution)/shard_map/ppermute | solution.py:520
  301.0 7.7 %shard_map.140 = (f32[320,2560]{1,0:T(8,128)}, bf16[320,2560]{1,0:T(8,128)(2,1)}, f32[320,2560]{1,0:T(8,128)}) custom-call(s32[5]{0:T(128)} %stack.38.place_ref, f32[8,128]{1,0:T(8,128)} %add_add_fusion.square_ref, bf16[4,80,1280]{2,1,0:T(8,128)(2,1)} %copy-done.3, bf16[4,80,1280]{2,1,0:T(8,128)(2,1)} %copy-done.4, bf16[320,2560]{1,0:T(8,128)(2,1)} %weight_ref.1, ...), custom_call_target="tpu_custom_call" | custom-call | tf_op jit(solution)/shard_map/pallas_call | solution.py:400
  (143 shorter events, 89.1 us)
Async XLA Ops:
  4.0 45.5 %all-to-all-start = ((bf16[16,16,3584]{2,1,0:T(8,128)(2,1)}), bf16[16,16,3584]{2,1,0:T(8,128)(2,1)S(1)}, u32[]{:S(2)}, u32[]{:S(2)}) async-start(bf16[16,16,3584]{2,1,0:T(8,128)(2,1)} %bitcast.38), calls=%async_computation | async-start | bytes 3670016 | tf_op jit(solution)/shard_map/all_to_all | solution.py:456
  9.8 25.1 %collective-permute-start.1 = (f32[1,8]{1,0:T(1,128)S(1)}, f32[1,8]{1,0:T(1,128)S(1)}, u32[]{:S(2)}, u32[]{:S(2)}) collective-permute-start(f32[1,8]{1,0:T(1,128)S(1)} %maximum_bitcast_fusion), channel_id=1, source_target_pairs={{0,1},{1,0},{2,3},{3,2},{4,5},{5,4},{6,7},{7,6},{8,9},{9,8},{10,11... | collective-permute-start | bytes 104 | tf_op jit(solution)/shard_map/ppermute | solution.py:445
  50.7 61.2 %all-to-all-start.1 = ((bf16[16,16,6272]{2,1,0:T(8,128)(2,1)}), bf16[16,16,6272]{2,1,0:T(8,128)(2,1)S(1)}, u32[]{:S(2)}, u32[]{:S(2)}) async-start(bf16[16,16,6272]{2,1,0:T(8,128)(2,1)} %bitcast.37), calls=%async_computation.1 | async-start | bytes 6422528 | tf_op jit(solution)/shard_map/all_to_all | solution.py:470
  56.5 39.5 %collective-permute-start.6 = (bf16[640,1280]{1,0:T(8,128)(2,1)S(1)}, bf16[640,1280]{1,0:T(8,128)(2,1)}, u32[]{:S(2)}, u32[]{:S(2)}) collective-permute-start(bf16[640,1280]{1,0:T(8,128)(2,1)S(1)} %pad_maximum_fusion.w0), channel_id=1, source_target_pairs={{0,2},{2,4},{4,6},{6,0},{1,3},{3,5},{5,7},{7,1},{8,10},{10,12},{12... | collective-permute-start | bytes 4915208 | tf_op jit(solution)/shard_map/ppermute | solution.py:438
  56.6 43.8 %collective-permute-start.7 = (bf16[640,1280]{1,0:T(8,128)(2,1)S(1)}, bf16[640,1280]{1,0:T(8,128)(2,1)S(1)}, u32[]{:S(2)}, u32[]{:S(2)}) collective-permute-start(bf16[640,1280]{1,0:T(8,128)(2,1)S(1)} %pad_maximum_fusion.w0), channel_id=1, source_target_pairs={{0,6},{2,0},{4,2},{6,4},{1,7},{3,1},{5,3},{7,5},{8,14},{10,8},{12,... | collective-permute-start | bytes 4915208 | tf_op jit(solution)/shard_map/ppermute | solution.py:439
  59.8 44.8 %collective-permute-start.10 = (bf16[640,1280]{1,0:T(8,128)(2,1)S(1)}, bf16[640,1280]{1,0:T(8,128)(2,1)}, u32[]{:S(2)}, u32[]{:S(2)}) collective-permute-start(bf16[640,1280]{1,0:T(8,128)(2,1)S(1)} %pad_maximum_fusion.w0), channel_id=1, source_target_pairs={{16,1},{1,16},{0,17},{17,0},{18,3},{3,18},{2,19},{19,2},{20,5},{5,... | collective-permute-start | bytes 4915208 | tf_op jit(solution)/shard_map/ppermute | solution.py:440
  96.0 38.9 %collective-permute-start.11 = (bf16[640,1280]{1,0:T(8,128)(2,1)}, bf16[640,1280]{1,0:T(8,128)(2,1)}, u32[]{:S(2)}, u32[]{:S(2)}) collective-permute-start(bf16[640,1280]{1,0:T(8,128)(2,1)} %collective-permute-done.6.sm), channel_id=1, source_target_pairs={{16,1},{1,16},{0,17},{17,0},{18,3},{3,18},{2,19},{19,2},{20,5},{5,... | collective-permute-start | bytes 4915208 | tf_op jit(solution)/shard_map/ppermute | solution.py:460
  100.4 20.7 %collective-permute-start.8 = (bf16[320,1280]{1,0:T(8,128)(2,1)}, bf16[320,1280]{1,0:T(8,128)(2,1)}, u32[]{:S(2)}, u32[]{:S(2)}) collective-permute-start(bf16[320,1280]{1,0:T(8,128)(2,1)} %slice.28), channel_id=1, source_target_pairs={{0,2},{2,4},{4,6},{6,0},{1,3},{3,5},{5,7},{7,1},{8,10},{10,12},{12... | collective-permute-start | bytes 2457608 | tf_op jit(solution)/shard_map/ppermute | solution.py:458
  101.4 36.6 %collective-permute-start.9 = (bf16[320,1280]{1,0:T(8,128)(2,1)}, bf16[320,1280]{1,0:T(8,128)(2,1)}, u32[]{:S(2)}, u32[]{:S(2)}) collective-permute-start(bf16[320,1280]{1,0:T(8,128)(2,1)} %slice.29), channel_id=1, source_target_pairs={{0,6},{2,0},{4,2},{6,4},{1,7},{3,1},{5,3},{7,5},{8,14},{10,8},{12,... | collective-permute-start | bytes 2457608 | tf_op jit(solution)/shard_map/ppermute | solution.py:459
  104.6 51.8 %collective-permute-start.12 = (bf16[640,1280]{1,0:T(8,128)(2,1)}, bf16[640,1280]{1,0:T(8,128)(2,1)}, u32[]{:S(2)}, u32[]{:S(2)}) collective-permute-start(bf16[640,1280]{1,0:T(8,128)(2,1)} %collective-permute-done.10.o0), channel_id=1, source_target_pairs={{0,6},{2,0},{4,2},{6,4},{1,7},{3,1},{5,3},{7,5},{8,14},{10,8},{12,... | collective-permute-start | bytes 4915208 | tf_op jit(solution)/shard_map/ppermute | solution.py:461
  111.9 26.7 %collective-permute-start = (bf16[256,2560]{1,0:T(8,128)(2,1)}, bf16[256,2560]{1,0:T(8,128)(2,1)}, u32[]{:S(2)}, u32[]{:S(2)}) collective-permute-start(bf16[256,2560]{1,0:T(8,128)(2,1)} %shard_map.131.own_p.own_ref), channel_id=1, source_target_pairs={{0,8},{8,0},{1,9},{9,1},{2,10},{10,2},{3,11},{11,3},{4,12},{12,4},... | collective-permute-start | bytes 3932168 | tf_op jit(solution)/shard_map/ppermute | solution.py:473
  121.1 36.6 %collective-permute-start.5 = (bf16[256,2560]{1,0:T(8,128)(2,1)}, bf16[256,2560]{1,0:T(8,128)(2,1)S(1)}, u32[]{:S(2)}, u32[]{:S(2)}) collective-permute-start(bf16[256,2560]{1,0:T(8,128)(2,1)} %shard_map.133.own_r), channel_id=1, source_target_pairs={{0,8},{8,0},{1,9},{9,1},{2,10},{10,2},{3,11},{11,3},{4,12},{12,4},... | collective-permute-start | bytes 3932168 | tf_op jit(solution)/shard_map/ppermute | solution.py:479
  134.9 20.3 %collective-permute-start.13 = (bf16[320,1280]{1,0:T(8,128)(2,1)}, bf16[320,1280]{1,0:T(8,128)(2,1)S(1)}, u32[]{:S(2)}, u32[]{:S(2)}) collective-permute-start(bf16[320,1280]{1,0:T(8,128)(2,1)} %collective-permute-done.8.s2p), channel_id=1, source_target_pairs={{16,1},{1,16},{0,17},{17,0},{18,3},{3,18},{2,19},{19,2},{20,5},{5,... | collective-permute-start | bytes 2457608 | tf_op jit(solution)/shard_map/ppermute | solution.py:475
  138.0 19.7 %collective-permute-start.14 = (bf16[320,1280]{1,0:T(8,128)(2,1)S(1)}, bf16[320,1280]{1,0:T(8,128)(2,1)}, u32[]{:S(2)}, u32[]{:S(2)}) collective-permute-start(bf16[320,1280]{1,0:T(8,128)(2,1)S(1)} %slice.30), channel_id=1, source_target_pairs={{0,2},{2,4},{4,6},{6,0},{1,3},{3,5},{5,7},{7,1},{8,10},{10,12},{12... | collective-permute-start | bytes 2457608 | tf_op jit(solution)/shard_map/ppermute | solution.py:476
  187.4 22.1 %collective-permute-start.22 = (bf16[8,80,640]{2,1,0:T(8,128)(2,1)}, bf16[8,80,640]{2,1,0:T(8,128)(2,1)S(1)}, u32[]{:S(2)}, u32[]{:S(2)}) collective-permute-start(bf16[8,80,640]{2,1,0:T(8,128)(2,1)} %get-tuple-element.34), channel_id=1, source_target_pairs={{0,32},{32,64},{64,96},{96,0},{1,33},{33,65},{65,97},{97,1},{2,34}... | collective-permute-start | bytes 2457608 | tf_op jit(solution)/shard_map/ppermute | solution.py:500
  188.9 39.0 %collective-permute-start.23 = (bf16[8,80,640]{2,1,0:T(8,128)(2,1)}, bf16[8,80,640]{2,1,0:T(8,128)(2,1)S(1)}, u32[]{:S(2)}, u32[]{:S(2)}) collective-permute-start(bf16[8,80,640]{2,1,0:T(8,128)(2,1)} %get-tuple-element.35), channel_id=1, source_target_pairs={{0,64},{32,96},{64,0},{96,32},{1,65},{33,97},{65,1},{97,33},{2,66}... | collective-permute-start | bytes 2457608 | tf_op jit(solution)/shard_map/ppermute | solution.py:500
  191.5 36.4 %collective-permute-start.24 = (bf16[8,80,640]{2,1,0:T(8,128)(2,1)}, bf16[8,80,640]{2,1,0:T(8,128)(2,1)S(1)}, u32[]{:S(2)}, u32[]{:S(2)}) collective-permute-start(bf16[8,80,640]{2,1,0:T(8,128)(2,1)} %get-tuple-element.36), channel_id=1, source_target_pairs={{0,96},{32,0},{64,32},{96,64},{1,97},{33,1},{65,33},{97,65},{2,98}... | collective-permute-start | bytes 2457608 | tf_op jit(solution)/shard_map/ppermute | solution.py:500
  193.0 43.1 %collective-permute-start.16 = (bf16[640,640]{1,0:T(8,128)(2,1)}, bf16[640,640]{1,0:T(8,128)(2,1)S(1)}, u32[]{:S(2)}, u32[]{:S(2)}) collective-permute-start(bf16[640,640]{1,0:T(8,128)(2,1)} %get-tuple-element.26), channel_id=1, source_target_pairs={{0,2},{2,4},{4,6},{6,0},{1,3},{3,5},{5,7},{7,1},{8,10},{10,12},{12... | collective-permute-start | bytes 2457608 | tf_op jit(solution)/shard_map/ppermute | solution.py:499
  193.0 43.1 %collective-permute-start.17 = (bf16[640,640]{1,0:T(8,128)(2,1)}, bf16[640,640]{1,0:T(8,128)(2,1)S(1)}, u32[]{:S(2)}, u32[]{:S(2)}) collective-permute-start(bf16[640,640]{1,0:T(8,128)(2,1)} %get-tuple-element.27), channel_id=1, source_target_pairs={{0,4},{2,6},{4,0},{6,2},{1,5},{3,7},{5,1},{7,3},{8,12},{10,14},{12... | collective-permute-start | bytes 2457608 | tf_op jit(solution)/shard_map/ppermute | solution.py:499
  209.4 26.7 %collective-permute-start.18 = (bf16[640,640]{1,0:T(8,128)(2,1)}, bf16[640,640]{1,0:T(8,128)(2,1)S(1)}, u32[]{:S(2)}, u32[]{:S(2)}) collective-permute-start(bf16[640,640]{1,0:T(8,128)(2,1)} %get-tuple-element.28), channel_id=1, source_target_pairs={{0,6},{2,0},{4,2},{6,4},{1,7},{3,1},{5,3},{7,5},{8,14},{10,8},{12,... | collective-permute-start | bytes 2457608 | tf_op jit(solution)/shard_map/ppermute | solution.py:499
  232.1 12.1 %collective-permute-start.25 = (bf16[2,80,640]{2,1,0:T(8,128)(2,1)}, bf16[2,80,640]{2,1,0:T(8,128)(2,1)S(1)}, u32[]{:S(2)}, u32[]{:S(2)}) collective-permute-start(bf16[2,80,640]{2,1,0:T(8,128)(2,1)} %get-tuple-element.38), channel_id=1, source_target_pairs={{0,2},{2,4},{4,6},{6,0},{1,3},{3,5},{5,7},{7,1},{8,10},{10,12},{12... | collective-permute-start | bytes 614408 | tf_op jit(solution)/shard_map/ppermute | solution.py:504
  232.1 13.6 %collective-permute-start.26 = (bf16[2,80,640]{2,1,0:T(8,128)(2,1)}, bf16[2,80,640]{2,1,0:T(8,128)(2,1)S(1)}, u32[]{:S(2)}, u32[]{:S(2)}) collective-permute-start(bf16[2,80,640]{2,1,0:T(8,128)(2,1)} %get-tuple-element.39), channel_id=1, source_target_pairs={{0,4},{2,6},{4,0},{6,2},{1,5},{3,7},{5,1},{7,3},{8,12},{10,14},{12... | collective-permute-start | bytes 614408 | tf_op jit(solution)/shard_map/ppermute | solution.py:504
  241.7 11.4 %collective-permute-start.20 = (bf16[2,80,640]{2,1,0:T(8,128)(2,1)}, bf16[2,80,640]{2,1,0:T(8,128)(2,1)S(1)}, u32[]{:S(2)}, u32[]{:S(2)}) collective-permute-start(bf16[2,80,640]{2,1,0:T(8,128)(2,1)} %get-tuple-element.31), channel_id=1, source_target_pairs={{0,64},{32,96},{64,0},{96,32},{1,65},{33,97},{65,1},{97,33},{2,66}... | collective-permute-start | bytes 614408 | tf_op jit(solution)/shard_map/ppermute | solution.py:503
  270.3 9.8 %collective-permute-start.30 = (bf16[80,1280]{1,0:T(8,128)(2,1)S(1)}, bf16[80,1280]{1,0:T(8,128)(2,1)S(1)}, u32[]{:S(2)}, u32[]{:S(2)}) collective-permute-start(bf16[80,1280]{1,0:T(8,128)(2,1)S(1)} %add_convert_fusion), channel_id=1, source_target_pairs={{0,96},{32,0},{64,32},{96,64},{1,97},{33,1},{65,33},{97,65},{2,98}... | collective-permute-start | bytes 614408 | tf_op jit(solution)/shard_map/ppermute | solution.py:513
  (41 other events, 263.8 us)

commit v2 on v1

v2 whole, which is shorter than its diff:
```python
import functools
import math

import jax
import jax.numpy as jnp
from jax import lax
from jax.experimental import pallas as pl
from jax.experimental.pallas import tpu as pltpu
from jax.sharding import Mesh
from jax.sharding import PartitionSpec as P

HEADS = 20
KV_HEADS = 4
HEAD_DIM = 128
D_OUT = 2560
GROUP = 8
Q_WIDTH = 2560
ROWS = 256
SPAN = 16
SHARD = 320
HALF = 1280
CHUNK = 256
PIECE = 640
LATE = 384
TARGET_AT = 3584
FACTS_AT = 6144

kl_weight = 0.1
step_size = 0.02
ema_decay = 0.95
std_floor = 0.6
norm_epsilon = 1e-06

bf16 = jnp.bfloat16
f32 = jnp.float32
VMEM = pltpu.VMEM
SMEM = pltpu.SMEM
BIG = pltpu.CompilerParams(vmem_limit_bytes=56 * 1024 * 1024)
SMALL = pltpu.CompilerParams(vmem_limit_bytes=24 * 1024 * 1024)

DP = ("y", "xl", "c")
FSDP = ("z", "xh")
EVERY = DP + FSDP


def ring(step):
    return [(i, (i + step) % 4) for i in range(4)]


FLIP = [(0, 1), (1, 0)]
ACROSS = [(2, 1), (1, 2), (0, 3), (3, 0)]


def whole(shape=None):
    return pl.BlockSpec(memory_space=VMEM)


def scalars():
    return pl.BlockSpec(memory_space=SMEM)


def in_place():
    return pl.BlockSpec(memory_space=pl.ANY)


def dot(a, b):
    return jnp.dot(a, b, preferred_element_type=f32)


def one_hot_rows(slots_ref):
    return (lax.broadcasted_iota(jnp.int32, (ROWS, ROWS), 0) == slots_ref[...]).astype(bf16)


def pack_rows_kernel(slots_ref, q_ref, kv_ref, *rest):
    out_ref = rest[-1]
    pick = one_hot_rows(slots_ref)
    out_ref[:, :Q_WIDTH] = dot(pick, q_ref[...]).astype(bf16)
    out_ref[:, Q_WIDTH : Q_WIDTH + 1024] = dot(pick, kv_ref[...]).astype(bf16)


def pack_policy_kernel(rewards_ref, ids_ref, lengths_ref, slots_ref, q_ref, kv_ref, target_ref, *rest):
    out_ref = rest[-1]
    pack_rows_kernel(slots_ref, q_ref, kv_ref, out_ref)
    rows = dot(one_hot_rows(slots_ref), target_ref[...]).astype(bf16)
    left, right = slice(TARGET_AT, TARGET_AT + HALF), slice(TARGET_AT + HALF, TARGET_AT + D_OUT)
    for pair in range(ROWS // (2 * SPAN)):
        top = pair * 2 * SPAN
        one, two = slice(top, top + SPAN), slice(top + SPAN, top + 2 * SPAN)
        out_ref[one, left] = rows[one, :HALF]
        out_ref[one, right] = rows[two, :HALF]
        out_ref[two, left] = rows[one, HALF:]
        out_ref[two, right] = rows[two, HALF:]
    lane = lax.broadcasted_iota(jnp.int32, (8, 128), 1)
    facts = jnp.zeros((8, 128), f32)
    given = (rewards_ref[0], rewards_ref[1], ids_ref[0], ids_ref[1], lengths_ref[0, 0], lengths_ref[0, 1])
    for k, fact in enumerate(given):
        facts = jnp.where(lane % 8 == k, fact.astype(f32), facts)
    high = facts.astype(bf16).astype(f32)
    middle = (facts - high).astype(bf16).astype(f32)
    low = facts - high - middle
    coded = jnp.where(lane < 8, high, jnp.where(lane < 16, middle, low))
    out_ref[:, FACTS_AT:] = jnp.broadcast_to(coded[0:1], (ROWS, 128)).astype(bf16)


def pack(kernel, width, operands, after=(), small=()):
    return pl.pallas_call(
        kernel,
        in_specs=[scalars()] * len(small) + [whole()] * len(operands) + [in_place()] * len(after),
        out_specs=whole(),
        out_shape=jax.ShapeDtypeStruct((ROWS, width), bf16),
        compiler_params=BIG,
        cost_estimate=pl.CostEstimate(
            flops=2 * ROWS * ROWS * width, bytes_accessed=4 * ROWS * width, transcendentals=0
        ),
    )(*small, *operands, *after)


def attention_kernel(lengths_ref, q_ref, k_ref, v_ref, *rest):
    out_ref = rest[-1]
    row = lax.broadcasted_iota(jnp.int32, (ROWS, ROWS), 0)
    column = lax.broadcasted_iota(jnp.int32, (ROWS, ROWS), 1)
    bound = lengths_ref[0, 0]
    allowed = (column <= row) & ((column >= bound) | (row < bound))
    keys, values = k_ref[...], v_ref[...]
    for head in range(HEADS // KV_HEADS):
        lanes = slice(head * HEAD_DIM, (head + 1) * HEAD_DIM)
        scores = lax.dot_general(
            q_ref[:, lanes], keys, (((1,), (1,)), ((), ())), preferred_element_type=f32
        ) * (1.0 / math.sqrt(HEAD_DIM))
        scores = jnp.where(allowed, scores, -1e30)
        weights = jnp.exp(scores - jnp.max(scores, axis=1, keepdims=True))
        shares = (weights / jnp.sum(weights, axis=1, keepdims=True)).astype(bf16)
        out_ref[:, lanes] = dot(shares, values).astype(bf16)


def attend(rows, lengths, after):
    q_at, k_at, v_at = 0, Q_WIDTH, Q_WIDTH + 512
    width = Q_WIDTH // KV_HEADS
    return pl.pallas_call(
        attention_kernel,
        grid=(KV_HEADS,),
        in_specs=[
            scalars(),
            pl.BlockSpec((ROWS, width), lambda g: (0, q_at // width + g)),
            pl.BlockSpec((ROWS, HEAD_DIM), lambda g: (0, k_at // HEAD_DIM + g)),
            pl.BlockSpec((ROWS, HEAD_DIM), lambda g: (0, v_at // HEAD_DIM + g)),
        ]
        + [in_place()] * len(after),
        out_specs=pl.BlockSpec((ROWS, width), lambda g: (0, g)),
        out_shape=jax.ShapeDtypeStruct((ROWS, Q_WIDTH), bf16),
        compiler_params=BIG,
        cost_estimate=pl.CostEstimate(
            flops=4 * HEADS * ROWS * ROWS * HEAD_DIM, bytes_accessed=4 << 20, transcendentals=HEADS * ROWS * ROWS
        ),
    )(lengths, rows, rows, rows, *after)


def facts_kernel(coded_ref, out_ref):
    for block in range(ROWS // SPAN):
        coded = coded_ref[block * SPAN : (block + 1) * SPAN, :].astype(f32)[:8]
        facts = coded + pltpu.roll(coded, 128 - 8, 1) + pltpu.roll(coded, 128 - 16, 1)
        out_ref[block : block + 1, :] = facts[0:1]


def advantage_kernel(place_ref, facts_ref, out_ref):
    facts = facts_ref[...]
    row = lax.broadcasted_iota(jnp.int32, facts.shape, 0)
    lane = lax.broadcasted_iota(jnp.int32, facts.shape, 1)
    ids = pltpu.roll(facts, 128 - 2, 1)
    own = place_ref[0] * 4 + place_ref[1] * 2 + place_ref[2]
    other = place_ref[0] * 4 + place_ref[1] * 2 + 1 - place_ref[2]

    def fact(device, at):
        return jnp.sum(jnp.where((row == device) & (lane == at), facts, 0.0))

    for j in range(4):
        device, mine = (own, other)[j // 2], j % 2
        reward, group = fact(device, mine), fact(device, 2 + mine)
        held = jnp.where((lane < 2) & (ids == group), facts, 0.0)
        center = jnp.sum(held, keepdims=True) / GROUP
        second = jnp.sum(held * held, keepdims=True) / GROUP
        spread = jnp.maximum(jnp.sqrt(jnp.maximum(second - center * center, 0.0)), std_floor)
        out_ref[j : j + 1, :] = jnp.broadcast_to((reward - center) / spread, (1, 128))
        out_ref[4 + j : 5 + j, :] = jnp.full((1, 128), fact(device, 4 + mine), f32)


def project_most_kernel(
    place_ref, own_p, other_p, own_r, other_r,
    p0, spp, o0p, smp, s2p, omp, e0, spe, o0e, sme, s2e, ome,
    y_p, y_r, late_p, late_r, rows_p, rows_r, weight_p, weight_r, sems,
):
    z, xh = place_ref[3], place_ref[4]

    def place_of(dz, side):
        return pl.multiple_of((lax.rem(z + 4 + dz, 4) * 2 + side) * SHARD, 64)

    here, there = xh, 1 - xh
    copies = []
    for own, other, rows, weight, blocks, sem in (
        (own_p, other_p, rows_p, weight_p, (p0, smp, spp, o0p, s2p, omp), sems.at[0]),
        (own_r, other_r, rows_r, weight_r, (e0, sme, spe, o0e, s2e, ome), sems.at[1]),
    ):
        group = [
            pltpu.make_async_copy(own, rows.at[pl.ds(0, ROWS), :], sem),
            pltpu.make_async_copy(other, rows.at[pl.ds(ROWS, ROWS), :], sem),
        ]
        for block, dz, side in zip(blocks, (0, -1, 1, 0, 2, -1), (here, here, here, there, here, there)):
            group.append(pltpu.make_async_copy(block, weight.at[pl.ds(place_of(dz, side), SHARD), :], sem))
        for copy in group:
            copy.start()
        copies.append(group)
    for weight in (weight_p, weight_r):
        for dz in (1, 2):
            weight[pl.ds(place_of(dz, there), SHARD), :] = jnp.zeros((SHARD, HALF), bf16)

    def run(rows, weight, out, late):
        def step(j, carry):
            at = pl.multiple_of(j * CHUNK, CHUNK)
            out[:, pl.ds(at, CHUNK)] = dot(rows[...], weight[:, pl.ds(at, CHUNK)])
            return carry

        lax.fori_loop(0, HALF // CHUNK, step, 0)
        for k, dz in enumerate((1, 2)):
            at = pl.multiple_of(lax.rem(z + dz, 4) * PIECE, 128)
            part = rows[:, pl.ds(at, PIECE)].astype(f32)
            part = jnp.where(there == 0, part, pltpu.roll(part, PIECE - SHARD, 1))
            late[:, k * LATE : (k + 1) * LATE] = part[:, :LATE].astype(bf16)

    for copy in copies[0]:
        copy.wait()
    run(rows_p, weight_p, y_p, late_p)
    for copy in copies[1]:
        copy.wait()
    run(rows_r, weight_r, y_r, late_r)


def project_most(place, outs, weights):
    return pl.pallas_call(
        project_most_kernel,
        in_specs=[scalars()] + [in_place()] * (len(outs) + len(weights)),
        out_specs=[whole()] * 4,
        out_shape=[jax.ShapeDtypeStruct((2 * ROWS, HALF), f32)] * 2
        + [jax.ShapeDtypeStruct((2 * ROWS, 2 * LATE), bf16)] * 2,
        scratch_shapes=[
            VMEM((2 * ROWS, Q_WIDTH), bf16),
            VMEM((2 * ROWS, Q_WIDTH), bf16),
            VMEM((Q_WIDTH, HALF), bf16),
            VMEM((Q_WIDTH, HALF), bf16),
            pltpu.SemaphoreType.DMA((2,)),
        ],
        compiler_params=BIG,
        cost_estimate=pl.CostEstimate(
            flops=8 * ROWS * Q_WIDTH * HALF, bytes_accessed=24 << 20, transcendentals=0
        ),
    )(place, *outs, *weights)


def project_last_kernel(
    place_ref, rows_p, rows_r, opp, o2p, ope, o2e, y_p, y_r, mine_ref, theirs_ref,
    y_ref, stats_ref, late_p, late_r, sums,
):
    j = pl.program_id(0)

    @pl.when(j == 0)
    def _():
        sums[...] = jnp.zeros_like(sums)
        for late in (late_p, late_r):
            late[SHARD:LATE, :] = jnp.zeros((LATE - SHARD, CHUNK), bf16)
            late[LATE + SHARD :, :] = jnp.zeros((LATE - SHARD, CHUNK), bf16)

    for late, first, second in ((late_p, opp, o2p), (late_r, ope, o2e)):
        late[:SHARD, :] = first[...]
        late[LATE : LATE + SHARD, :] = second[...]

    def lanes_of(value):
        return value[:, :128] + value[:, 128:]

    target = jnp.concatenate([mine_ref[...], theirs_ref[...]], axis=0).astype(f32)
    y = y_p[...] + dot(rows_p[...], late_p[...])
    y_ref[...] = y
    sums[0] += lanes_of(y * y)
    sums[1] += lanes_of(y * target)
    y = y_r[...] + dot(rows_r[...], late_r[...])
    sums[2] += lanes_of(y * y)
    sums[3] += lanes_of(y * target)

    @pl.when(j == HALF // CHUNK - 1)
    def _():
        lane = lax.broadcasted_iota(jnp.int32, (2 * ROWS, 128), 1)
        stats = jnp.zeros((2 * ROWS, 128), f32)
        for k in range(4):
            stats = jnp.where(lane == k, jnp.sum(sums[k], axis=1, keepdims=True), stats)
        stats_ref[...] = stats


def project_last(place, parts, weights, target):
    steps = HALF // CHUNK
    chunk = lambda rows: pl.BlockSpec((rows, CHUNK), lambda j, place: (0, j))
    fixed = lambda width: pl.BlockSpec((2 * ROWS, width), lambda j, place: (0, 0))
    y_p, y_r, rows_p, rows_r = parts
    return pl.pallas_call(
        project_last_kernel,
        grid_spec=pltpu.PrefetchScalarGridSpec(
            num_scalar_prefetch=1,
            grid=(steps,),
            in_specs=[fixed(2 * LATE)] * 2
            + [chunk(SHARD)] * 4
            + [chunk(2 * ROWS)] * 2
            + [
                pl.BlockSpec((ROWS, CHUNK), lambda j, place: (0, TARGET_AT // CHUNK + place[2] * steps + j)),
                pl.BlockSpec((ROWS, CHUNK), lambda j, place: (0, TARGET_AT // CHUNK + (1 - place[2]) * steps + j)),
            ],
            out_specs=[chunk(2 * ROWS), fixed(128)],
            scratch_shapes=[
                VMEM((2 * LATE, CHUNK), bf16),
                VMEM((2 * LATE, CHUNK), bf16),
                VMEM((4, 2 * ROWS, 128), f32),
            ],
        ),
        out_shape=[
            jax.ShapeDtypeStruct((2 * ROWS, HALF), f32),
            jax.ShapeDtypeStruct((2 * ROWS, 128), f32),
        ],
        compiler_params=BIG,
        cost_estimate=pl.CostEstimate(
            flops=2 * ROWS * Q_WIDTH * HALF, bytes_accessed=10 << 20, transcendentals=0
        ),
    )(place, rows_p, rows_r, *weights, y_p, y_r, target, target)


def gradient_kernel(
    place_ref, own_ref, other_ref, y_ref, stats_ref, more_ref, target_ref, facts_ref,
    a0, a1, a2, a3, grad, rows,
):
    c, z = place_ref[2], place_ref[3]
    rows[:ROWS, :] = own_ref[...]
    rows[ROWS:, :] = other_ref[...]
    row = lax.broadcasted_iota(jnp.int32, (ROWS, 1), 0)
    for side in range(2):
        here = slice(side * ROWS, (side + 1) * ROWS)
        there = slice((1 - side) * ROWS, (2 - side) * ROWS)
        stats = stats_ref[here, :] + more_ref[there, :]
        policy_squares, policy_products = stats[:, 0:1], stats[:, 1:2]
        reference_squares, reference_products = stats[:, 2:3], stats[:, 3:4]
        one, two = 2 * side, 2 * side + 1
        early = row.astype(f32) < facts_ref[4 + one : 5 + one, 0:1]
        length = jnp.where(early, facts_ref[4 + one : 5 + one, 0:1], facts_ref[4 + two : 5 + two, 0:1])
        advantage = jnp.where(early, facts_ref[one : one + 1, 0:1], facts_ref[two : two + 1, 0:1])
        policy_norm = jnp.sqrt(policy_squares / D_OUT + norm_epsilon)
        reference_norm = jnp.sqrt(reference_squares / D_OUT + norm_epsilon)
        policy_self = policy_squares / (policy_norm * policy_norm)
        policy_cross = policy_products / policy_norm
        reference_self = reference_squares / (reference_norm * reference_norm)
        reference_cross = reference_products / reference_norm
        gain = ((policy_self - reference_self) - 2.0 * (policy_cross - reference_cross)) * (
            1.0 / (4.0 * math.sqrt(D_OUT))
        )
        weight = (advantage - kl_weight * (1.0 - jnp.exp(gain))) / length
        along = (policy_self - policy_cross) / D_OUT
        scale = weight / policy_norm
        slope = scale * (1.0 - along) / policy_norm
        side_lanes = c if side == 0 else 1 - c
        target = target_ref[:, pl.ds(pl.multiple_of(TARGET_AT + side_lanes * HALF, 128), HALF)].astype(f32)
        grad[here, :] = (y_ref[here, :] * slope - target * scale).astype(bf16)

    for d, out in enumerate((a0, a1, a2, a3)):
        first = pl.multiple_of(lax.rem(z + d, 4) * PIECE, 128)
        out[...] = outer(rows[:, pl.ds(first, PIECE)], grad[:, :PIECE])


def outer(rows, grad):
    return lax.dot_general(rows, grad, (((0,), (0,)), ((), ())), preferred_element_type=f32).astype(bf16)


def second_half_kernel(place_ref, own_ref, other_ref, grad_ref, b0, b1, b2, b3, rows, terms):
    rows[:ROWS, :] = own_ref[...]
    rows[ROWS:, :] = other_ref[...]
    for k in range(4):
        terms[...] = outer(rows[:, k * PIECE : (k + 1) * PIECE], grad_ref[:, PIECE:]).reshape(2, 4, 80, PIECE)
        for d, out in enumerate((b0, b1, b2, b3)):
            out[2 * k : 2 * k + 2] = terms[:, lax.rem(place_ref[0] + d, 4)]


def gradient(place, own, other, y, stats, more, target, facts):
    cost = pl.CostEstimate(flops=2 * ROWS * Q_WIDTH * HALF, bytes_accessed=8 << 20, transcendentals=0)
    *first, grad = pl.pallas_call(
        gradient_kernel,
        in_specs=[scalars()] + [whole()] * 7,
        out_specs=[whole()] * 5,
        out_shape=[jax.ShapeDtypeStruct((PIECE, PIECE), bf16)] * 4
        + [jax.ShapeDtypeStruct((2 * ROWS, HALF), bf16)],
        scratch_shapes=[VMEM((2 * ROWS, Q_WIDTH), bf16)],
        compiler_params=SMALL,
        cost_estimate=cost,
    )(place, own, other, y, stats, more, target, facts)
    second = pl.pallas_call(
        second_half_kernel,
        in_specs=[scalars()] + [whole()] * 3,
        out_specs=[whole()] * 4,
        out_shape=[jax.ShapeDtypeStruct((8, 80, PIECE), bf16)] * 4,
        scratch_shapes=[VMEM((2 * ROWS, Q_WIDTH), bf16), VMEM((2, 4, 80, PIECE), bf16)],
        compiler_params=SMALL,
        cost_estimate=cost,
    )(place, own, other, grad)
    return first, second


def total_of(refs, index):
    total = refs[0][index].astype(f32)
    for ref in refs[1:]:
        total = total + ref[index].astype(f32)
    return total


def sum_kernel(axis, place_at, place_ref, *refs):
    parts, outs = refs[:4], refs[4:]
    own = place_ref[place_at]
    for d, out in enumerate(outs):
        at = lax.rem(own + d, 4)
        index = (slice(None), at) if axis == 1 else (at,)
        out[...] = total_of(parts, index).astype(bf16)


def sum_blocks(place, parts, axis, place_at):
    shape = (2, 80, PIECE)
    return pl.pallas_call(
        functools.partial(sum_kernel, axis, place_at),
        in_specs=[scalars()] + [whole()] * 4,
        out_specs=[whole()] * 4,
        out_shape=[jax.ShapeDtypeStruct(shape, bf16)] * 4,
        compiler_params=SMALL,
        cost_estimate=pl.CostEstimate(flops=4 << 20, bytes_accessed=5 << 20, transcendentals=0),
    )(place, *parts)


def last_sum_kernel(place_ref, *refs):
    first, second, keep, send = refs[:4], refs[4:8], refs[8], refs[9]
    xh = place_ref[4]
    for out, at in ((keep, xh), (send, 1 - xh)):
        out[:, :PIECE] = total_of(first, (at,)).astype(bf16)
        out[:, PIECE:] = total_of(second, (at,)).astype(bf16)


def last_sum(place, first, second):
    return pl.pallas_call(
        last_sum_kernel,
        in_specs=[scalars()] + [whole()] * 8,
        out_specs=[whole()] * 2,
        out_shape=[jax.ShapeDtypeStruct((80, HALF), bf16)] * 2,
        compiler_params=SMALL,
    )(place, *first, *second)


def step_kernel(
    place_ref, square_ref, mine_ref, theirs_ref, weight_ref, ema_ref,
    update_out, moved_out, next_out, update, moved, after, sems,
):
    scale = lax.rsqrt(square_ref[0:1, 0:1] / (Q_WIDTH * D_OUT) + norm_epsilon)
    y_at, c = place_ref[0], place_ref[2]
    copies = []
    for d in range(4):
        rows = pl.ds(pl.multiple_of(lax.rem(y_at + d, 4) * 80, 16), 80)
        for side, grad_ref in ((c, mine_ref), (1 - c, theirs_ref)):
            lanes = pl.ds(pl.multiple_of(side * HALF, 128), HALF)
            step = grad_ref[d].astype(f32) * scale
            weight = weight_ref[rows, lanes].astype(f32) - step_size * step
            update[rows, lanes] = step
            moved[rows, lanes] = weight.astype(bf16)
            after[rows, lanes] = ema_decay * ema_ref[rows, lanes] + (1.0 - ema_decay) * weight
        for k, (source, out) in enumerate(((update, update_out), (moved, moved_out), (after, next_out))):
            copies.append(pltpu.make_async_copy(source.at[rows, :], out.at[rows, :], sems.at[k, d]))
            copies[-1].start()
    for copy in copies:
        copy.wait()


def take_step(place, square_sum, mine, theirs, policy_weight, ema_weight):
    return pl.pallas_call(
        step_kernel,
        in_specs=[scalars()] + [whole()] * 5,
        out_specs=[in_place()] * 3,
        out_shape=[
            jax.ShapeDtypeStruct((SHARD, D_OUT), f32),
            jax.ShapeDtypeStruct((SHARD, D_OUT), bf16),
            jax.ShapeDtypeStruct((SHARD, D_OUT), f32),
        ],
        scratch_shapes=[
            VMEM((SHARD, D_OUT), f32),
            VMEM((SHARD, D_OUT), bf16),
            VMEM((SHARD, D_OUT), f32),
            pltpu.SemaphoreType.DMA((3, 4)),
        ],
        compiler_params=pltpu.CompilerParams(vmem_limit_bytes=24 * 1024 * 1024),
    )(place, square_sum, mine, theirs, policy_weight, ema_weight)


def local(
    q_policy,
    kv_policy,
    q_reference,
    kv_reference,
    target,
    send_slot,
    lengths,
    rewards,
    group_ids,
    policy_weight,
    ema_weight,
):
    place = jnp.stack([lax.axis_index(name) for name in EVERY]).astype(jnp.int32)
    c = place[2]
    send = lax.ppermute

    X = ("xl", "xh")

    def half(weight):
        return lax.dynamic_slice_in_dim(weight, c * HALF, HALF, 1).astype(bf16)

    p0, e0 = half(policy_weight), half(ema_weight)
    smp, spp, o0p = send(p0, "z", ring(1)), send(p0, "z", ring(-1)), send(p0, X, ACROSS)
    sme, spe, o0e = send(e0, "z", ring(1)), send(e0, "z", ring(-1)), send(e0, X, ACROSS)
    s2p, s2e = send(smp, "z", ring(1)), send(spe, "z", ring(-1))
    omp, ome = send(smp, X, ACROSS), send(sme, X, ACROSS)
    opp, ope = send(o0p, "z", ring(-1)), send(o0e, "z", ring(-1))
    o2p, o2e = send(s2p, X, ACROSS), send(ome, "z", ring(1))

    exchange = functools.partial(lax.all_to_all, axis_name=DP, split_axis=0, concat_axis=0, tiled=True)
    rows_policy = exchange(
        pack(
            pack_policy_kernel,
            FACTS_AT + 128,
            (send_slot, q_policy, kv_policy, target),
            small=(rewards, group_ids, lengths),
        )
    )
    rows_reference = exchange(
        pack(
            pack_rows_kernel,
            Q_WIDTH + 1024,
            (send_slot, q_reference, kv_reference),
            after=(rows_policy, smp, spp, o0p, sme, spe, o0e),
        )
    )
    out_policy = attend(rows_policy, lengths, ())
    other_policy = send(out_policy, "c", FLIP)
    out_reference = attend(rows_reference, lengths, (s2p, s2e, omp, ome, opp))
    other_reference = send(out_reference, "c", FLIP)

    facts = pl.pallas_call(
        facts_kernel,
        grid=(1,),
        in_specs=[pl.BlockSpec((ROWS, 128), lambda i: (0, FACTS_AT // 128))],
        out_specs=pl.BlockSpec((SPAN, 128), lambda i: (0, 0)),
        out_shape=jax.ShapeDtypeStruct((SPAN, 128), f32),
        compiler_params=SMALL,
    )(rows_policy)
    facts = jnp.concatenate([facts, send(facts, "xh", FLIP)], axis=0)
    facts = jnp.concatenate([facts] + [send(facts, "z", ring(d)) for d in (1, 2, 3)], axis=0)
    advantages = pl.pallas_call(
        advantage_kernel,
        in_specs=[scalars(), whole()],
        out_specs=whole(),
        out_shape=jax.ShapeDtypeStruct((8, 128), f32),
        compiler_params=SMALL,
    )(place, facts)

    outs = (out_policy, other_policy, out_reference, other_reference)
    parts = project_most(place, outs, (p0, spp, o0p, smp, s2p, omp, e0, spe, o0e, sme, s2e, ome))
    y_policy, stats = project_last(place, parts, (opp, o2p, ope, o2e), rows_policy)
    more = send(stats, "c", FLIP)
    first, second = gradient(
        place, out_policy, other_policy, y_policy, stats, more, rows_policy, advantages
    )

    first = [first[0]] + [send(first[d], "z", ring(d)) for d in (1, 2, 3)]
    second = [second[0]] + [send(second[d], "y", ring(d)) for d in (1, 2, 3)]
    first = sum_blocks(place, [piece.reshape(2, 4, 80, PIECE) for piece in first], 1, 0)
    second = sum_blocks(place, [piece.reshape(4, 2, 80, PIECE) for piece in second], 0, 3)
    first = [first[0]] + [send(first[d], "y", ring(d)) for d in (1, 2, 3)]
    second = [second[0]] + [send(second[d], "z", ring(d)) for d in (1, 2, 3)]
    kept, given = last_sum(place, first, second)

    def add(one, two):
        return (one.astype(f32) + two.astype(f32)).astype(bf16)

    block = add(kept, send(given, X, ACROSS))
    block = add(block, send(block, "xl", FLIP))

    mine = jnp.stack([block] + [send(block, "y", ring(-d)) for d in (1, 2, 3)])
    theirs = send(mine, "c", FLIP)
    square = jnp.sum(jnp.square(mine.astype(f32)), axis=(1, 2)) + jnp.sum(
        jnp.square(theirs.astype(f32)), axis=(1, 2)
    )
    square = (square[0] + square[2]) + (square[1] + square[3])
    square = jnp.broadcast_to(square, (8, 128))
    square = square + send(square, X, ACROSS)
    square = (square + send(square, "z", ring(2))) + (send(square, "z", ring(1)) + send(square, "z", ring(3)))
    return tuple(take_step(place, square, mine, theirs, policy_weight, ema_weight))


def solution(mesh):
    names = Mesh(mesh.devices.reshape(4, 2, 2, 4, 2), EVERY)
    rows, whole_rows = P(EVERY, None), P(EVERY)
    in_specs = (rows,) * 7 + (whole_rows,) * 2 + (P(FSDP, None),) * 2
    out_specs = (P(FSDP, None),) * 3
    return jax.shard_map(local, mesh=names, in_specs=in_specs, out_specs=out_specs, check_vma=False)
```

time: 309 us -> 282 us (0.913)
  waiting for transfers between devices: 153 us -> 129 us
  other arithmetic: 3.85 us -> 0.74 us
    ppermute x1, waiting for transfers between devices: 19.6 us -> 4.25 us  [local(): facts = jnp.concatenate([facts, send(facts, 'xh', FLIP)], axis=0)]
    ppermute x11 -> x16, starting transfers between devices: 16.3 us -> 25.8 us  [the longest x2 3.93 us: local(): opp, ope = (send(o0p, 'z', ring(-1)), send(o0e, 'z', ring(-1)))]
    ppermute x11 -> x16, waiting for transfers between devices: 76.6 us -> 67.1 us  [the longest x2 19.1 us: local(): omp, ome = (send(smp, X, ACROSS), send(sme, X, ACROSS))]
    pallas_call x6 -> x9, Pallas kernels: 43.2 us -> 48.2 us  [the longest x1 15.7 us: project_most(): pl.pallas_call(project_most_kernel, in_specs=[scalars()] + [in_place()] *...]
    ppermute x3, starting transfers between devices: 6.56 us -> 2.11 us  [local(): first = [first[0]] + [send(first[d], 'z', ring(d)) for d in (1, 2, 3)]]
    slice x3 -> x0, local copies, waits for them, and re-layouts: 4.36 us -> none  [the longest x1 2.14 us: local(): s2p = send(sm[:SHARD], 'z', ring(1))]
    pallas_call x2, Pallas kernels: 6.02 us -> 1.93 us  [sum_blocks(): pl.pallas_call(functools.partial(sum_kernel, axis, place_at), in_specs=[s...]
    ppermute x3, waiting for transfers between devices: 28.4 us -> 32.3 us  [local(): second = [second[0]] + [send(second[d], 'y', ring(d)) for d in (1, 2, 3)]]
  transfers between devices with their start and end apart: 40 -> 45, of which waited for: 22 -> 25; matrix products, arithmetic and copies ran while one was open for 3% -> 1% of each run, Pallas kernels for 9% -> 15%
where the time goes in v2:
time: 282 us; the launch traced here: 281 us
  waiting for transfers between devices  129 us (46%)
  starting transfers between devices  68.6 us (24%)
  Pallas kernels  64.7 us (23%)
  local copies, waits for them, and re-layouts  14.2 us (5%)
  between operations  3.68 us (1%)
    ppermute x3, waiting for transfers between devices, local(): second = [second[0]] + [send(second[d], 'y', ring(d)) for d in (1, 2, 3)]  32.3 us
    ppermute x2, waiting for transfers between devices, local(): omp, ome = (send(smp, X, ACROSS), send(sme, X, ACROSS))  19.1 us
    pallas_call x1, Pallas kernels, project_most(): pl.pallas_call(project_most_kernel, in_specs=[scalars()] + [in_place()] *...  15.7 us
    ppermute x1, waiting for transfers between devices, local(): send(e0, 'z', ring(1))  15.3 us
    pallas_call x2, Pallas kernels, attend(): pl.pallas_call(attention_kernel, grid=(KV_HEADS,), in_specs=[scalars(), p...  13.8 us
    ppermute x1, waiting for transfers between devices, local(): send(p0, 'z', ring(1))  13.1 us
    pallas_call x1, Pallas kernels, project_last(): pl.pallas_call(project_last_kernel, grid_spec=pltpu.PrefetchScalarGridSpe...  10.5 us
    unnamed x58, local copies, waits for them, and re-layouts  10.3 us
  transfers between devices with their start and end apart: 45, of which 25 were waited for; matrix products, arithmetic and copies ran while one was open for 1% of the time, Pallas kernels for 15%

profile of v2, /device:TPU:0, one launch (start us, length us, event | category | flops | bytes accessed | tf_op | source)
XLA Modules:
  0.0 281.4 jit_solution(13037767412213748760)
XLA Ops:
  0.6 4.6 %shard_map.130 = bf16[256,6272]{1,0:T(8,128)(2,1)} custom-call(f32[2]{0:T(128)} %rewards_ref.1, s32[2]{0:T(128)} %ids_ref.1, s32[1,2]{1,0:T(1,128)} %lengths_ref.5, s32[1,256]{1,0:T(1,128)} %slots_ref.3, bf16[256,2560]{1,0:T(8,128)(2,1)} %q_ref.2, bf16[256,1024]{1,0:T(8,128)(2,1)} %kv_ref.2, bf16[256,2560]{1,0:T(8,128)(2,1)} %target_ref.1), custom_call_target="tpu_custom_call" | custom-call | flops 822083584 | bytes 6422528 | tf_op jit(solution)/shard_map/pallas_call | solution.py:106
  5.2 5.6 %all-to-all-start = ((bf16[16,16,6272]{2,1,0:T(8,128)(2,1)}), bf16[16,16,6272]{2,1,0:T(8,128)(2,1)S(1)}, u32[]{:S(2)}, u32[]{:S(2)}) async-start(bf16[16,16,6272]{2,1,0:T(8,128)(2,1)} %bitcast.41), calls=%async_computation | async-start | bytes 6422528 | tf_op jit(solution)/shard_map/all_to_all | solution.py:528
  22.1 13.1 %collective-permute-done.1.rest_1_.smp = bf16[320,1280]{1,0:T(8,128)(2,1)S(1)} collective-permute-done((bf16[320,1280]{1,0:T(8,128)(2,1)S(1)}, bf16[320,1280]{1,0:T(8,128)(2,1)S(1)}, u32[]{:S(2)}, u32[]{:S(2)}) %collective-permute-start.1) | collective-permute-done | bytes 819232 | tf_op jit(solution)/shard_map/ppermute | solution.py:520
  37.2 15.3 %collective-permute-done.4.rest_4_.sme = bf16[320,1280]{1,0:T(8,128)(2,1)S(1)} collective-permute-done((bf16[320,1280]{1,0:T(8,128)(2,1)S(1)}, bf16[320,1280]{1,0:T(8,128)(2,1)S(1)}, u32[]{:S(2)}, u32[]{:S(2)}) %collective-permute-start.4) | collective-permute-done | bytes 819232 | tf_op jit(solution)/shard_map/ppermute | solution.py:521
  59.5 3.3 %shard_map.132 = bf16[256,3584]{1,0:T(8,128)(2,1)} custom-call(s32[1,256]{1,0:T(1,128)} %slots_ref.3, bf16[256,2560]{1,0:T(8,128)(2,1)} %q_ref.3, bf16[256,1024]{1,0:T(8,128)(2,1)} %kv_ref.3, bf16[256,6272]{1,0:T(8,128)(2,1)} %bitcast.22, bf16[320,1280]{1,0:T(8,128)(2,1)} %copy-done.11, bf16[320,1280]{1,0:T(8,128)(2,1)} %collective-permute-done.2.rest_2_.spp, ...), custom_call_target="tpu_custom_call" | custom-call | flops 469762048 | bytes 3670016 | tf_op jit(solution)/shard_map/pallas_call | solution.py:106
  62.8 4.5 %all-to-all-start.1 = ((bf16[16,16,3584]{2,1,0:T(8,128)(2,1)}), bf16[16,16,3584]{2,1,0:T(8,128)(2,1)S(1)}, u32[]{:S(2)}, u32[]{:S(2)}) async-start(bf16[16,16,3584]{2,1,0:T(8,128)(2,1)} %bitcast.42), calls=%async_computation.1 | async-start | bytes 3670016 | tf_op jit(solution)/shard_map/all_to_all | solution.py:536
  75.2 6.8 %shard_map.131.own_p.own_ref = bf16[256,2560]{1,0:T(8,128)(2,1)} custom-call(s32[1,2]{1,0:T(1,128)} %lengths_ref.5, bf16[256,6272]{1,0:T(8,128)(2,1)} %bitcast.23, bf16[256,6272]{1,0:T(8,128)(2,1)} %bitcast.24, bf16[256,6272]{1,0:T(8,128)(2,1)} %bitcast.25), custom_call_target="tpu_custom_call" | custom-call | flops 671088640 | bytes 4194304 | tf_op jit(solution)/shard_map/pallas_call | solution.py:139
  82.0 7.2 %collective-permute-done.7.rest_0_.s2p = bf16[320,1280]{1,0:T(8,128)(2,1)S(1)} collective-permute-done((bf16[320,1280]{1,0:T(8,128)(2,1)S(1)}, bf16[320,1280]{1,0:T(8,128)(2,1)S(1)}, u32[]{:S(2)}, u32[]{:S(2)}) %collective-permute-start.7) | collective-permute-done | bytes 819232 | tf_op jit(solution)/shard_map/ppermute | solution.py:522
  91.5 16.8 %collective-permute-done.9.rest_2_.omp = bf16[320,1280]{1,0:T(8,128)(2,1)S(1)} collective-permute-done((bf16[320,1280]{1,0:T(8,128)(2,1)S(1)}, bf16[320,1280]{1,0:T(8,128)(2,1)S(1)}, u32[]{:S(2)}, u32[]{:S(2)}) %collective-permute-start.9) | collective-permute-done | bytes 819232 | tf_op jit(solution)/shard_map/ppermute | solution.py:523
  111.4 7.0 %shard_map.133.own_r = bf16[256,2560]{1,0:T(8,128)(2,1)} custom-call(s32[1,2]{1,0:T(1,128)} %lengths_ref.5, bf16[256,3584]{1,0:T(8,128)(2,1)} %bitcast.38, bf16[256,3584]{1,0:T(8,128)(2,1)} %bitcast.39, bf16[256,3584]{1,0:T(8,128)(2,1)} %bitcast.40, bf16[320,1280]{1,0:T(8,128)(2,1)} %copy-done.20, bf16[320,1280]{1,0:T(8,128)(2,1)} %collective-permute-done.8.rest_1_.s2e, ...), custom_call_target="tpu_custom_call" | custom-call | flops 671088640 | bytes 4194304 | tf_op jit(solution)/shard_map/pallas_call | solution.py:139
  124.0 4.2 %collective-permute-done.17 = f32[16,128]{1,0:T(8,128)S(1)} collective-permute-done((f32[16,128]{1,0:T(8,128)S(1)}, f32[16,128]{1,0:T(8,128)S(1)}, u32[]{:S(2)}, u32[]{:S(2)}) %collective-permute-start.17) | collective-permute-done | bytes 8224 | tf_op jit(solution)/shard_map/ppermute | solution.py:557
  128.6 4.4 %collective-permute-start.19 = (f32[32,128]{1,0:T(8,128)S(1)}, f32[32,128]{1,0:T(8,128)S(1)}, u32[]{:S(2)}, u32[]{:S(2)}) collective-permute-start(f32[32,128]{1,0:T(8,128)S(1)} %pad_maximum_fusion.1), channel_id=1, source_target_pairs={{0,4},{2,6},{4,0},{6,2},{1,5},{3,7},{5,1},{7,3},{8,12},{10,14},{12... | collective-permute-start | bytes 49160 | tf_op jit(solution)/shard_map/ppermute | solution.py:558
  133.0 15.7 %shard_map.134 = (f32[512,1280]{1,0:T(8,128)}, f32[512,1280]{1,0:T(8,128)}, bf16[512,768]{1,0:T(8,128)(2,1)}, bf16[512,768]{1,0:T(8,128)(2,1)}) custom-call(s32[5]{0:T(128)} %stack.38.place_ref, bf16[256,2560]{1,0:T(8,128)(2,1)} %shard_map.131.own_p.own_ref, bf16[256,2560]{1,0:T(8,128)(2,1)} %collective-permute-done.other_p.other_ref, ...), custom_call_target="tpu_custom_call" | custom-call | flops 6710886400 | bytes 25165824 | tf_op jit(solution)/shard_map/pallas_call | solution.py:238
  150.3 10.5 %shard_map.135 = (f32[512,1280]{1,0:T(8,128)}, f32[512,128]{1,0:T(8,128)}) custom-call(s32[5]{0:T(128)} %stack.38.place_ref, bf16[512,768]{1,0:T(8,128)(2,1)} %get-tuple-element.28.rows_p, bf16[512,768]{1,0:T(8,128)(2,1)} %get-tuple-element.29.rows_r, bf16[320,1280]{1,0:T(8,128)(2,1)} %copy-done.10, bf16[320,1280]{1,0:T(8,128)(2,1)} %copy-done.25, ...), custom_call_target="tpu_custom_call" | custom-call | flops 1677721600 | bytes 10485760 | tf_op jit(solution)/shard_map/pallas_call | solution.py:301
  165.3 4.5 %shard_map.138 = (bf16[640,640]{1,0:T(8,128)(2,1)S(1)}, bf16[640,640]{1,0:T(8,128)(2,1)S(1)}, bf16[640,640]{1,0:T(8,128)(2,1)S(1)}, bf16[640,640]{1,0:T(8,128)(2,1)S(1)}, bf16[512,1280]{1,0:T(8,128)(2,1)S(1)}) custom-call(s32[5]{0:T(128)S(1)} %copy-done.8, bf16[256,2560]{1,0:T(8,128)(2,1)S(1)} %copy-done.3, ...), custom_call_target="tpu_custom_call" | custom-call | flops 1677721600 | bytes 8388608 | tf_op jit(solution)/shard_map/pallas_call | solution.py:386
  169.8 4.1 %shard_map.140 = (bf16[8,80,640]{2,1,0:T(8,128)(2,1)S(1)}, bf16[8,80,640]{2,1,0:T(8,128)(2,1)S(1)}, bf16[8,80,640]{2,1,0:T(8,128)(2,1)S(1)}, bf16[8,80,640]{2,1,0:T(8,128)(2,1)S(1)}) custom-call(s32[5]{0:T(128)S(1)} %copy-done.8, bf16[256,2560]{1,0:T(8,128)(2,1)S(1)} %copy-done.3, bf16[256,2560]{1,0:T(8,128)(2,1)} %collective-permute-done.other_p.other_ref, ...), custom_call_target="tpu_custom_call" | custom-call | flops 1677721600 | bytes 8388608 | tf_op jit(solution)/shard_map/pallas_call | solution.py:396
  181.4 14.1 %collective-permute-done.27 = bf16[8,80,640]{2,1,0:T(8,128)(2,1)S(1)} collective-permute-done((bf16[8,80,640]{2,1,0:T(8,128)(2,1)S(1)}, bf16[8,80,640]{2,1,0:T(8,128)(2,1)S(1)}, u32[]{:S(2)}, u32[]{:S(2)}) %collective-permute-start.27) | collective-permute-done | bytes 819232 | tf_op jit(solution)/shard_map/ppermute | solution.py:576
  195.8 18.1 %collective-permute-done.28 = bf16[8,80,640]{2,1,0:T(8,128)(2,1)S(1)} collective-permute-done((bf16[8,80,640]{2,1,0:T(8,128)(2,1)S(1)}, bf16[8,80,640]{2,1,0:T(8,128)(2,1)S(1)}, u32[]{:S(2)}, u32[]{:S(2)}) %collective-permute-start.28) | collective-permute-done | bytes 819232 | tf_op jit(solution)/shard_map/ppermute | solution.py:576
  230.2 3.3 %collective-permute-done.25.refs_2_ = bf16[2,80,640]{2,1,0:T(8,128)(2,1)S(1)} collective-permute-done((bf16[2,80,640]{2,1,0:T(8,128)(2,1)S(1)}, bf16[2,80,640]{2,1,0:T(8,128)(2,1)S(1)}, u32[]{:S(2)}, u32[]{:S(2)}) %collective-permute-start.25) | collective-permute-done | bytes 204832 | tf_op jit(solution)/shard_map/ppermute | solution.py:579
  236.6 5.2 %collective-permute-done.33 = bf16[80,1280]{1,0:T(8,128)(2,1)S(1)} collective-permute-done((bf16[80,1280]{1,0:T(8,128)(2,1)S(1)}, bf16[80,1280]{1,0:T(8,128)(2,1)S(1)}, u32[]{:S(2)}, u32[]{:S(2)}) %collective-permute-start.33) | collective-permute-done | bytes 204832 | tf_op jit(solution)/shard_map/ppermute | solution.py:586
  242.0 5.7 %collective-permute-done.34 = bf16[80,1280]{1,0:T(8,128)(2,1)S(1)} collective-permute-done((bf16[80,1280]{1,0:T(8,128)(2,1)S(1)}, bf16[80,1280]{1,0:T(8,128)(2,1)S(1)}, u32[]{:S(2)}, u32[]{:S(2)}) %collective-permute-start.34) | collective-permute-done | bytes 204832 | tf_op jit(solution)/shard_map/ppermute | solution.py:587
  247.8 3.8 %collective-permute-start.35 = (bf16[80,1280]{1,0:T(8,128)(2,1)S(1)}, bf16[80,1280]{1,0:T(8,128)(2,1)S(1)}, u32[]{:S(2)}, u32[]{:S(2)}) collective-permute-start(bf16[80,1280]{1,0:T(8,128)(2,1)S(1)} %add_convert_fusion), channel_id=1, source_target_pairs={{0,96},{32,0},{64,32},{96,64},{1,97},{33,1},{65,33},{97,65},{2,98}... | collective-permute-start | bytes 614408 | tf_op jit(solution)/shard_map/ppermute | solution.py:589
  252.6 4.5 %collective-permute-done.35 = bf16[80,1280]{1,0:T(8,128)(2,1)S(1)} collective-permute-done((bf16[80,1280]{1,0:T(8,128)(2,1)S(1)}, bf16[80,1280]{1,0:T(8,128)(2,1)S(1)}, u32[]{:S(2)}, u32[]{:S(2)}) %collective-permute-start.35) | collective-permute-done | bytes 204832 | tf_op jit(solution)/shard_map/ppermute | solution.py:589
  277.1 4.2 %shard_map.143 = (f32[320,2560]{1,0:T(8,128)}, bf16[320,2560]{1,0:T(8,128)(2,1)}, f32[320,2560]{1,0:T(8,128)}) custom-call(s32[5]{0:T(128)S(1)} %copy-done.8, f32[8,128]{1,0:T(8,128)S(1)} %add_add_fusion.square_ref, bf16[4,80,1280]{2,1,0:T(8,128)(2,1)S(1)} %get-tuple-element.54.mine_ref, bf16[4,80,1280]{2,1,0:T(8,128)(2,1)S(1)} %collective-permute-done.38.theirs_ref, ...), custom_call_target="tpu_custom_call" | custom-call | tf_op jit(solution)/shard_map/pallas_call | solution.py:478
  (152 shorter events, 91.1 us)
Async XLA Ops:
  5.2 52.6 %all-to-all-start = ((bf16[16,16,6272]{2,1,0:T(8,128)(2,1)}), bf16[16,16,6272]{2,1,0:T(8,128)(2,1)S(1)}, u32[]{:S(2)}, u32[]{:S(2)}) async-start(bf16[16,16,6272]{2,1,0:T(8,128)(2,1)} %bitcast.41), calls=%async_computation | async-start | bytes 6422528 | tf_op jit(solution)/shard_map/all_to_all | solution.py:528
  12.0 23.2 %collective-permute-start.1 = (bf16[320,1280]{1,0:T(8,128)(2,1)S(1)}, bf16[320,1280]{1,0:T(8,128)(2,1)S(1)}, u32[]{:S(2)}, u32[]{:S(2)}) collective-permute-start(bf16[320,1280]{1,0:T(8,128)(2,1)S(1)} %constant_dynamic-slice_fusion.p0), channel_id=1, source_target_pairs={{0,2},{2,4},{4,6},{6,0},{1,3},{3,5},{5,7},{7,1},{8,10},{10,12},{12... | collective-permute-start | bytes 2457608 | tf_op jit(solution)/shard_map/ppermute | solution.py:520
  14.0 23.2 %collective-permute-start.3 = (bf16[320,1280]{1,0:T(8,128)(2,1)S(1)}, bf16[320,1280]{1,0:T(8,128)(2,1)S(1)}, u32[]{:S(2)}, u32[]{:S(2)}) collective-permute-start(bf16[320,1280]{1,0:T(8,128)(2,1)S(1)} %constant_dynamic-slice_fusion.p0), channel_id=1, source_target_pairs={{16,1},{1,16},{0,17},{17,0},{18,3},{3,18},{2,19},{19,2},{20,5},{5,... | collective-permute-start | bytes 2457608 | tf_op jit(solution)/shard_map/ppermute | solution.py:520
  18.7 33.8 %collective-permute-start.4 = (bf16[320,1280]{1,0:T(8,128)(2,1)S(1)}, bf16[320,1280]{1,0:T(8,128)(2,1)S(1)}, u32[]{:S(2)}, u32[]{:S(2)}) collective-permute-start(bf16[320,1280]{1,0:T(8,128)(2,1)S(1)} %dynamic-slice_convert_fusion.e0), channel_id=1, source_target_pairs={{0,2},{2,4},{4,6},{6,0},{1,3},{3,5},{5,7},{7,1},{8,10},{10,12},{12... | collective-permute-start | bytes 2457608 | tf_op jit(solution)/shard_map/ppermute | solution.py:521
  20.7 31.8 %collective-permute-start.5 = (bf16[320,1280]{1,0:T(8,128)(2,1)S(1)}, bf16[320,1280]{1,0:T(8,128)(2,1)S(1)}, u32[]{:S(2)}, u32[]{:S(2)}) collective-permute-start(bf16[320,1280]{1,0:T(8,128)(2,1)S(1)} %dynamic-slice_convert_fusion.e0), channel_id=1, source_target_pairs={{0,6},{2,0},{4,2},{6,4},{1,7},{3,1},{5,3},{7,5},{8,14},{10,8},{12,... | collective-permute-start | bytes 2457608 | tf_op jit(solution)/shard_map/ppermute | solution.py:521
  22.0 31.0 %collective-permute-start.6 = (bf16[320,1280]{1,0:T(8,128)(2,1)S(1)}, bf16[320,1280]{1,0:T(8,128)(2,1)S(1)}, u32[]{:S(2)}, u32[]{:S(2)}) collective-permute-start(bf16[320,1280]{1,0:T(8,128)(2,1)S(1)} %dynamic-slice_convert_fusion.e0), channel_id=1, source_target_pairs={{16,1},{1,16},{0,17},{17,0},{18,3},{3,18},{2,19},{19,2},{20,5},{5,... | collective-permute-start | bytes 2457608 | tf_op jit(solution)/shard_map/ppermute | solution.py:521
  35.2 22.6 %collective-permute-start.2 = (bf16[320,1280]{1,0:T(8,128)(2,1)S(1)}, bf16[320,1280]{1,0:T(8,128)(2,1)}, u32[]{:S(2)}, u32[]{:S(2)}) collective-permute-start(bf16[320,1280]{1,0:T(8,128)(2,1)S(1)} %constant_dynamic-slice_fusion.p0), channel_id=1, source_target_pairs={{0,6},{2,0},{4,2},{6,4},{1,7},{3,1},{5,3},{7,5},{8,14},{10,8},{12,... | collective-permute-start | bytes 2457608 | tf_op jit(solution)/shard_map/ppermute | solution.py:520
  62.8 47.3 %all-to-all-start.1 = ((bf16[16,16,3584]{2,1,0:T(8,128)(2,1)}), bf16[16,16,3584]{2,1,0:T(8,128)(2,1)S(1)}, u32[]{:S(2)}, u32[]{:S(2)}) async-start(bf16[16,16,3584]{2,1,0:T(8,128)(2,1)} %bitcast.42), calls=%async_computation.1 | async-start | bytes 3670016 | tf_op jit(solution)/shard_map/all_to_all | solution.py:536
  67.3 21.9 %collective-permute-start.7 = (bf16[320,1280]{1,0:T(8,128)(2,1)S(1)}, bf16[320,1280]{1,0:T(8,128)(2,1)S(1)}, u32[]{:S(2)}, u32[]{:S(2)}) collective-permute-start(bf16[320,1280]{1,0:T(8,128)(2,1)S(1)} %copy-done.12), channel_id=1, source_target_pairs={{0,2},{2,4},{4,6},{6,0},{1,3},{3,5},{5,7},{7,1},{8,10},{10,12},{12... | collective-permute-start | bytes 2457608 | tf_op jit(solution)/shard_map/ppermute | solution.py:522
  69.0 22.5 %collective-permute-start.10 = (bf16[320,1280]{1,0:T(8,128)(2,1)}, bf16[320,1280]{1,0:T(8,128)(2,1)S(1)}, u32[]{:S(2)}, u32[]{:S(2)}) collective-permute-start(bf16[320,1280]{1,0:T(8,128)(2,1)} %copy-done.15), channel_id=1, source_target_pairs={{16,1},{1,16},{0,17},{17,0},{18,3},{3,18},{2,19},{19,2},{20,5},{5,... | collective-permute-start | bytes 2457608 | tf_op jit(solution)/shard_map/ppermute | solution.py:523
  70.9 37.4 %collective-permute-start.9 = (bf16[320,1280]{1,0:T(8,128)(2,1)S(1)}, bf16[320,1280]{1,0:T(8,128)(2,1)S(1)}, u32[]{:S(2)}, u32[]{:S(2)}) collective-permute-start(bf16[320,1280]{1,0:T(8,128)(2,1)S(1)} %copy-done.12), channel_id=1, source_target_pairs={{16,1},{1,16},{0,17},{17,0},{18,3},{3,18},{2,19},{19,2},{20,5},{5,... | collective-permute-start | bytes 2457608 | tf_op jit(solution)/shard_map/ppermute | solution.py:523
  72.3 36.0 %collective-permute-start.11 = (bf16[320,1280]{1,0:T(8,128)(2,1)S(1)}, bf16[320,1280]{1,0:T(8,128)(2,1)S(1)}, u32[]{:S(2)}, u32[]{:S(2)}) collective-permute-start(bf16[320,1280]{1,0:T(8,128)(2,1)S(1)} %copy-done.14), channel_id=1, source_target_pairs={{0,6},{2,0},{4,2},{6,4},{1,7},{3,1},{5,3},{7,5},{8,14},{10,8},{12,... | collective-permute-start | bytes 2457608 | tf_op jit(solution)/shard_map/ppermute | solution.py:524
  73.9 36.3 %collective-permute-start.8 = (bf16[320,1280]{1,0:T(8,128)(2,1)}, bf16[320,1280]{1,0:T(8,128)(2,1)}, u32[]{:S(2)}, u32[]{:S(2)}) collective-permute-start(bf16[320,1280]{1,0:T(8,128)(2,1)} %copy-done.17), channel_id=1, source_target_pairs={{0,6},{2,0},{4,2},{6,4},{1,7},{3,1},{5,3},{7,5},{8,14},{10,8},{12,... | collective-permute-start | bytes 2457608 | tf_op jit(solution)/shard_map/ppermute | solution.py:522
  89.2 39.1 %collective-permute-start = (bf16[256,2560]{1,0:T(8,128)(2,1)}, bf16[256,2560]{1,0:T(8,128)(2,1)}, u32[]{:S(2)}, u32[]{:S(2)}) collective-permute-start(bf16[256,2560]{1,0:T(8,128)(2,1)} %shard_map.131.own_p.own_ref), channel_id=1, source_target_pairs={{0,8},{8,0},{1,9},{9,1},{2,10},{10,2},{3,11},{11,3},{4,12},{12,4},... | collective-permute-start | bytes 3932168 | tf_op jit(solution)/shard_map/ppermute | solution.py:545
  119.0 29.7 %collective-permute-start.14 = (bf16[320,1280]{1,0:T(8,128)(2,1)}, bf16[320,1280]{1,0:T(8,128)(2,1)S(1)}, u32[]{:S(2)}, u32[]{:S(2)}) collective-permute-start(bf16[320,1280]{1,0:T(8,128)(2,1)} %copy-done.16), channel_id=1, source_target_pairs={{0,6},{2,0},{4,2},{6,4},{1,7},{3,1},{5,3},{7,5},{8,14},{10,8},{12,... | collective-permute-start | bytes 2457608 | tf_op jit(solution)/shard_map/ppermute | solution.py:524
  121.3 27.5 %collective-permute-start.13 = (bf16[320,1280]{1,0:T(8,128)(2,1)}, bf16[320,1280]{1,0:T(8,128)(2,1)S(1)}, u32[]{:S(2)}, u32[]{:S(2)}) collective-permute-start(bf16[320,1280]{1,0:T(8,128)(2,1)} %copy-done.20), channel_id=1, source_target_pairs={{16,1},{1,16},{0,17},{17,0},{18,3},{3,18},{2,19},{19,2},{20,5},{5,... | collective-permute-start | bytes 2457608 | tf_op jit(solution)/shard_map/ppermute | solution.py:525
  128.3 32.6 %collective-permute-start.18 = (f32[32,128]{1,0:T(8,128)S(1)}, f32[32,128]{1,0:T(8,128)S(1)}, u32[]{:S(2)}, u32[]{:S(2)}) collective-permute-start(f32[32,128]{1,0:T(8,128)S(1)} %pad_maximum_fusion.1), channel_id=1, source_target_pairs={{0,2},{2,4},{4,6},{6,0},{1,3},{3,5},{5,7},{7,1},{8,10},{10,12},{12... | collective-permute-start | bytes 49160 | tf_op jit(solution)/shard_map/ppermute | solution.py:558
  128.6 32.3 %collective-permute-start.19 = (f32[32,128]{1,0:T(8,128)S(1)}, f32[32,128]{1,0:T(8,128)S(1)}, u32[]{:S(2)}, u32[]{:S(2)}) collective-permute-start(f32[32,128]{1,0:T(8,128)S(1)} %pad_maximum_fusion.1), channel_id=1, source_target_pairs={{0,4},{2,6},{4,0},{6,2},{1,5},{3,7},{5,1},{7,3},{8,12},{10,14},{12... | collective-permute-start | bytes 49160 | tf_op jit(solution)/shard_map/ppermute | solution.py:558
  173.9 21.6 %collective-permute-start.27 = (bf16[8,80,640]{2,1,0:T(8,128)(2,1)S(1)}, bf16[8,80,640]{2,1,0:T(8,128)(2,1)S(1)}, u32[]{:S(2)}, u32[]{:S(2)}) collective-permute-start(bf16[8,80,640]{2,1,0:T(8,128)(2,1)S(1)} %get-tuple-element.44), channel_id=1, source_target_pairs={{0,32},{32,64},{64,96},{96,0},{1,33},{33,65},{65,97},{97,1},{2,34}... | collective-permute-start | bytes 2457608 | tf_op jit(solution)/shard_map/ppermute | solution.py:576
  175.5 38.5 %collective-permute-start.28 = (bf16[8,80,640]{2,1,0:T(8,128)(2,1)S(1)}, bf16[8,80,640]{2,1,0:T(8,128)(2,1)S(1)}, u32[]{:S(2)}, u32[]{:S(2)}) collective-permute-start(bf16[8,80,640]{2,1,0:T(8,128)(2,1)S(1)} %get-tuple-element.45), channel_id=1, source_target_pairs={{0,64},{32,96},{64,0},{96,32},{1,65},{33,97},{65,1},{97,33},{2,66}... | collective-permute-start | bytes 2457608 | tf_op jit(solution)/shard_map/ppermute | solution.py:576
  178.2 35.8 %collective-permute-start.29 = (bf16[8,80,640]{2,1,0:T(8,128)(2,1)S(1)}, bf16[8,80,640]{2,1,0:T(8,128)(2,1)S(1)}, u32[]{:S(2)}, u32[]{:S(2)}) collective-permute-start(bf16[8,80,640]{2,1,0:T(8,128)(2,1)S(1)} %get-tuple-element.46), channel_id=1, source_target_pairs={{0,96},{32,0},{64,32},{96,64},{1,97},{33,1},{65,33},{97,65},{2,98}... | collective-permute-start | bytes 2457608 | tf_op jit(solution)/shard_map/ppermute | solution.py:576
  179.6 38.2 %collective-permute-start.21 = (bf16[640,640]{1,0:T(8,128)(2,1)S(1)}, bf16[640,640]{1,0:T(8,128)(2,1)S(1)}, u32[]{:S(2)}, u32[]{:S(2)}) collective-permute-start(bf16[640,640]{1,0:T(8,128)(2,1)S(1)} %get-tuple-element.35), channel_id=1, source_target_pairs={{0,2},{2,4},{4,6},{6,0},{1,3},{3,5},{5,7},{7,1},{8,10},{10,12},{12... | collective-permute-start | bytes 2457608 | tf_op jit(solution)/shard_map/ppermute | solution.py:575
  181.4 38.4 %collective-permute-start.22 = (bf16[640,640]{1,0:T(8,128)(2,1)S(1)}, bf16[640,640]{1,0:T(8,128)(2,1)S(1)}, u32[]{:S(2)}, u32[]{:S(2)}) collective-permute-start(bf16[640,640]{1,0:T(8,128)(2,1)S(1)} %get-tuple-element.36), channel_id=1, source_target_pairs={{0,4},{2,6},{4,0},{6,2},{1,5},{3,7},{5,1},{7,3},{8,12},{10,14},{12... | collective-permute-start | bytes 2457608 | tf_op jit(solution)/shard_map/ppermute | solution.py:575
  195.5 24.3 %collective-permute-start.23 = (bf16[640,640]{1,0:T(8,128)(2,1)S(1)}, bf16[640,640]{1,0:T(8,128)(2,1)S(1)}, u32[]{:S(2)}, u32[]{:S(2)}) collective-permute-start(bf16[640,640]{1,0:T(8,128)(2,1)S(1)} %get-tuple-element.37), channel_id=1, source_target_pairs={{0,6},{2,0},{4,2},{6,4},{1,7},{3,1},{5,3},{7,5},{8,14},{10,8},{12,... | collective-permute-start | bytes 2457608 | tf_op jit(solution)/shard_map/ppermute | solution.py:575
  (48 other events, 482.5 us)

commit v3 on v2

--- a/solution.py
+++ b/solution.py
@@ -20,10 +20,11 @@
 SHARD = 320
 HALF = 1280
 CHUNK = 256
+WIDE = 640
 PIECE = 640
 LATE = 384
-TARGET_AT = 3584
-FACTS_AT = 6144
+TARGET_AT = 2560
+FACTS_AT = 3584
 
 kl_weight = 0.1
 step_size = 0.02
@@ -38,6 +39,8 @@
 BIG = pltpu.CompilerParams(vmem_limit_bytes=56 * 1024 * 1024)
 SMALL = pltpu.CompilerParams(vmem_limit_bytes=24 * 1024 * 1024)
 
+BRIEF = pl.CostEstimate(flops=1, bytes_accessed=1, transcendentals=0)
+
 DP = ("y", "xl", "c")
 FSDP = ("z", "xh")
 EVERY = DP + FSDP
@@ -71,25 +74,16 @@
     return (lax.broadcasted_iota(jnp.int32, (ROWS, ROWS), 0) == slots_ref[...]).astype(bf16)
 
 
-def pack_rows_kernel(slots_ref, q_ref, kv_ref, *rest):
+def pack_rows_kernel(kv_at, slots_ref, q_ref, kv_ref, *rest):
     out_ref = rest[-1]
     pick = one_hot_rows(slots_ref)
     out_ref[:, :Q_WIDTH] = dot(pick, q_ref[...]).astype(bf16)
-    out_ref[:, Q_WIDTH : Q_WIDTH + 1024] = dot(pick, kv_ref[...]).astype(bf16)
-
-
-def pack_policy_kernel(rewards_ref, ids_ref, lengths_ref, slots_ref, q_ref, kv_ref, target_ref, *rest):
+    out_ref[:, kv_at : kv_at + 1024] = dot(pick, kv_ref[...]).astype(bf16)
+
+
+def pack_policy_kernel(rewards_ref, ids_ref, lengths_ref, slots_ref, q_ref, kv_ref, *rest):
     out_ref = rest[-1]
-    pack_rows_kernel(slots_ref, q_ref, kv_ref, out_ref)
-    rows = dot(one_hot_rows(slots_ref), target_ref[...]).astype(bf16)
-    left, right = slice(TARGET_AT, TARGET_AT + HALF), slice(TARGET_AT + HALF, TARGET_AT + D_OUT)
-    for pair in range(ROWS // (2 * SPAN)):
-        top = pair * 2 * SPAN
-        one, two = slice(top, top + SPAN), slice(top + SPAN, top + 2 * SPAN)
-        out_ref[one, left] = rows[one, :HALF]
-        out_ref[one, right] = rows[two, :HALF]
-        out_ref[two, left] = rows[one, HALF:]
-        out_ref[two, right] = rows[two, HALF:]
+    pack_rows_kernel(Q_WIDTH, slots_ref, q_ref, kv_ref, out_ref)
     lane = lax.broadcasted_iota(jnp.int32, (8, 128), 1)
     facts = jnp.zeros((8, 128), f32)
     given = (rewards_ref[0], rewards_ref[1], ids_ref[0], ids_ref[1], lengths_ref[0, 0], lengths_ref[0, 1])
@@ -102,6 +96,20 @@
     out_ref[:, FACTS_AT:] = jnp.broadcast_to(coded[0:1], (ROWS, 128)).astype(bf16)
 
 
+def pack_reference_kernel(slots_ref, q_ref, kv_ref, target_ref, *rest):
+    out_ref = rest[-1]
+    pack_rows_kernel(TARGET_AT + D_OUT, slots_ref, q_ref, kv_ref, out_ref)
+    rows = dot(one_hot_rows(slots_ref), target_ref[...]).astype(bf16)
+    left, right = slice(TARGET_AT, TARGET_AT + HALF), slice(TARGET_AT + HALF, TARGET_AT + D_OUT)
+    for pair in range(ROWS // (2 * SPAN)):
+        top = pair * 2 * SPAN
+        one, two = slice(top, top + SPAN), slice(top + SPAN, top + 2 * SPAN)
+        out_ref[one, left] = rows[one, :HALF]
+        out_ref[one, right] = rows[two, :HALF]
+        out_ref[two, left] = rows[one, HALF:]
+        out_ref[two, right] = rows[two, HALF:]
+
+
 def pack(kernel, width, operands, after=(), small=()):
     return pl.pallas_call(
         kernel,
@@ -109,10 +117,22 @@
         out_specs=whole(),
         out_shape=jax.ShapeDtypeStruct((ROWS, width), bf16),
         compiler_params=BIG,
-        cost_estimate=pl.CostEstimate(
-            flops=2 * ROWS * ROWS * width, bytes_accessed=4 * ROWS * width, transcendentals=0
-        ),
+        cost_estimate=BRIEF,
     )(*small, *operands, *after)
+
+
+def gate_kernel(rows_ref, *rest):
+    pass
+
+
+def hold(rows, after):
+    return pl.pallas_call(
+        gate_kernel,
+        in_specs=[in_place()] * (1 + len(after)),
+        out_specs=in_place(),
+        out_shape=jax.ShapeDtypeStruct(rows.shape, rows.dtype),
+        input_output_aliases={0: 0},
+    )(rows, *after)
 
 
 def attention_kernel(lengths_ref, q_ref, k_ref, v_ref, *rest):
@@ -133,8 +153,8 @@
         out_ref[:, lanes] = dot(shares, values).astype(bf16)
 
 
-def attend(rows, lengths, after):
-    q_at, k_at, v_at = 0, Q_WIDTH, Q_WIDTH + 512
+def attend(rows, lengths, kv_at, after=()):
+    q_at, k_at, v_at = 0, kv_at, kv_at + 512
     width = Q_WIDTH // KV_HEADS
     return pl.pallas_call(
         attention_kernel,
@@ -149,9 +169,7 @@
         out_specs=pl.BlockSpec((ROWS, width), lambda g: (0, g)),
         out_shape=jax.ShapeDtypeStruct((ROWS, Q_WIDTH), bf16),
         compiler_params=BIG,
-        cost_estimate=pl.CostEstimate(
-            flops=4 * HEADS * ROWS * ROWS * HEAD_DIM, bytes_accessed=4 << 20, transcendentals=HEADS * ROWS * ROWS
-        ),
+        cost_estimate=BRIEF,
     )(lengths, rows, rows, rows, *after)
 
 
@@ -167,8 +185,8 @@
     row = lax.broadcasted_iota(jnp.int32, facts.shape, 0)
     lane = lax.broadcasted_iota(jnp.int32, facts.shape, 1)
     ids = pltpu.roll(facts, 128 - 2, 1)
-    own = place_ref[0] * 4 + place_ref[1] * 2 + place_ref[2]
-    other = place_ref[0] * 4 + place_ref[1] * 2 + 1 - place_ref[2]
+    chip = (place_ref[3] * 2 + place_ref[4]) * SPAN + place_ref[0] * 4 + place_ref[1] * 2
+    own, other = chip + place_ref[2], chip + 1 - place_ref[2]
 
     def fact(device, at):
         return jnp.sum(jnp.where((row == device) & (lane == at), facts, 0.0))
@@ -185,33 +203,40 @@
 
 
 def project_most_kernel(
-    place_ref, own_p, other_p, own_r, other_r,
-    p0, spp, o0p, smp, s2p, omp, e0, spe, o0e, sme, s2e, ome,
+    place_ref, own_p, other_p, own_r, other_r, w0, sm, sp, s2, o0, om, op,
     y_p, y_r, late_p, late_r, rows_p, rows_r, weight_p, weight_r, sems,
 ):
     z, xh = place_ref[3], place_ref[4]
+    here, there = xh, 1 - xh
 
     def place_of(dz, side):
         return pl.multiple_of((lax.rem(z + 4 + dz, 4) * 2 + side) * SHARD, 64)
 
-    here, there = xh, 1 - xh
+    blocks = (
+        (w0, 0, here), (sm, -1, here), (sp, 1, here), (s2, 2, here),
+        (o0, 0, there), (om, -1, there), (op, 1, there),
+    )
     copies = []
-    for own, other, rows, weight, blocks, sem in (
-        (own_p, other_p, rows_p, weight_p, (p0, smp, spp, o0p, s2p, omp), sems.at[0]),
-        (own_r, other_r, rows_r, weight_r, (e0, sme, spe, o0e, s2e, ome), sems.at[1]),
+    for k, (own, other, rows, weight) in enumerate(
+        ((own_p, other_p, rows_p, weight_p), (own_r, other_r, rows_r, weight_r))
     ):
         group = [
-            pltpu.make_async_copy(own, rows.at[pl.ds(0, ROWS), :], sem),
-            pltpu.make_async_copy(other, rows.at[pl.ds(ROWS, ROWS), :], sem),
+            pltpu.make_async_copy(own, rows.at[pl.ds(0, ROWS), :], sems.at[k]),
+            pltpu.make_async_copy(other, rows.at[pl.ds(ROWS, ROWS), :], sems.at[k]),
         ]
-        for block, dz, side in zip(blocks, (0, -1, 1, 0, 2, -1), (here, here, here, there, here, there)):
-            group.append(pltpu.make_async_copy(block, weight.at[pl.ds(place_of(dz, side), SHARD), :], sem))
+        for block, dz, side in blocks:
+            group.append(
+                pltpu.make_async_copy(
+                    block.at[pl.ds(k * SHARD, SHARD), :],
+                    weight.at[pl.ds(place_of(dz, side), SHARD), :],
+                    sems.at[k],
+                )
+            )
         for copy in group:
             copy.start()
         copies.append(group)
     for weight in (weight_p, weight_r):
-        for dz in (1, 2):
-            weight[pl.ds(place_of(dz, there), SHARD), :] = jnp.zeros((SHARD, HALF), bf16)
+        weight[pl.ds(place_of(2, there), SHARD), :] = jnp.zeros((SHARD, HALF), bf16)
 
     def run(rows, weight, out, late):
         def step(j, carry):
@@ -220,11 +245,9 @@
             return carry
 
         lax.fori_loop(0, HALF // CHUNK, step, 0)
-        for k, dz in enumerate((1, 2)):
-            at = pl.multiple_of(lax.rem(z + dz, 4) * PIECE, 128)
-            part = rows[:, pl.ds(at, PIECE)].astype(f32)
-            part = jnp.where(there == 0, part, pltpu.roll(part, PIECE - SHARD, 1))
-            late[:, k * LATE : (k + 1) * LATE] = part[:, :LATE].astype(bf16)
+        part = rows[:, pl.ds(pl.multiple_of(lax.rem(z + 2, 4) * PIECE, 128), PIECE)].astype(f32)
+        part = jnp.where(there == 0, part, pltpu.roll(part, PIECE - SHARD, 1))
+        late[...] = part[:, :LATE].astype(bf16)
 
     for copy in copies[0]:
         copy.wait()
@@ -240,7 +263,7 @@
         in_specs=[scalars()] + [in_place()] * (len(outs) + len(weights)),
         out_specs=[whole()] * 4,
         out_shape=[jax.ShapeDtypeStruct((2 * ROWS, HALF), f32)] * 2
-        + [jax.ShapeDtypeStruct((2 * ROWS, 2 * LATE), bf16)] * 2,
+        + [jax.ShapeDtypeStruct((2 * ROWS, LATE), bf16)] * 2,
         scratch_shapes=[
             VMEM((2 * ROWS, Q_WIDTH), bf16),
             VMEM((2 * ROWS, Q_WIDTH), bf16),
@@ -249,14 +272,19 @@
             pltpu.SemaphoreType.DMA((2,)),
         ],
         compiler_params=BIG,
-        cost_estimate=pl.CostEstimate(
-            flops=8 * ROWS * Q_WIDTH * HALF, bytes_accessed=24 << 20, transcendentals=0
-        ),
+        cost_estimate=BRIEF,
     )(place, *outs, *weights)
 
 
+def lanes_of(value):
+    total = value[:, :128]
+    for k in range(1, value.shape[1] // 128):
+        total = total + value[:, k * 128 : (k + 1) * 128]
+    return total
+
+
 def project_last_kernel(
-    place_ref, rows_p, rows_r, opp, o2p, ope, o2e, y_p, y_r, mine_ref, theirs_ref,
+    place_ref, rows_p, rows_r, o2p, o2e, y_p, y_r, mine_ref, theirs_ref,
     y_ref, stats_ref, late_p, late_r, sums,
 ):
     j = pl.program_id(0)
@@ -265,15 +293,10 @@
     def _():
         sums[...] = jnp.zeros_like(sums)
         for late in (late_p, late_r):
-            late[SHARD:LATE, :] = jnp.zeros((LATE - SHARD, CHUNK), bf16)
-            late[LATE + SHARD :, :] = jnp.zeros((LATE - SHARD, CHUNK), bf16)
-
-    for late, first, second in ((late_p, opp, o2p), (late_r, ope, o2e)):
-        late[:SHARD, :] = first[...]
-        late[LATE : LATE + SHARD, :] = second[...]
-
-    def lanes_of(value):
-        return value[:, :128] + value[:, 128:]
+            late[SHARD:, :] = jnp.zeros((LATE - SHARD, WIDE), bf16)
+
+    late_p[:SHARD, :] = o2p[...]
+    late_r[:SHARD, :] = o2e[...]
 
     target = jnp.concatenate([mine_ref[...], theirs_ref[...]], axis=0).astype(f32)
     y = y_p[...] + dot(rows_p[...], late_p[...])
@@ -284,7 +307,7 @@
     sums[2] += lanes_of(y * y)
     sums[3] += lanes_of(y * target)
 
-    @pl.when(j == HALF // CHUNK - 1)
+    @pl.when(j == HALF // WIDE - 1)
     def _():
         lane = lax.broadcasted_iota(jnp.int32, (2 * ROWS, 128), 1)
         stats = jnp.zeros((2 * ROWS, 128), f32)
@@ -294,8 +317,8 @@
 
 
 def project_last(place, parts, weights, target):
-    steps = HALF // CHUNK
-    chunk = lambda rows: pl.BlockSpec((rows, CHUNK), lambda j, place: (0, j))
+    steps = HALF // WIDE
+    chunk = lambda rows: pl.BlockSpec((rows, WIDE), lambda j, place: (0, j))
     fixed = lambda width: pl.BlockSpec((2 * ROWS, width), lambda j, place: (0, 0))
     y_p, y_r, rows_p, rows_r = parts
     return pl.pallas_call(
@@ -303,17 +326,17 @@
         grid_spec=pltpu.PrefetchScalarGridSpec(
             num_scalar_prefetch=1,
             grid=(steps,),
-            in_specs=[fixed(2 * LATE)] * 2
-            + [chunk(SHARD)] * 4
+            in_specs=[fixed(LATE)] * 2
+            + [chunk(SHARD)] * 2
             + [chunk(2 * ROWS)] * 2
             + [
-                pl.BlockSpec((ROWS, CHUNK), lambda j, place: (0, TARGET_AT // CHUNK + place[2] * steps + j)),
-                pl.BlockSpec((ROWS, CHUNK), lambda j, place: (0, TARGET_AT // CHUNK + (1 - place[2]) * steps + j)),
+                pl.BlockSpec((ROWS, WIDE), lambda j, place: (0, TARGET_AT // WIDE + place[2] * steps + j)),
+                pl.BlockSpec((ROWS, WIDE), lambda j, place: (0, TARGET_AT // WIDE + (1 - place[2]) * steps + j)),
             ],
             out_specs=[chunk(2 * ROWS), fixed(128)],
             scratch_shapes=[
-                VMEM((2 * LATE, CHUNK), bf16),
-                VMEM((2 * LATE, CHUNK), bf16),
+                VMEM((LATE, WIDE), bf16),
+                VMEM((LATE, WIDE), bf16),
                 VMEM((4, 2 * ROWS, 128), f32),
             ],
         ),
@@ -329,10 +352,10 @@
 
 
 def gradient_kernel(
-    place_ref, own_ref, other_ref, y_ref, stats_ref, more_ref, target_ref, facts_ref,
+    place_ref, own_ref, other_ref, y_ref, stats_ref, more_ref, mine_ref, theirs_ref, facts_ref,
     a0, a1, a2, a3, grad, rows,
 ):
-    c, z = place_ref[2], place_ref[3]
+    z = place_ref[3]
     rows[:ROWS, :] = own_ref[...]
     rows[ROWS:, :] = other_ref[...]
     row = lax.broadcasted_iota(jnp.int32, (ROWS, 1), 0)
@@ -359,8 +382,7 @@
         along = (policy_self - policy_cross) / D_OUT
         scale = weight / policy_norm
         slope = scale * (1.0 - along) / policy_norm
-        side_lanes = c if side == 0 else 1 - c
-        target = target_ref[:, pl.ds(pl.multiple_of(TARGET_AT + side_lanes * HALF, 128), HALF)].astype(f32)
+        target = (mine_ref if side == 0 else theirs_ref)[...].astype(f32)
         grad[here, :] = (y_ref[here, :] * slope - target * scale).astype(bf16)
 
     for d, out in enumerate((a0, a1, a2, a3)):
@@ -385,14 +407,23 @@
     cost = pl.CostEstimate(flops=2 * ROWS * Q_WIDTH * HALF, bytes_accessed=8 << 20, transcendentals=0)
     *first, grad = pl.pallas_call(
         gradient_kernel,
-        in_specs=[scalars()] + [whole()] * 7,
-        out_specs=[whole()] * 5,
+        grid_spec=pltpu.PrefetchScalarGridSpec(
+            num_scalar_prefetch=1,
+            grid=(1,),
+            in_specs=[whole()] * 5
+            + [
+                pl.BlockSpec((ROWS, HALF), lambda i, place: (0, TARGET_AT // HALF + place[2])),
+                pl.BlockSpec((ROWS, HALF), lambda i, place: (0, TARGET_AT // HALF + 1 - place[2])),
+                whole(),
+            ],
+            out_specs=[whole()] * 5,
+            scratch_shapes=[VMEM((2 * ROWS, Q_WIDTH), bf16)],
+        ),
         out_shape=[jax.ShapeDtypeStruct((PIECE, PIECE), bf16)] * 4
         + [jax.ShapeDtypeStruct((2 * ROWS, HALF), bf16)],
-        scratch_shapes=[VMEM((2 * ROWS, Q_WIDTH), bf16)],
         compiler_params=SMALL,
         cost_estimate=cost,
-    )(place, own, other, y, stats, more, target, facts)
+    )(place, own, other, y, stats, more, target, target, facts)
     second = pl.pallas_call(
         second_half_kernel,
         in_specs=[scalars()] + [whole()] * 3,
@@ -474,6 +505,15 @@
         copy.wait()
 
 
+def square_kernel(mine_ref, theirs_ref, out_ref):
+    def block(d):
+        mine, theirs = mine_ref[d].astype(f32), theirs_ref[d].astype(f32)
+        return jnp.sum(mine * mine, keepdims=True) + jnp.sum(theirs * theirs, keepdims=True)
+
+    total = (block(0) + block(2)) + (block(1) + block(3))
+    out_ref[...] = jnp.broadcast_to(total, (8, 128))
+
+
 def take_step(place, square_sum, mine, theirs, policy_weight, ema_weight):
     return pl.pallas_call(
         step_kernel,
@@ -516,36 +556,27 @@
     def half(weight):
         return lax.dynamic_slice_in_dim(weight, c * HALF, HALF, 1).astype(bf16)
 
-    p0, e0 = half(policy_weight), half(ema_weight)
-    smp, spp, o0p = send(p0, "z", ring(1)), send(p0, "z", ring(-1)), send(p0, X, ACROSS)
-    sme, spe, o0e = send(e0, "z", ring(1)), send(e0, "z", ring(-1)), send(e0, X, ACROSS)
-    s2p, s2e = send(smp, "z", ring(1)), send(spe, "z", ring(-1))
-    omp, ome = send(smp, X, ACROSS), send(sme, X, ACROSS)
-    opp, ope = send(o0p, "z", ring(-1)), send(o0e, "z", ring(-1))
-    o2p, o2e = send(s2p, X, ACROSS), send(ome, "z", ring(1))
+    w0 = jnp.concatenate([half(policy_weight), half(ema_weight)], axis=0)
+    sm, sp, o0 = send(w0, "z", ring(1)), send(w0, "z", ring(-1)), send(w0, X, ACROSS)
+    s2, op, om = send(sm, "z", ring(1)), send(o0, "z", ring(-1)), send(sm, X, ACROSS)
+    o2p, o2e = send(s2[:SHARD], X, ACROSS), send(om[SHARD:], "z", ring(1))
 
     exchange = functools.partial(lax.all_to_all, axis_name=DP, split_axis=0, concat_axis=0, tiled=True)
     rows_policy = exchange(
         pack(
             pack_policy_kernel,
             FACTS_AT + 128,
-            (send_slot, q_policy, kv_policy, target),
+            (send_slot, q_policy, kv_policy),
             small=(rewards, group_ids, lengths),
+            after=(w0,),
         )
     )
-    rows_reference = exchange(
-        pack(
-            pack_rows_kernel,
-            Q_WIDTH + 1024,
-            (send_slot, q_reference, kv_reference),
-            after=(rows_policy, smp, spp, o0p, sme, spe, o0e),
-        )
+    packed = pack(
+        pack_reference_kernel, Q_WIDTH + D_OUT + 1024, (send_slot, q_reference, kv_reference, target)
     )
-    out_policy = attend(rows_policy, lengths, ())
+    rows_reference = exchange(hold(packed, (rows_policy, sm, sp, o0)))
+    out_policy = attend(rows_policy, lengths, Q_WIDTH)
     other_policy = send(out_policy, "c", FLIP)
-    out_reference = attend(rows_reference, lengths, (s2p, s2e, omp, ome, opp))
-    other_reference = send(out_reference, "c", FLIP)
-
     facts = pl.pallas_call(
         facts_kernel,
         grid=(1,),
@@ -554,8 +585,8 @@
         out_shape=jax.ShapeDtypeStruct((SPAN, 128), f32),
         compiler_params=SMALL,
     )(rows_policy)
-    facts = jnp.concatenate([facts, send(facts, "xh", FLIP)], axis=0)
-    facts = jnp.concatenate([facts] + [send(facts, "z", ring(d)) for d in (1, 2, 3)], axis=0)
+    facts = jnp.broadcast_to(facts[None], (8, SPAN, 128)).reshape(8 * SPAN, 128)
+    facts = lax.all_to_all(facts, FSDP, split_axis=0, concat_axis=0, tiled=True)
     advantages = pl.pallas_call(
         advantage_kernel,
         in_specs=[scalars(), whole()],
@@ -564,16 +595,21 @@
         compiler_params=SMALL,
     )(place, facts)
 
+    out_reference = attend(rows_reference, lengths, TARGET_AT + D_OUT, (advantages,))
+    other_reference = send(out_reference, "c", FLIP)
+
     outs = (out_policy, other_policy, out_reference, other_reference)
-    parts = project_most(place, outs, (p0, spp, o0p, smp, s2p, omp, e0, spe, o0e, sme, s2e, ome))
-    y_policy, stats = project_last(place, parts, (opp, o2p, ope, o2e), rows_policy)
+    parts = project_most(place, outs, (w0, sm, sp, s2, o0, om, op))
+    y_policy, stats = project_last(place, parts, (o2p, o2e), rows_reference)
     more = send(stats, "c", FLIP)
     first, second = gradient(
-        place, out_policy, other_policy, y_policy, stats, more, rows_policy, advantages
+        place, out_policy, other_policy, y_policy, stats, more, rows_reference, advantages
     )
 
     first = [first[0]] + [send(first[d], "z", ring(d)) for d in (1, 2, 3)]
-    second = [second[0]] + [send(second[d], "y", ring(d)) for d in (1, 2, 3)]
+    near = send(second[1], "y", ring(1))
+    far = send(hold(second[2], (near,)), "y", ring(2))
+    second = [second[0], near, far, send(second[3], "y", ring(3))]
     first = sum_blocks(place, [piece.reshape(2, 4, 80, PIECE) for piece in first], 1, 0)
     second = sum_blocks(place, [piece.reshape(4, 2, 80, PIECE) for piece in second], 0, 3)
     first = [first[0]] + [send(first[d], "y", ring(d)) for d in (1, 2, 3)]
@@ -588,11 +624,13 @@
 
     mine = jnp.stack([block] + [send(block, "y", ring(-d)) for d in (1, 2, 3)])
     theirs = send(mine, "c", FLIP)
-    square = jnp.sum(jnp.square(mine.astype(f32)), axis=(1, 2)) + jnp.sum(
-        jnp.square(theirs.astype(f32)), axis=(1, 2)
-    )
-    square = (square[0] + square[2]) + (square[1] + square[3])
-    square = jnp.broadcast_to(square, (8, 128))
+    square = pl.pallas_call(
+        square_kernel,
+        in_specs=[whole()] * 2,
+        out_specs=whole(),
+        out_shape=jax.ShapeDtypeStruct((8, 128), f32),
+        compiler_params=SMALL,
+    )(mine, theirs)
     square = square + send(square, X, ACROSS)
     square = (square + send(square, "z", ring(2))) + (send(square, "z", ring(1)) + send(square, "z", ring(3)))
     return tuple(take_step(place, square, mine, theirs, policy_weight, ema_weight))

time: 282 us -> 264 us (0.936)
  waiting for transfers between devices: 129 us -> 117 us
    ppermute x21 -> x11, waiting for transfers between devices: 95.2 us -> 23 us  [the longest x1 13.8 us: local(): near = send(second[1], 'y', ring(1))]
    all_to_all x1 -> x2, waiting for transfers between devices: 0.01 us -> 23.9 us  [the longest x1 23.9 us: local(): rows_reference = exchange(hold(packed, (rows_policy, sm, sp, o0)))]
    all_to_all x1, waiting for transfers between devices: 0.01 us -> 18.5 us  [local(): exchange(pack(pack_policy_kernel, FACTS_AT + 128, (send_slot, q_policy, k...]
    ppermute x3, waiting for transfers between devices: 0.78 us -> 17.3 us  [local(): first = [first[0]] + [send(first[d], 'z', ring(d)) for d in (1, 2, 3)]]
    ppermute x21 -> x11, starting transfers between devices: 33.7 us -> 21 us  [the longest x2 3.62 us: local(): o2p, o2e = (send(s2[:SHARD], X, ACROSS), send(om[SHARD:], 'z', ring(1)))]
    all_to_all x1 -> x2, starting transfers between devices: 4.48 us -> 12 us  [the longest x1 7.48 us: local(): facts = lax.all_to_all(facts, FSDP, split_axis=0, concat_axis=0, tiled=True)]
    pallas_call x1, Pallas kernels: 10.5 us -> 7.31 us  [project_last(): pl.pallas_call(project_last_kernel, grid_spec=pltpu.PrefetchScalarGridSpe...]
    ppermute x3, waiting for transfers between devices: 2.49 us -> 5.66 us  [local(): second = [second[0]] + [send(second[d], 'z', ring(d)) for d in (1, 2, 3)]]
  transfers between devices with their start and end apart: 45 -> 36, of which waited for: 25 -> 24; matrix products, arithmetic and copies ran while one was open for 1% -> 1% of each run, Pallas kernels for 15% -> 14%
where the time goes in v3:
time: 264 us
  waiting for transfers between devices  117 us (44%)
  starting transfers between devices  66.3 us (25%)
  Pallas kernels  64.1 us (24%)
  local copies, waits for them, and re-layouts  13.7 us (5%)
    all_to_all x1, waiting for transfers between devices, local(): rows_reference = exchange(hold(packed, (rows_policy, sm, sp, o0)))  23.9 us
    all_to_all x1, waiting for transfers between devices, local(): exchange(pack(pack_policy_kernel, FACTS_AT + 128, (send_slot, q_policy, k...  18.5 us
    ppermute x3, waiting for transfers between devices, local(): first = [first[0]] + [send(first[d], 'z', ring(d)) for d in (1, 2, 3)]  17.3 us
    pallas_call x1, Pallas kernels, project_most(): pl.pallas_call(project_most_kernel, in_specs=[scalars()] + [in_place()] *...  14.6 us
    ppermute x1, waiting for transfers between devices, local(): near = send(second[1], 'y', ring(1))  13.8 us
    pallas_call x2, Pallas kernels, attend(): pl.pallas_call(attention_kernel, grid=(KV_HEADS,), in_specs=[scalars(), p...  13.7 us
    unnamed x36, local copies, waits for them, and re-layouts  8.74 us
    pallas_call x2, Pallas kernels, pack(): pl.pallas_call(kernel, in_specs=[scalars()] * len(small) + [whole()] * le...  7.89 us
  transfers between devices with their start and end apart: 36, of which 24 were waited for; matrix products, arithmetic and copies ran while one was open for 1% of the time, Pallas kernels for 14%

profile of v3, /device:TPU:0, one launch (start us, length us, event | category | flops | bytes accessed | tf_op | source)
XLA Modules:
  0.0 263.8 jit_solution(3522763673567380465)
XLA Ops:
  3.7 3.4 %shard_map.130 = bf16[256,3712]{1,0:T(8,128)(2,1)} custom-call(f32[2]{0:T(128)} %rewards_ref.1, s32[2]{0:T(128)} %ids_ref.1, s32[1,2]{1,0:T(1,128)} %lengths_ref.5, s32[1,256]{1,0:T(1,128)} %slots_ref.3, bf16[256,2560]{1,0:T(8,128)(2,1)} %q_ref.2, bf16[256,1024]{1,0:T(8,128)(2,1)} %kv_ref.2, bf16[640,1280]{1,0:T(8,128)(2,1)} %pad_maximum_fusion.rest_0_.w0), custom_call_target="tpu_custom_call" | custom-call | flops 1 | bytes 1 | tf_op jit(solution)/shard_map/pallas_call | solution.py:114
  7.0 5.6 %all-to-all-start = ((bf16[16,16,3712]{2,1,0:T(8,128)(2,1)}), bf16[16,16,3712]{2,1,0:T(8,128)(2,1)S(1)}, u32[]{:S(2)}, u32[]{:S(2)}) async-start(bf16[16,16,3712]{2,1,0:T(8,128)(2,1)} %bitcast.41), calls=%async_computation | async-start | bytes 3801088 | tf_op jit(solution)/shard_map/all_to_all | solution.py:565
  14.6 3.1 %collective-permute-start.3 = (bf16[640,1280]{1,0:T(8,128)(2,1)}, bf16[640,1280]{1,0:T(8,128)(2,1)}, u32[]{:S(2)}, u32[]{:S(2)}) collective-permute-start(bf16[640,1280]{1,0:T(8,128)(2,1)} %pad_maximum_fusion.rest_0_.w0), channel_id=1, source_target_pairs={{16,1},{1,16},{0,17},{17,0},{18,3},{3,18},{2,19},{19,2},{20,5},{5,... | collective-permute-start | bytes 4915208 | tf_op jit(solution)/shard_map/ppermute | solution.py:560
  20.0 18.5 %all-to-all-done = bf16[16,16,3712]{2,1,0:T(8,128)(2,1)S(1)} async-done(((bf16[16,16,3712]{2,1,0:T(8,128)(2,1)}), bf16[16,16,3712]{2,1,0:T(8,128)(2,1)S(1)}, u32[]{:S(2)}, u32[]{:S(2)}) %all-to-all-start) | async-done | bytes 1900576 | tf_op jit(solution)/shard_map/all_to_all | solution.py:565
  39.3 7.5 %all-to-all-start.2 = ((f32[8,16,128]{2,1,0:T(8,128)}), f32[8,16,128]{2,1,0:T(8,128)S(1)}, u32[]{:S(2)}, u32[]{:S(2)}) async-start(f32[8,16,128]{2,1,0:T(8,128)} %broadcast_in_dim.2), calls=%async_computation.2 | async-start | bytes 131072 | tf_op jit(solution)/shard_map/all_to_all | solution.py:589
  46.7 4.5 %shard_map.132.rows_ref = bf16[256,6144]{1,0:T(8,128)(2,1)} custom-call(s32[1,256]{1,0:T(1,128)} %slots_ref.3, bf16[256,2560]{1,0:T(8,128)(2,1)} %q_ref.3, bf16[256,1024]{1,0:T(8,128)(2,1)} %kv_ref.3, bf16[256,2560]{1,0:T(8,128)(2,1)} %target_ref.1), custom_call_target="tpu_custom_call" | custom-call | flops 1 | bytes 1 | tf_op jit(solution)/shard_map/pallas_call | solution.py:114
  56.1 4.5 %all-to-all-start.1 = ((bf16[16,16,6144]{2,1,0:T(8,128)(2,1)}), bf16[16,16,6144]{2,1,0:T(8,128)(2,1)S(1)}, u32[]{:S(2)}, u32[]{:S(2)}) async-start(bf16[16,16,6144]{2,1,0:T(8,128)(2,1)} %bitcast.40), calls=%async_computation.1 | async-start | bytes 6291456 | tf_op jit(solution)/shard_map/all_to_all | solution.py:577
  67.1 6.9 %shard_map.131.own_p.own_ref = bf16[256,2560]{1,0:T(8,128)(2,1)} custom-call(s32[1,2]{1,0:T(1,128)} %lengths_ref.5, bf16[256,3712]{1,0:T(8,128)(2,1)} %bitcast.31, bf16[256,3712]{1,0:T(8,128)(2,1)} %bitcast.32, bf16[256,3712]{1,0:T(8,128)(2,1)} %bitcast.33), custom_call_target="tpu_custom_call" | custom-call | flops 1 | bytes 1 | tf_op jit(solution)/shard_map/pallas_call | solution.py:159
  75.8 23.9 %all-to-all-done.1 = bf16[16,16,6144]{2,1,0:T(8,128)(2,1)S(1)} async-done(((bf16[16,16,6144]{2,1,0:T(8,128)(2,1)}), bf16[16,16,6144]{2,1,0:T(8,128)(2,1)S(1)}, u32[]{:S(2)}, u32[]{:S(2)}) %all-to-all-start.1) | async-done | bytes 3145760 | tf_op jit(solution)/shard_map/all_to_all | solution.py:577
  101.4 6.8 %shard_map.136.own_r = bf16[256,2560]{1,0:T(8,128)(2,1)} custom-call(s32[1,2]{1,0:T(1,128)} %lengths_ref.5, bf16[256,6144]{1,0:T(8,128)(2,1)} %bitcast.22, bf16[256,6144]{1,0:T(8,128)(2,1)} %bitcast.23, bf16[256,6144]{1,0:T(8,128)(2,1)} %bitcast.24, f32[8,128]{1,0:T(8,128)} %copy-done.13), custom_call_target="tpu_custom_call" | custom-call | flops 1 | bytes 1 | tf_op jit(solution)/shard_map/pallas_call | solution.py:159
  115.3 14.6 %shard_map.137 = (f32[512,1280]{1,0:T(8,128)}, f32[512,1280]{1,0:T(8,128)}, bf16[512,384]{1,0:T(8,128)(2,1)}, bf16[512,384]{1,0:T(8,128)(2,1)}) custom-call(s32[5]{0:T(128)} %copy-done.11, bf16[256,2560]{1,0:T(8,128)(2,1)} %shard_map.131.own_p.own_ref, bf16[256,2560]{1,0:T(8,128)(2,1)} %collective-permute-done.other_p.other_ref, ...), custom_call_target="tpu_custom_call" | custom-call | flops 1 | bytes 1 | tf_op jit(solution)/shard_map/pallas_call | solution.py:261
  135.2 7.3 %shard_map.138 = (f32[512,1280]{1,0:T(8,128)}, f32[512,128]{1,0:T(8,128)}) custom-call(s32[5]{0:T(128)} %copy-done.11, bf16[512,384]{1,0:T(8,128)(2,1)} %get-tuple-element.28.rows_p, bf16[512,384]{1,0:T(8,128)(2,1)} %get-tuple-element.29.rows_r, bf16[320,1280]{1,0:T(8,128)(2,1)} %copy-done.16, bf16[320,1280]{1,0:T(8,128)(2,1)} %copy-done.17, ...), custom_call_target="tpu_custom_call" | custom-call | flops 1677721600 | bytes 10485760 | tf_op jit(solution)/shard_map/pallas_call | solution.py:324
  147.1 5.8 %shard_map.139 = (bf16[640,640]{1,0:T(8,128)(2,1)S(1)}, bf16[640,640]{1,0:T(8,128)(2,1)}, bf16[640,640]{1,0:T(8,128)(2,1)}, bf16[640,640]{1,0:T(8,128)(2,1)}, bf16[512,1280]{1,0:T(8,128)(2,1)S(1)}) custom-call(s32[5]{0:T(128)S(1)} %copy-done.12, bf16[256,2560]{1,0:T(8,128)(2,1)S(1)} %copy-done.3, bf16[256,2560]{1,0:T(8,128)(2,1)} %collective-permute-done.other_p.other_ref, ...), custom_call_target="tpu_custom_call" | custom-call | flops 1677721600 | bytes 8388608 | tf_op jit(solution)/shard_map/pallas_call | solution.py:408
  152.9 5.0 %shard_map.141 = (bf16[8,80,640]{2,1,0:T(8,128)(2,1)S(1)}, bf16[8,80,640]{2,1,0:T(8,128)(2,1)S(1)}, bf16[8,80,640]{2,1,0:T(8,128)(2,1)S(1)}, bf16[8,80,640]{2,1,0:T(8,128)(2,1)}) custom-call(s32[5]{0:T(128)S(1)} %copy-done.12, bf16[256,2560]{1,0:T(8,128)(2,1)S(1)} %copy-done.3, bf16[256,2560]{1,0:T(8,128)(2,1)} %collective-permute-done.other_p.other_ref, ...), custom_call_target="tpu_custom_call" | custom-call | flops 1677721600 | bytes 8388608 | tf_op jit(solution)/shard_map/pallas_call | solution.py:427
  163.3 3.2 %collective-permute-start.19 = (bf16[8,80,640]{2,1,0:T(8,128)(2,1)}, bf16[8,80,640]{2,1,0:T(8,128)(2,1)S(1)}, u32[]{:S(2)}, u32[]{:S(2)}) collective-permute-start(bf16[8,80,640]{2,1,0:T(8,128)(2,1)} %get-tuple-element.46), channel_id=1, source_target_pairs={{0,96},{32,0},{64,32},{96,64},{1,97},{33,1},{65,33},{97,65},{2,98}... | collective-permute-start | bytes 2457608 | tf_op jit(solution)/shard_map/ppermute | solution.py:612
  166.6 13.8 %collective-permute-done.17.rest_0_ = bf16[8,80,640]{2,1,0:T(8,128)(2,1)S(1)} collective-permute-done((bf16[8,80,640]{2,1,0:T(8,128)(2,1)S(1)}, bf16[8,80,640]{2,1,0:T(8,128)(2,1)S(1)}, u32[]{:S(2)}, u32[]{:S(2)}) %collective-permute-start.17) | collective-permute-done | bytes 819232 | tf_op jit(solution)/shard_map/ppermute | solution.py:610
  181.6 16.6 %collective-permute-done.11 = bf16[640,640]{1,0:T(8,128)(2,1)} collective-permute-done((bf16[640,640]{1,0:T(8,128)(2,1)}, bf16[640,640]{1,0:T(8,128)(2,1)}, u32[]{:S(2)}, u32[]{:S(2)}) %collective-permute-start.11) | collective-permute-done | bytes 819232 | tf_op jit(solution)/shard_map/ppermute | solution.py:609
  202.3 3.2 %collective-permute-start.15 = (bf16[2,80,640]{2,1,0:T(8,128)(2,1)S(1)}, bf16[2,80,640]{2,1,0:T(8,128)(2,1)S(1)}, u32[]{:S(2)}, u32[]{:S(2)}) collective-permute-start(bf16[2,80,640]{2,1,0:T(8,128)(2,1)S(1)} %get-tuple-element.40), channel_id=1, source_target_pairs={{0,64},{32,96},{64,0},{96,32},{1,65},{33,97},{65,1},{97,33},{2,66}... | collective-permute-start | bytes 614408 | tf_op jit(solution)/shard_map/ppermute | solution.py:615
  214.3 5.2 %collective-permute-done.21.refs_6_ = bf16[2,80,640]{2,1,0:T(8,128)(2,1)S(1)} collective-permute-done((bf16[2,80,640]{2,1,0:T(8,128)(2,1)S(1)}, bf16[2,80,640]{2,1,0:T(8,128)(2,1)S(1)}, u32[]{:S(2)}, u32[]{:S(2)}) %collective-permute-start.21) | collective-permute-done | bytes 204832 | tf_op jit(solution)/shard_map/ppermute | solution.py:616
  222.6 4.6 %collective-permute-done.23 = bf16[80,1280]{1,0:T(8,128)(2,1)S(1)} collective-permute-done((bf16[80,1280]{1,0:T(8,128)(2,1)S(1)}, bf16[80,1280]{1,0:T(8,128)(2,1)S(1)}, u32[]{:S(2)}, u32[]{:S(2)}) %collective-permute-start.23) | collective-permute-done | bytes 204832 | tf_op jit(solution)/shard_map/ppermute | solution.py:622
  227.5 5.6 %collective-permute-done.24 = bf16[80,1280]{1,0:T(8,128)(2,1)S(1)} collective-permute-done((bf16[80,1280]{1,0:T(8,128)(2,1)S(1)}, bf16[80,1280]{1,0:T(8,128)(2,1)S(1)}, u32[]{:S(2)}, u32[]{:S(2)}) %collective-permute-start.24) | collective-permute-done | bytes 204832 | tf_op jit(solution)/shard_map/ppermute | solution.py:623
  233.9 3.2 %collective-permute-start.26 = (bf16[80,1280]{1,0:T(8,128)(2,1)S(1)}, bf16[80,1280]{1,0:T(8,128)(2,1)S(1)}, u32[]{:S(2)}, u32[]{:S(2)}) collective-permute-start(bf16[80,1280]{1,0:T(8,128)(2,1)S(1)} %add_convert_fusion), channel_id=1, source_target_pairs={{0,64},{32,96},{64,0},{96,32},{1,65},{33,97},{65,1},{97,33},{2,66}... | collective-permute-start | bytes 614408 | tf_op jit(solution)/shard_map/ppermute | solution.py:625
  248.9 3.1 %collective-permute-done.29 = f32[8,128]{1,0:T(8,128)S(1)} collective-permute-done((f32[8,128]{1,0:T(8,128)S(1)}, f32[8,128]{1,0:T(8,128)S(1)}, u32[]{:S(2)}, u32[]{:S(2)}) %collective-permute-start.29) | collective-permute-done | bytes 4128 | tf_op jit(solution)/shard_map/ppermute | solution.py:634
  259.4 4.2 %shard_map.146 = (f32[320,2560]{1,0:T(8,128)}, bf16[320,2560]{1,0:T(8,128)(2,1)}, f32[320,2560]{1,0:T(8,128)}) custom-call(s32[5]{0:T(128)S(1)} %copy-done.12, f32[8,128]{1,0:T(8,128)S(1)} %add_add_fusion.square_ref, bf16[4,80,1280]{2,1,0:T(8,128)(2,1)S(1)} %pad_maximum_fusion.1.mine_ref, bf16[4,80,1280]{2,1,0:T(8,128)(2,1)S(1)} %collective-permute-done.28.theirs_ref, ...), custom_call_target="tpu_custom_call" | custom-call | tf_op jit(solution)/shard_map/pallas_call | solution.py:518
  (112 shorter events, 82.9 us)
Async XLA Ops:
  7.0 31.4 %all-to-all-start = ((bf16[16,16,3712]{2,1,0:T(8,128)(2,1)}), bf16[16,16,3712]{2,1,0:T(8,128)(2,1)S(1)}, u32[]{:S(2)}, u32[]{:S(2)}) async-start(bf16[16,16,3712]{2,1,0:T(8,128)(2,1)} %bitcast.41), calls=%async_computation | async-start | bytes 3801088 | tf_op jit(solution)/shard_map/all_to_all | solution.py:565
  12.6 41.0 %collective-permute-start.1 = (bf16[640,1280]{1,0:T(8,128)(2,1)}, bf16[640,1280]{1,0:T(8,128)(2,1)}, u32[]{:S(2)}, u32[]{:S(2)}) collective-permute-start(bf16[640,1280]{1,0:T(8,128)(2,1)} %pad_maximum_fusion.rest_0_.w0), channel_id=1, source_target_pairs={{0,2},{2,4},{4,6},{6,0},{1,3},{3,5},{5,7},{7,1},{8,10},{10,12},{12... | collective-permute-start | bytes 4915208 | tf_op jit(solution)/shard_map/ppermute | solution.py:560
  14.6 40.0 %collective-permute-start.3 = (bf16[640,1280]{1,0:T(8,128)(2,1)}, bf16[640,1280]{1,0:T(8,128)(2,1)}, u32[]{:S(2)}, u32[]{:S(2)}) collective-permute-start(bf16[640,1280]{1,0:T(8,128)(2,1)} %pad_maximum_fusion.rest_0_.w0), channel_id=1, source_target_pairs={{16,1},{1,16},{0,17},{17,0},{18,3},{3,18},{2,19},{19,2},{20,5},{5,... | collective-permute-start | bytes 4915208 | tf_op jit(solution)/shard_map/ppermute | solution.py:560
  17.7 38.3 %collective-permute-start.2 = (bf16[640,1280]{1,0:T(8,128)(2,1)}, bf16[640,1280]{1,0:T(8,128)(2,1)}, u32[]{:S(2)}, u32[]{:S(2)}) collective-permute-start(bf16[640,1280]{1,0:T(8,128)(2,1)} %pad_maximum_fusion.rest_0_.w0), channel_id=1, source_target_pairs={{0,6},{2,0},{4,2},{6,4},{1,7},{3,1},{5,3},{7,5},{8,14},{10,8},{12,... | collective-permute-start | bytes 4915208 | tf_op jit(solution)/shard_map/ppermute | solution.py:560
  39.3 16.8 %all-to-all-start.2 = ((f32[8,16,128]{2,1,0:T(8,128)}), f32[8,16,128]{2,1,0:T(8,128)S(1)}, u32[]{:S(2)}, u32[]{:S(2)}) async-start(f32[8,16,128]{2,1,0:T(8,128)} %broadcast_in_dim.2), calls=%async_computation.2 | async-start | bytes 131072 | tf_op jit(solution)/shard_map/all_to_all | solution.py:589
  56.1 43.6 %all-to-all-start.1 = ((bf16[16,16,6144]{2,1,0:T(8,128)(2,1)}), bf16[16,16,6144]{2,1,0:T(8,128)(2,1)S(1)}, u32[]{:S(2)}, u32[]{:S(2)}) async-start(bf16[16,16,6144]{2,1,0:T(8,128)(2,1)} %bitcast.40), calls=%async_computation.1 | async-start | bytes 6291456 | tf_op jit(solution)/shard_map/all_to_all | solution.py:577
  60.6 47.6 %collective-permute-start.5 = (bf16[640,1280]{1,0:T(8,128)(2,1)}, bf16[640,1280]{1,0:T(8,128)(2,1)}, u32[]{:S(2)}, u32[]{:S(2)}) collective-permute-start(bf16[640,1280]{1,0:T(8,128)(2,1)} %collective-permute-done.1.rest_1_.sm), channel_id=1, source_target_pairs={{0,2},{2,4},{4,6},{6,0},{1,3},{3,5},{5,7},{7,1},{8,10},{10,12},{12... | collective-permute-start | bytes 4915208 | tf_op jit(solution)/shard_map/ppermute | solution.py:561
  63.4 48.2 %collective-permute-start.6 = (bf16[640,1280]{1,0:T(8,128)(2,1)}, bf16[640,1280]{1,0:T(8,128)(2,1)}, u32[]{:S(2)}, u32[]{:S(2)}) collective-permute-start(bf16[640,1280]{1,0:T(8,128)(2,1)} %collective-permute-done.1.rest_1_.sm), channel_id=1, source_target_pairs={{16,1},{1,16},{0,17},{17,0},{18,3},{3,18},{2,19},{19,2},{20,5},{5,... | collective-permute-start | bytes 4915208 | tf_op jit(solution)/shard_map/ppermute | solution.py:561
  65.2 49.0 %collective-permute-start.7 = (bf16[640,1280]{1,0:T(8,128)(2,1)}, bf16[640,1280]{1,0:T(8,128)(2,1)}, u32[]{:S(2)}, u32[]{:S(2)}) collective-permute-start(bf16[640,1280]{1,0:T(8,128)(2,1)} %collective-permute-done.3.rest_3_.o0), channel_id=1, source_target_pairs={{0,6},{2,0},{4,2},{6,4},{1,7},{3,1},{5,3},{7,5},{8,14},{10,8},{12,... | collective-permute-start | bytes 4915208 | tf_op jit(solution)/shard_map/ppermute | solution.py:561
  74.0 40.3 %collective-permute-start = (bf16[256,2560]{1,0:T(8,128)(2,1)}, bf16[256,2560]{1,0:T(8,128)(2,1)}, u32[]{:S(2)}, u32[]{:S(2)}) collective-permute-start(bf16[256,2560]{1,0:T(8,128)(2,1)} %shard_map.131.own_p.own_ref), channel_id=1, source_target_pairs={{0,8},{8,0},{1,9},{9,1},{2,10},{10,2},{3,11},{11,3},{4,12},{12,4},... | collective-permute-start | bytes 3932168 | tf_op jit(solution)/shard_map/ppermute | solution.py:579
  109.4 21.9 %collective-permute-start.8 = (bf16[320,1280]{1,0:T(8,128)(2,1)S(1)}, bf16[320,1280]{1,0:T(8,128)(2,1)S(1)}, u32[]{:S(2)}, u32[]{:S(2)}) collective-permute-start(bf16[320,1280]{1,0:T(8,128)(2,1)S(1)} %slice.8), channel_id=1, source_target_pairs={{16,1},{1,16},{0,17},{17,0},{18,3},{3,18},{2,19},{19,2},{20,5},{5,... | collective-permute-start | bytes 2457608 | tf_op jit(solution)/shard_map/ppermute | solution.py:562
  112.8 21.6 %collective-permute-start.9 = (bf16[320,1280]{1,0:T(8,128)(2,1)S(1)}, bf16[320,1280]{1,0:T(8,128)(2,1)S(1)}, u32[]{:S(2)}, u32[]{:S(2)}) collective-permute-start(bf16[320,1280]{1,0:T(8,128)(2,1)S(1)} %slice.9), channel_id=1, source_target_pairs={{0,2},{2,4},{4,6},{6,0},{1,3},{3,5},{5,7},{7,1},{8,10},{10,12},{12... | collective-permute-start | bytes 2457608 | tf_op jit(solution)/shard_map/ppermute | solution.py:562
  158.8 21.5 %collective-permute-start.17 = (bf16[8,80,640]{2,1,0:T(8,128)(2,1)S(1)}, bf16[8,80,640]{2,1,0:T(8,128)(2,1)S(1)}, u32[]{:S(2)}, u32[]{:S(2)}) collective-permute-start(bf16[8,80,640]{2,1,0:T(8,128)(2,1)S(1)} %get-tuple-element.44), channel_id=1, source_target_pairs={{0,32},{32,64},{64,96},{96,0},{1,33},{33,65},{65,97},{97,1},{2,34}... | collective-permute-start | bytes 2457608 | tf_op jit(solution)/shard_map/ppermute | solution.py:610
  158.8 39.4 %collective-permute-start.11 = (bf16[640,640]{1,0:T(8,128)(2,1)}, bf16[640,640]{1,0:T(8,128)(2,1)}, u32[]{:S(2)}, u32[]{:S(2)}) collective-permute-start(bf16[640,640]{1,0:T(8,128)(2,1)} %get-tuple-element.35), channel_id=1, source_target_pairs={{0,2},{2,4},{4,6},{6,0},{1,3},{3,5},{5,7},{7,1},{8,10},{10,12},{12... | collective-permute-start | bytes 2457608 | tf_op jit(solution)/shard_map/ppermute | solution.py:609
  159.2 39.0 %collective-permute-start.12 = (bf16[640,640]{1,0:T(8,128)(2,1)}, bf16[640,640]{1,0:T(8,128)(2,1)}, u32[]{:S(2)}, u32[]{:S(2)}) collective-permute-start(bf16[640,640]{1,0:T(8,128)(2,1)} %get-tuple-element.36), channel_id=1, source_target_pairs={{0,4},{2,6},{4,0},{6,2},{1,5},{3,7},{5,1},{7,3},{8,12},{10,14},{12... | collective-permute-start | bytes 2457608 | tf_op jit(solution)/shard_map/ppermute | solution.py:609
  161.4 37.4 %collective-permute-start.13 = (bf16[640,640]{1,0:T(8,128)(2,1)}, bf16[640,640]{1,0:T(8,128)(2,1)}, u32[]{:S(2)}, u32[]{:S(2)}) collective-permute-start(bf16[640,640]{1,0:T(8,128)(2,1)} %get-tuple-element.37), channel_id=1, source_target_pairs={{0,6},{2,0},{4,2},{6,4},{1,7},{3,1},{5,3},{7,5},{8,14},{10,8},{12,... | collective-permute-start | bytes 2457608 | tf_op jit(solution)/shard_map/ppermute | solution.py:609
  163.3 42.2 %collective-permute-start.19 = (bf16[8,80,640]{2,1,0:T(8,128)(2,1)}, bf16[8,80,640]{2,1,0:T(8,128)(2,1)S(1)}, u32[]{:S(2)}, u32[]{:S(2)}) collective-permute-start(bf16[8,80,640]{2,1,0:T(8,128)(2,1)} %get-tuple-element.46), channel_id=1, source_target_pairs={{0,96},{32,0},{64,32},{96,64},{1,97},{33,1},{65,33},{97,65},{2,98}... | collective-permute-start | bytes 2457608 | tf_op jit(solution)/shard_map/ppermute | solution.py:612
  181.2 24.3 %collective-permute-start.18 = (bf16[8,80,640]{2,1,0:T(8,128)(2,1)}, bf16[8,80,640]{2,1,0:T(8,128)(2,1)S(1)}, u32[]{:S(2)}, u32[]{:S(2)}) collective-permute-start(bf16[8,80,640]{2,1,0:T(8,128)(2,1)} %shard_map.142), channel_id=1, source_target_pairs={{0,64},{32,96},{64,0},{96,32},{1,65},{33,97},{65,1},{97,33},{2,66}... | collective-permute-start | bytes 2457608 | tf_op jit(solution)/shard_map/ppermute | solution.py:611
  201.0 9.7 %collective-permute-start.14 = (bf16[2,80,640]{2,1,0:T(8,128)(2,1)S(1)}, bf16[2,80,640]{2,1,0:T(8,128)(2,1)S(1)}, u32[]{:S(2)}, u32[]{:S(2)}) collective-permute-start(bf16[2,80,640]{2,1,0:T(8,128)(2,1)S(1)} %get-tuple-element.39), channel_id=1, source_target_pairs={{0,32},{32,64},{64,96},{96,0},{1,33},{33,65},{65,97},{97,1},{2,34}... | collective-permute-start | bytes 614408 | tf_op jit(solution)/shard_map/ppermute | solution.py:615
  202.3 11.5 %collective-permute-start.15 = (bf16[2,80,640]{2,1,0:T(8,128)(2,1)S(1)}, bf16[2,80,640]{2,1,0:T(8,128)(2,1)S(1)}, u32[]{:S(2)}, u32[]{:S(2)}) collective-permute-start(bf16[2,80,640]{2,1,0:T(8,128)(2,1)S(1)} %get-tuple-element.40), channel_id=1, source_target_pairs={{0,64},{32,96},{64,0},{96,32},{1,65},{33,97},{65,1},{97,33},{2,66}... | collective-permute-start | bytes 614408 | tf_op jit(solution)/shard_map/ppermute | solution.py:615
  205.5 8.3 %collective-permute-start.16 = (bf16[2,80,640]{2,1,0:T(8,128)(2,1)S(1)}, bf16[2,80,640]{2,1,0:T(8,128)(2,1)S(1)}, u32[]{:S(2)}, u32[]{:S(2)}) collective-permute-start(bf16[2,80,640]{2,1,0:T(8,128)(2,1)S(1)} %get-tuple-element.41), channel_id=1, source_target_pairs={{0,96},{32,0},{64,32},{96,64},{1,97},{33,1},{65,33},{97,65},{2,98}... | collective-permute-start | bytes 614408 | tf_op jit(solution)/shard_map/ppermute | solution.py:615
  206.5 7.8 %collective-permute-start.20 = (bf16[2,80,640]{2,1,0:T(8,128)(2,1)S(1)}, bf16[2,80,640]{2,1,0:T(8,128)(2,1)S(1)}, u32[]{:S(2)}, u32[]{:S(2)}) collective-permute-start(bf16[2,80,640]{2,1,0:T(8,128)(2,1)S(1)} %get-tuple-element.48), channel_id=1, source_target_pairs={{0,2},{2,4},{4,6},{6,0},{1,3},{3,5},{5,7},{7,1},{8,10},{10,12},{12... | collective-permute-start | bytes 614408 | tf_op jit(solution)/shard_map/ppermute | solution.py:616
  207.8 11.6 %collective-permute-start.21 = (bf16[2,80,640]{2,1,0:T(8,128)(2,1)S(1)}, bf16[2,80,640]{2,1,0:T(8,128)(2,1)S(1)}, u32[]{:S(2)}, u32[]{:S(2)}) collective-permute-start(bf16[2,80,640]{2,1,0:T(8,128)(2,1)S(1)} %get-tuple-element.49), channel_id=1, source_target_pairs={{0,4},{2,6},{4,0},{6,2},{1,5},{3,7},{5,1},{7,3},{8,12},{10,14},{12... | collective-permute-start | bytes 614408 | tf_op jit(solution)/shard_map/ppermute | solution.py:616
  210.7 8.8 %collective-permute-start.22 = (bf16[2,80,640]{2,1,0:T(8,128)(2,1)S(1)}, bf16[2,80,640]{2,1,0:T(8,128)(2,1)S(1)}, u32[]{:S(2)}, u32[]{:S(2)}) collective-permute-start(bf16[2,80,640]{2,1,0:T(8,128)(2,1)S(1)} %get-tuple-element.50), channel_id=1, source_target_pairs={{0,6},{2,0},{4,2},{6,4},{1,7},{3,1},{5,3},{7,5},{8,14},{10,8},{12,... | collective-permute-start | bytes 614408 | tf_op jit(solution)/shard_map/ppermute | solution.py:616
  (30 other events, 192.1 us)

commit v4 on v3

--- a/solution.py
+++ b/solution.py
@@ -24,7 +24,7 @@
 PIECE = 640
 LATE = 384
 TARGET_AT = 2560
-FACTS_AT = 3584
+FACTS_AT = 6144
 
 kl_weight = 0.1
 step_size = 0.02
@@ -37,6 +37,7 @@
 VMEM = pltpu.VMEM
 SMEM = pltpu.SMEM
 BIG = pltpu.CompilerParams(vmem_limit_bytes=56 * 1024 * 1024)
+HUGE = pltpu.CompilerParams(vmem_limit_bytes=63 * 1024 * 1024)
 SMALL = pltpu.CompilerParams(vmem_limit_bytes=24 * 1024 * 1024)
 
 BRIEF = pl.CostEstimate(flops=1, bytes_accessed=1, transcendentals=0)
@@ -81,22 +82,7 @@
     out_ref[:, kv_at : kv_at + 1024] = dot(pick, kv_ref[...]).astype(bf16)
 
 
-def pack_policy_kernel(rewards_ref, ids_ref, lengths_ref, slots_ref, q_ref, kv_ref, *rest):
-    out_ref = rest[-1]
-    pack_rows_kernel(Q_WIDTH, slots_ref, q_ref, kv_ref, out_ref)
-    lane = lax.broadcasted_iota(jnp.int32, (8, 128), 1)
-    facts = jnp.zeros((8, 128), f32)
-    given = (rewards_ref[0], rewards_ref[1], ids_ref[0], ids_ref[1], lengths_ref[0, 0], lengths_ref[0, 1])
-    for k, fact in enumerate(given):
-        facts = jnp.where(lane % 8 == k, fact.astype(f32), facts)
-    high = facts.astype(bf16).astype(f32)
-    middle = (facts - high).astype(bf16).astype(f32)
-    low = facts - high - middle
-    coded = jnp.where(lane < 8, high, jnp.where(lane < 16, middle, low))
-    out_ref[:, FACTS_AT:] = jnp.broadcast_to(coded[0:1], (ROWS, 128)).astype(bf16)
-
-
-def pack_reference_kernel(slots_ref, q_ref, kv_ref, target_ref, *rest):
+def pack_policy_kernel(rewards_ref, ids_ref, lengths_ref, slots_ref, q_ref, kv_ref, target_ref, *rest):
     out_ref = rest[-1]
     pack_rows_kernel(TARGET_AT + D_OUT, slots_ref, q_ref, kv_ref, out_ref)
     rows = dot(one_hot_rows(slots_ref), target_ref[...]).astype(bf16)
@@ -108,6 +94,16 @@
         out_ref[one, right] = rows[two, :HALF]
         out_ref[two, left] = rows[one, HALF:]
         out_ref[two, right] = rows[two, HALF:]
+    lane = lax.broadcasted_iota(jnp.int32, (8, 128), 1)
+    facts = jnp.zeros((8, 128), f32)
+    given = (rewards_ref[0], rewards_ref[1], ids_ref[0], ids_ref[1], lengths_ref[0, 0], lengths_ref[0, 1])
+    for k, fact in enumerate(given):
+        facts = jnp.where(lane % 8 == k, fact.astype(f32), facts)
+    high = facts.astype(bf16).astype(f32)
+    middle = (facts - high).astype(bf16).astype(f32)
+    low = facts - high - middle
+    coded = jnp.where(lane < 8, high, jnp.where(lane < 16, middle, low))
+    out_ref[:, FACTS_AT:] = jnp.broadcast_to(coded[0:1], (ROWS, 128)).astype(bf16)
 
 
 def pack(kernel, width, operands, after=(), small=()):
@@ -133,6 +129,23 @@
         out_shape=jax.ShapeDtypeStruct(rows.shape, rows.dtype),
         input_output_aliases={0: 0},
     )(rows, *after)
+
+
+def halves_kernel(first_ref, second_ref, policy_ref, averaged_ref):
+    policy_ref[...] = first_ref[...]
+    averaged_ref[...] = second_ref[...]
+
+
+def halves(first, second):
+    part = lambda at: pl.BlockSpec((SHARD, HALF), lambda i: (at, 0))
+    return pl.pallas_call(
+        halves_kernel,
+        grid=(1,),
+        in_specs=[part(0), part(1)],
+        out_specs=[part(0)] * 2,
+        out_shape=[jax.ShapeDtypeStruct((SHARD, HALF), bf16)] * 2,
+        compiler_params=BIG,
+    )(first, second)
 
 
 def attention_kernel(lengths_ref, q_ref, k_ref, v_ref, *rest):
@@ -180,12 +193,12 @@
         out_ref[block : block + 1, :] = facts[0:1]
 
 
-def advantage_kernel(place_ref, facts_ref, out_ref):
-    facts = facts_ref[...]
+def advantage_kernel(place_ref, one, two, three, four, out_ref):
+    facts = jnp.concatenate([one[...], two[...], three[...], four[...]], axis=0)
     row = lax.broadcasted_iota(jnp.int32, facts.shape, 0)
     lane = lax.broadcasted_iota(jnp.int32, facts.shape, 1)
     ids = pltpu.roll(facts, 128 - 2, 1)
-    chip = (place_ref[3] * 2 + place_ref[4]) * SPAN + place_ref[0] * 4 + place_ref[1] * 2
+    chip = place_ref[0] * 4 + place_ref[1] * 2
     own, other = chip + place_ref[2], chip + 1 - place_ref[2]
 
     def fact(device, at):
@@ -203,7 +216,7 @@
 
 
 def project_most_kernel(
-    place_ref, own_p, other_p, own_r, other_r, w0, sm, sp, s2, o0, om, op,
+    place_ref, own_p, other_p, own_r, other_r, w0, sm, sp, s2, o0, om, op, after,
     y_p, y_r, late_p, late_r, rows_p, rows_r, weight_p, weight_r, sems,
 ):
     z, xh = place_ref[3], place_ref[4]
@@ -271,7 +284,7 @@
             VMEM((Q_WIDTH, HALF), bf16),
             pltpu.SemaphoreType.DMA((2,)),
         ],
-        compiler_params=BIG,
+        compiler_params=HUGE,
         cost_estimate=BRIEF,
     )(place, *outs, *weights)
 
@@ -284,7 +297,7 @@
 
 
 def project_last_kernel(
-    place_ref, rows_p, rows_r, o2p, o2e, y_p, y_r, mine_ref, theirs_ref,
+    place_ref, rows_p, rows_r, o2p, o2e, y_p, y_r, mine_ref, theirs_ref, after,
     y_ref, stats_ref, late_p, late_r, sums,
 ):
     j = pl.program_id(0)
@@ -316,7 +329,7 @@
         stats_ref[...] = stats
 
 
-def project_last(place, parts, weights, target):
+def project_last(place, parts, weights, target, after):
     steps = HALF // WIDE
     chunk = lambda rows: pl.BlockSpec((rows, WIDE), lambda j, place: (0, j))
     fixed = lambda width: pl.BlockSpec((2 * ROWS, width), lambda j, place: (0, 0))
@@ -332,6 +345,7 @@
             + [
                 pl.BlockSpec((ROWS, WIDE), lambda j, place: (0, TARGET_AT // WIDE + place[2] * steps + j)),
                 pl.BlockSpec((ROWS, WIDE), lambda j, place: (0, TARGET_AT // WIDE + (1 - place[2]) * steps + j)),
+                in_place(),
             ],
             out_specs=[chunk(2 * ROWS), fixed(128)],
             scratch_shapes=[
@@ -344,20 +358,25 @@
             jax.ShapeDtypeStruct((2 * ROWS, HALF), f32),
             jax.ShapeDtypeStruct((2 * ROWS, 128), f32),
         ],
-        compiler_params=BIG,
+        compiler_params=HUGE,
         cost_estimate=pl.CostEstimate(
             flops=2 * ROWS * Q_WIDTH * HALF, bytes_accessed=10 << 20, transcendentals=0
         ),
-    )(place, rows_p, rows_r, *weights, y_p, y_r, target, target)
+    )(place, rows_p, rows_r, *weights, y_p, y_r, target, target, after)
 
 
 def gradient_kernel(
     place_ref, own_ref, other_ref, y_ref, stats_ref, more_ref, mine_ref, theirs_ref, facts_ref,
-    a0, a1, a2, a3, grad, rows,
+    a0, a1, a2, a3, b0, b1, b2, b3, rows, grad, terms, y, sems, first_out, second_out, out_sems,
 ):
-    z = place_ref[3]
-    rows[:ROWS, :] = own_ref[...]
-    rows[ROWS:, :] = other_ref[...]
+    y_at, z = place_ref[0], place_ref[3]
+    fetch = []
+    for side, source in enumerate((own_ref, other_ref)):
+        part = pl.ds(side * ROWS, ROWS)
+        fetch.append(pltpu.make_async_copy(y_ref.at[part, :], y.at[part, :], sems.at[side]))
+        fetch.append(pltpu.make_async_copy(source, rows.at[part, :], sems.at[2]))
+    for copy in (fetch[0], fetch[2], fetch[1], fetch[3]):
+        copy.start()
     row = lax.broadcasted_iota(jnp.int32, (ROWS, 1), 0)
     for side in range(2):
         here = slice(side * ROWS, (side + 1) * ROWS)
@@ -383,57 +402,68 @@
         scale = weight / policy_norm
         slope = scale * (1.0 - along) / policy_norm
         target = (mine_ref if side == 0 else theirs_ref)[...].astype(f32)
-        grad[here, :] = (y_ref[here, :] * slope - target * scale).astype(bf16)
+        fetch[2 * side].wait()
+        grad[here, :] = (y[here, :] * slope - target * scale).astype(bf16)
+
+    fetch[1].wait()
+    fetch[3].wait()
+    copies = []
+
+    def give(source, out, at):
+        copies.append(pltpu.make_async_copy(source, out, out_sems.at[at]))
+        copies[-1].start()
 
     for d, out in enumerate((a0, a1, a2, a3)):
-        first = pl.multiple_of(lax.rem(z + d, 4) * PIECE, 128)
-        out[...] = outer(rows[:, pl.ds(first, PIECE)], grad[:, :PIECE])
+        at = lax.rem(z + d, 4)
+        term = outer(rows[:, pl.ds(pl.multiple_of(at * PIECE, 128), PIECE)], grad[...])
+        first_out[d] = term[:, :PIECE]
+        give(first_out.at[d], out, d)
+        terms[...] = term[:, PIECE:].reshape(2, 4, 80, PIECE)
+        for k, second in enumerate((b0, b1, b2, b3)):
+            here = pl.ds(2 * at, 2)
+            second_out[k, here] = terms[:, lax.rem(y_at + k, 4)]
+            give(second_out.at[k, here], second.at[here], 4 + 4 * d + k)
+    for copy in copies:
+        copy.wait()
 
 
 def outer(rows, grad):
     return lax.dot_general(rows, grad, (((0,), (0,)), ((), ())), preferred_element_type=f32).astype(bf16)
 
 
-def second_half_kernel(place_ref, own_ref, other_ref, grad_ref, b0, b1, b2, b3, rows, terms):
-    rows[:ROWS, :] = own_ref[...]
-    rows[ROWS:, :] = other_ref[...]
-    for k in range(4):
-        terms[...] = outer(rows[:, k * PIECE : (k + 1) * PIECE], grad_ref[:, PIECE:]).reshape(2, 4, 80, PIECE)
-        for d, out in enumerate((b0, b1, b2, b3)):
-            out[2 * k : 2 * k + 2] = terms[:, lax.rem(place_ref[0] + d, 4)]
-
-
 def gradient(place, own, other, y, stats, more, target, facts):
-    cost = pl.CostEstimate(flops=2 * ROWS * Q_WIDTH * HALF, bytes_accessed=8 << 20, transcendentals=0)
-    *first, grad = pl.pallas_call(
+    pieces = pl.pallas_call(
         gradient_kernel,
         grid_spec=pltpu.PrefetchScalarGridSpec(
             num_scalar_prefetch=1,
             grid=(1,),
-            in_specs=[whole()] * 5
+            in_specs=[in_place()] * 3
+            + [pl.BlockSpec((2 * ROWS, 128), lambda i, place: (0, 0))] * 2
             + [
                 pl.BlockSpec((ROWS, HALF), lambda i, place: (0, TARGET_AT // HALF + place[2])),
                 pl.BlockSpec((ROWS, HALF), lambda i, place: (0, TARGET_AT // HALF + 1 - place[2])),
-                whole(),
+                pl.BlockSpec((8, 128), lambda i, place: (0, 0)),
             ],
-            out_specs=[whole()] * 5,
-            scratch_shapes=[VMEM((2 * ROWS, Q_WIDTH), bf16)],
+            out_specs=[in_place()] * 8,
+            scratch_shapes=[
+                VMEM((2 * ROWS, Q_WIDTH), bf16),
+                VMEM((2 * ROWS, HALF), bf16),
+                VMEM((2, 4, 80, PIECE), bf16),
+                VMEM((2 * ROWS, HALF), f32),
+                pltpu.SemaphoreType.DMA((3,)),
+                VMEM((4, PIECE, PIECE), bf16),
+                VMEM((4, 8, 80, PIECE), bf16),
+                pltpu.SemaphoreType.DMA((20,)),
+            ],
         ),
         out_shape=[jax.ShapeDtypeStruct((PIECE, PIECE), bf16)] * 4
-        + [jax.ShapeDtypeStruct((2 * ROWS, HALF), bf16)],
-        compiler_params=SMALL,
-        cost_estimate=cost,
+        + [jax.ShapeDtypeStruct((8, 80, PIECE), bf16)] * 4,
+        compiler_params=HUGE,
+        cost_estimate=pl.CostEstimate(
+            flops=4 * ROWS * Q_WIDTH * HALF, bytes_accessed=16 << 20, transcendentals=0
+        ),
     )(place, own, other, y, stats, more, target, target, facts)
-    second = pl.pallas_call(
-        second_half_kernel,
-        in_specs=[scalars()] + [whole()] * 3,
-        out_specs=[whole()] * 4,
-        out_shape=[jax.ShapeDtypeStruct((8, 80, PIECE), bf16)] * 4,
-        scratch_shapes=[VMEM((2 * ROWS, Q_WIDTH), bf16), VMEM((2, 4, 80, PIECE), bf16)],
-        compiler_params=SMALL,
-        cost_estimate=cost,
-    )(place, own, other, grad)
-    return first, second
+    return pieces[:4], pieces[4:]
 
 
 def total_of(refs, index):
@@ -559,23 +589,23 @@
     w0 = jnp.concatenate([half(policy_weight), half(ema_weight)], axis=0)
     sm, sp, o0 = send(w0, "z", ring(1)), send(w0, "z", ring(-1)), send(w0, X, ACROSS)
     s2, op, om = send(sm, "z", ring(1)), send(o0, "z", ring(-1)), send(sm, X, ACROSS)
-    o2p, o2e = send(s2[:SHARD], X, ACROSS), send(om[SHARD:], "z", ring(1))
+    late_p, late_e = halves(s2, om)
+    o2p, o2e = send(late_p, X, ACROSS), send(late_e, "z", ring(1))
 
     exchange = functools.partial(lax.all_to_all, axis_name=DP, split_axis=0, concat_axis=0, tiled=True)
     rows_policy = exchange(
         pack(
             pack_policy_kernel,
             FACTS_AT + 128,
-            (send_slot, q_policy, kv_policy),
+            (send_slot, q_policy, kv_policy, target),
             small=(rewards, group_ids, lengths),
-            after=(w0,),
         )
     )
     packed = pack(
-        pack_reference_kernel, Q_WIDTH + D_OUT + 1024, (send_slot, q_reference, kv_reference, target)
+        functools.partial(pack_rows_kernel, Q_WIDTH), Q_WIDTH + 1024, (send_slot, q_reference, kv_reference)
     )
     rows_reference = exchange(hold(packed, (rows_policy, sm, sp, o0)))
-    out_policy = attend(rows_policy, lengths, Q_WIDTH)
+    out_policy = attend(rows_policy, lengths, TARGET_AT + D_OUT)
     other_policy = send(out_policy, "c", FLIP)
     facts = pl.pallas_call(
         facts_kernel,
@@ -585,25 +615,23 @@
         out_shape=jax.ShapeDtypeStruct((SPAN, 128), f32),
         compiler_params=SMALL,
     )(rows_policy)
-    facts = jnp.broadcast_to(facts[None], (8, SPAN, 128)).reshape(8 * SPAN, 128)
-    facts = lax.all_to_all(facts, FSDP, split_axis=0, concat_axis=0, tiled=True)
+    facts = jnp.concatenate([facts, send(facts, "xh", FLIP)], axis=0)
     advantages = pl.pallas_call(
         advantage_kernel,
-        in_specs=[scalars(), whole()],
+        in_specs=[scalars()] + [whole()] * 4,
         out_specs=whole(),
         out_shape=jax.ShapeDtypeStruct((8, 128), f32),
         compiler_params=SMALL,
-    )(place, facts)
-
-    out_reference = attend(rows_reference, lengths, TARGET_AT + D_OUT, (advantages,))
+    )(place, facts, *[send(facts, "z", ring(d)) for d in (1, 2, 3)])
+    out_reference = attend(rows_reference, lengths, Q_WIDTH)
     other_reference = send(out_reference, "c", FLIP)
 
     outs = (out_policy, other_policy, out_reference, other_reference)
-    parts = project_most(place, outs, (w0, sm, sp, s2, o0, om, op))
-    y_policy, stats = project_last(place, parts, (o2p, o2e), rows_reference)
+    parts = project_most(place, outs, (w0, sm, sp, s2, o0, om, op, facts))
+    y_policy, stats = project_last(place, parts, (o2p, o2e), rows_policy, advantages)
     more = send(stats, "c", FLIP)
     first, second = gradient(
-        place, out_policy, other_policy, y_policy, stats, more, rows_reference, advantages
+        place, out_policy, other_policy, y_policy, stats, more, rows_policy, advantages
     )
 
     first = [first[0]] + [send(first[d], "z", ring(d)) for d in (1, 2, 3)]

time: 264 us -> 257 us (0.973)
  local copies, waits for them, and re-layouts: 13.7 us -> 6.76 us
  starting transfers between devices: 66.3 us -> 62.9 us
  waiting for transfers between devices: 117 us -> 120 us
    ppermute x1, waiting for transfers between devices: 2.34 us -> 29.8 us  [local(): send(w0, 'z', ring(1))]
    all_to_all x1, waiting for transfers between devices: 23.9 us -> 0.01 us  [local(): rows_reference = exchange(hold(packed, (rows_policy, sm, sp, o0)))]
    all_to_all x1, waiting for transfers between devices: 18.5 us -> 0.01 us  [local(): exchange(pack(pack_policy_kernel, FACTS_AT + 128, (send_slot, q_policy, k...]
    ppermute x2 -> x6, waiting for transfers between devices: 4.44 us -> 20 us  [the longest x1 17.8 us: local(): facts = jnp.concatenate([facts, send(facts, 'xh', FLIP)], axis=0)]
    all_to_all x1 -> x0, starting transfers between devices: 7.48 us -> none  [local(): facts = lax.all_to_all(facts, FSDP, split_axis=0, concat_axis=0, tiled=True)]
    ppermute x2 -> x6, starting transfers between devices: 3.62 us -> 9.65 us  [the longest x3 5.71 us: local(): send(facts, 'z', ring(d))]
    pallas_call x1, Pallas kernels: 5.84 us -> 9.81 us  [gradient(): pl.pallas_call(gradient_kernel, grid_spec=pltpu.PrefetchScalarGridSpec(nu...]
    unnamed x36 -> x32, local copies, waits for them, and re-layouts: 8.74 us -> 4.9 us
  transfers between devices with their start and end apart: 36 -> 39, of which waited for: 24 -> 23; matrix products, arithmetic and copies ran while one was open for 1% -> 1% of each run, Pallas kernels for 14% -> 15%
where the time goes in v4:
time: 257 us; the launch traced here: 256 us
  waiting for transfers between devices  120 us (47%)
  Pallas kernels  65.1 us (25%)
  starting transfers between devices  62.9 us (24%)
  local copies, waits for them, and re-layouts  6.76 us (3%)
    ppermute x1, waiting for transfers between devices, local(): send(w0, 'z', ring(1))  29.8 us
    ppermute x1, waiting for transfers between devices, local(): facts = jnp.concatenate([facts, send(facts, 'xh', FLIP)], axis=0)  17.8 us
    ppermute x3, waiting for transfers between devices, local(): first = [first[0]] + [send(first[d], 'z', ring(d)) for d in (1, 2, 3)]  15.9 us
    ppermute x1, waiting for transfers between devices, local(): near = send(second[1], 'y', ring(1))  14.8 us
    pallas_call x1, Pallas kernels, project_most(): pl.pallas_call(project_most_kernel, in_specs=[scalars()] + [in_place()] *...  14.6 us
    pallas_call x2, Pallas kernels, attend(): pl.pallas_call(attention_kernel, grid=(KV_HEADS,), in_specs=[scalars(), p...  13.7 us
    pallas_call x1, Pallas kernels, gradient(): pl.pallas_call(gradient_kernel, grid_spec=pltpu.PrefetchScalarGridSpec(nu...  9.81 us
    pallas_call x2, Pallas kernels, pack(): pl.pallas_call(kernel, in_specs=[scalars()] * len(small) + [whole()] * le...  7.89 us
  transfers between devices with their start and end apart: 39, of which 23 were waited for; matrix products, arithmetic and copies ran while one was open for 1% of the time, Pallas kernels for 15%

profile of v4, /device:TPU:0, one launch (start us, length us, event | category | flops | bytes accessed | tf_op | source)
XLA Modules:
  0.0 256.5 jit_solution(1711259821099682859)
XLA Ops:
  0.6 4.6 %shard_map.130 = bf16[256,6272]{1,0:T(8,128)(2,1)} custom-call(f32[2]{0:T(128)} %rewards_ref.1, s32[2]{0:T(128)} %ids_ref.1, s32[1,2]{1,0:T(1,128)} %lengths_ref.5, s32[1,256]{1,0:T(1,128)} %slots_ref.3, bf16[256,2560]{1,0:T(8,128)(2,1)} %q_ref.2, bf16[256,1024]{1,0:T(8,128)(2,1)} %kv_ref.2, bf16[256,2560]{1,0:T(8,128)(2,1)} %target_ref.1), custom_call_target="tpu_custom_call" | custom-call | flops 1 | bytes 1 | tf_op jit(solution)/shard_map/pallas_call | solution.py:110
  5.2 5.6 %all-to-all-start = ((bf16[16,16,6272]{2,1,0:T(8,128)(2,1)}), bf16[16,16,6272]{2,1,0:T(8,128)(2,1)S(1)}, u32[]{:S(2)}, u32[]{:S(2)}) async-start(bf16[16,16,6272]{2,1,0:T(8,128)(2,1)} %bitcast.37), calls=%async_computation | async-start | bytes 6422528 | tf_op jit(solution)/shard_map/all_to_all | solution.py:596
  14.7 3.2 %collective-permute-start.3 = (bf16[640,1280]{1,0:T(8,128)(2,1)S(1)}, bf16[640,1280]{1,0:T(8,128)(2,1)}, u32[]{:S(2)}, u32[]{:S(2)}) collective-permute-start(bf16[640,1280]{1,0:T(8,128)(2,1)S(1)} %pad_maximum_fusion.w0), channel_id=1, source_target_pairs={{16,1},{1,16},{0,17},{17,0},{18,3},{3,18},{2,19},{19,2},{20,5},{5,... | collective-permute-start | bytes 4915208 | tf_op jit(solution)/shard_map/ppermute | solution.py:590
  20.1 3.3 %shard_map.132.rows_ref = bf16[256,3584]{1,0:T(8,128)(2,1)} custom-call(s32[1,256]{1,0:T(1,128)} %slots_ref.3, bf16[256,2560]{1,0:T(8,128)(2,1)} %q_ref.3, bf16[256,1024]{1,0:T(8,128)(2,1)} %kv_ref.3), custom_call_target="tpu_custom_call" | custom-call | flops 1 | bytes 1 | tf_op jit(solution)/shard_map/pallas_call | solution.py:110
  23.4 29.8 %collective-permute-done.1.rest_1_.sm = bf16[640,1280]{1,0:T(8,128)(2,1)S(1)} collective-permute-done((bf16[640,1280]{1,0:T(8,128)(2,1)S(1)}, bf16[640,1280]{1,0:T(8,128)(2,1)S(1)}, u32[]{:S(2)}, u32[]{:S(2)}) %collective-permute-start.1) | collective-permute-done | bytes 1638432 | tf_op jit(solution)/shard_map/ppermute | solution.py:590
  57.1 4.7 %all-to-all-start.1 = ((bf16[16,16,3584]{2,1,0:T(8,128)(2,1)}), bf16[16,16,3584]{2,1,0:T(8,128)(2,1)}, u32[]{:S(2)}, u32[]{:S(2)}) async-start(bf16[16,16,3584]{2,1,0:T(8,128)(2,1)} %bitcast.36), calls=%async_computation.1 | async-start | bytes 3670016 | tf_op jit(solution)/shard_map/all_to_all | solution.py:607
  63.6 2.7 %collective-permute-start.6 = (bf16[640,1280]{1,0:T(8,128)(2,1)}, bf16[640,1280]{1,0:T(8,128)(2,1)}, u32[]{:S(2)}, u32[]{:S(2)}) collective-permute-start(bf16[640,1280]{1,0:T(8,128)(2,1)} %copy-done.13), channel_id=1, source_target_pairs={{16,1},{1,16},{0,17},{17,0},{18,3},{3,18},{2,19},{19,2},{20,5},{5,... | collective-permute-start | bytes 4915208 | tf_op jit(solution)/shard_map/ppermute | solution.py:591
  69.6 17.8 %collective-permute-done.8 = f32[16,128]{1,0:T(8,128)S(1)} collective-permute-done((f32[16,128]{1,0:T(8,128)S(1)}, f32[16,128]{1,0:T(8,128)S(1)}, u32[]{:S(2)}, u32[]{:S(2)}) %collective-permute-start.8) | collective-permute-done | bytes 8224 | tf_op jit(solution)/shard_map/ppermute | solution.py:618
  88.7 6.9 %shard_map.131.own_p.own_ref = bf16[256,2560]{1,0:T(8,128)(2,1)} custom-call(s32[1,2]{1,0:T(1,128)} %lengths_ref.5, bf16[256,6272]{1,0:T(8,128)(2,1)} %bitcast.22, bf16[256,6272]{1,0:T(8,128)(2,1)} %bitcast.23, bf16[256,6272]{1,0:T(8,128)(2,1)} %bitcast.24), custom_call_target="tpu_custom_call" | custom-call | flops 1 | bytes 1 | tf_op jit(solution)/shard_map/pallas_call | solution.py:172
  95.6 6.8 %shard_map.134.own_r = bf16[256,2560]{1,0:T(8,128)(2,1)} custom-call(s32[1,2]{1,0:T(1,128)} %lengths_ref.5, bf16[256,3584]{1,0:T(8,128)(2,1)} %bitcast.8.q_ref.k_ref.v_ref, bf16[256,3584]{1,0:T(8,128)(2,1)} %bitcast.8.q_ref.k_ref.v_ref, bf16[256,3584]{1,0:T(8,128)(2,1)} %bitcast.8.q_ref.k_ref.v_ref), custom_call_target="tpu_custom_call" | custom-call | flops 1 | bytes 1 | tf_op jit(solution)/shard_map/pallas_call | solution.py:172
  114.5 14.6 %shard_map.136 = (f32[512,1280]{1,0:T(8,128)}, f32[512,1280]{1,0:T(8,128)}, bf16[512,384]{1,0:T(8,128)(2,1)}, bf16[512,384]{1,0:T(8,128)(2,1)}) custom-call(s32[5]{0:T(128)} %copy-done.9, bf16[256,2560]{1,0:T(8,128)(2,1)} %shard_map.131.own_p.own_ref, bf16[256,2560]{1,0:T(8,128)(2,1)} %collective-permute-done.other_p.other_ref, ...), custom_call_target="tpu_custom_call" | custom-call | flops 1 | bytes 1 | tf_op jit(solution)/shard_map/pallas_call | solution.py:274
  131.8 6.8 %shard_map.139 = (f32[512,1280]{1,0:T(8,128)}, f32[512,128]{1,0:T(8,128)}) custom-call(s32[5]{0:T(128)} %copy-done.9, bf16[512,384]{1,0:T(8,128)(2,1)} %get-tuple-element.29.rows_p, bf16[512,384]{1,0:T(8,128)(2,1)} %get-tuple-element.30.rows_r, bf16[320,1280]{1,0:T(8,128)(2,1)} %collective-permute-done.9.o2p, bf16[320,1280]{1,0:T(8,128)(2,1)} %copy-done.14, ...), custom_call_target="tpu_custom_call" | custom-call | flops 1677721600 | bytes 10485760 | tf_op jit(solution)/shard_map/pallas_call | solution.py:337
  141.2 9.8 %shard_map.140 = (bf16[640,640]{1,0:T(8,128)(2,1)}, bf16[640,640]{1,0:T(8,128)(2,1)}, bf16[640,640]{1,0:T(8,128)(2,1)}, bf16[640,640]{1,0:T(8,128)(2,1)}, bf16[8...) custom-call(s32[5]{0:T(128)} %copy-done.9, ...), custom_call_target="tpu_custom_call" | custom-call | flops 3355443200 | bytes 16777216 | tf_op jit(solution)/shard_map/pallas_call | solution.py:435
  151.7 3.4 %collective-permute-start.16 = (bf16[640,640]{1,0:T(8,128)(2,1)}, bf16[640,640]{1,0:T(8,128)(2,1)}, u32[]{:S(2)}, u32[]{:S(2)}) collective-permute-start(bf16[640,640]{1,0:T(8,128)(2,1)} %get-tuple-element.39), channel_id=1, source_target_pairs={{0,4},{2,6},{4,0},{6,2},{1,5},{3,7},{5,1},{7,3},{8,12},{10,14},{12... | collective-permute-start | bytes 2457608 | tf_op jit(solution)/shard_map/ppermute | solution.py:637
  158.0 14.8 %collective-permute-done.21.rest_0_ = bf16[8,80,640]{2,1,0:T(8,128)(2,1)S(1)} collective-permute-done((bf16[8,80,640]{2,1,0:T(8,128)(2,1)}, bf16[8,80,640]{2,1,0:T(8,128)(2,1)S(1)}, u32[]{:S(2)}, u32[]{:S(2)}) %collective-permute-start.21) | collective-permute-done | bytes 819232 | tf_op jit(solution)/shard_map/ppermute | solution.py:638
  175.2 15.7 %collective-permute-done.16 = bf16[640,640]{1,0:T(8,128)(2,1)} collective-permute-done((bf16[640,640]{1,0:T(8,128)(2,1)}, bf16[640,640]{1,0:T(8,128)(2,1)}, u32[]{:S(2)}, u32[]{:S(2)}) %collective-permute-start.16) | collective-permute-done | bytes 819232 | tf_op jit(solution)/shard_map/ppermute | solution.py:637
  200.2 3.8 %collective-permute-start.25 = (bf16[2,80,640]{2,1,0:T(8,128)(2,1)S(1)}, bf16[2,80,640]{2,1,0:T(8,128)(2,1)S(1)}, u32[]{:S(2)}, u32[]{:S(2)}) collective-permute-start(bf16[2,80,640]{2,1,0:T(8,128)(2,1)S(1)} %get-tuple-element.51), channel_id=1, source_target_pairs={{0,4},{2,6},{4,0},{6,2},{1,5},{3,7},{5,1},{7,3},{8,12},{10,14},{12... | collective-permute-start | bytes 614408 | tf_op jit(solution)/shard_map/ppermute | solution.py:644
  207.6 4.9 %collective-permute-done.25.refs_6_ = bf16[2,80,640]{2,1,0:T(8,128)(2,1)S(1)} collective-permute-done((bf16[2,80,640]{2,1,0:T(8,128)(2,1)S(1)}, bf16[2,80,640]{2,1,0:T(8,128)(2,1)S(1)}, u32[]{:S(2)}, u32[]{:S(2)}) %collective-permute-start.25) | collective-permute-done | bytes 204832 | tf_op jit(solution)/shard_map/ppermute | solution.py:644
  214.8 5.4 %collective-permute-done.27 = bf16[80,1280]{1,0:T(8,128)(2,1)S(1)} collective-permute-done((bf16[80,1280]{1,0:T(8,128)(2,1)S(1)}, bf16[80,1280]{1,0:T(8,128)(2,1)S(1)}, u32[]{:S(2)}, u32[]{:S(2)}) %collective-permute-start.27) | collective-permute-done | bytes 204832 | tf_op jit(solution)/shard_map/ppermute | solution.py:650
  220.4 5.7 %collective-permute-done.28 = bf16[80,1280]{1,0:T(8,128)(2,1)S(1)} collective-permute-done((bf16[80,1280]{1,0:T(8,128)(2,1)S(1)}, bf16[80,1280]{1,0:T(8,128)(2,1)S(1)}, u32[]{:S(2)}, u32[]{:S(2)}) %collective-permute-start.28) | collective-permute-done | bytes 204832 | tf_op jit(solution)/shard_map/ppermute | solution.py:651
  229.1 2.9 %collective-permute-done.29 = bf16[80,1280]{1,0:T(8,128)(2,1)S(1)} collective-permute-done((bf16[80,1280]{1,0:T(8,128)(2,1)S(1)}, bf16[80,1280]{1,0:T(8,128)(2,1)S(1)}, u32[]{:S(2)}, u32[]{:S(2)}) %collective-permute-start.29) | collective-permute-done | bytes 204832 | tf_op jit(solution)/shard_map/ppermute | solution.py:653
  241.3 3.3 %collective-permute-done.33 = f32[8,128]{1,0:T(8,128)S(1)} collective-permute-done((f32[8,128]{1,0:T(8,128)S(1)}, f32[8,128]{1,0:T(8,128)S(1)}, u32[]{:S(2)}, u32[]{:S(2)}) %collective-permute-start.33) | collective-permute-done | bytes 4128 | tf_op jit(solution)/shard_map/ppermute | solution.py:662
  244.9 3.6 %collective-permute-start.35 = (f32[8,128]{1,0:T(8,128)S(1)}, f32[8,128]{1,0:T(8,128)S(1)}, u32[]{:S(2)}, u32[]{:S(2)}) collective-permute-start(f32[8,128]{1,0:T(8,128)S(1)} %add.25), channel_id=1, source_target_pairs={{0,2},{2,4},{4,6},{6,0},{1,3},{3,5},{5,7},{7,1},{8,10},{10,12},{12... | collective-permute-start | bytes 12296 | tf_op jit(solution)/shard_map/ppermute | solution.py:663
  252.1 4.2 %shard_map.146 = (f32[320,2560]{1,0:T(8,128)}, bf16[320,2560]{1,0:T(8,128)(2,1)}, f32[320,2560]{1,0:T(8,128)}) custom-call(s32[5]{0:T(128)S(1)} %copy-done.10, f32[8,128]{1,0:T(8,128)S(1)} %add_add_fusion.square_ref, bf16[4,80,1280]{2,1,0:T(8,128)(2,1)S(1)} %pad_maximum_fusion.1.mine_ref, bf16[4,80,1280]{2,1,0:T(8,128)(2,1)S(1)} %collective-permute-done.32.theirs_ref, ...), custom_call_target="tpu_custom_call" | custom-call | tf_op jit(solution)/shard_map/pallas_call | solution.py:548
  (112 shorter events, 71.3 us)
Async XLA Ops:
  5.2 50.3 %all-to-all-start = ((bf16[16,16,6272]{2,1,0:T(8,128)(2,1)}), bf16[16,16,6272]{2,1,0:T(8,128)(2,1)S(1)}, u32[]{:S(2)}, u32[]{:S(2)}) async-start(bf16[16,16,6272]{2,1,0:T(8,128)(2,1)} %bitcast.37), calls=%async_computation | async-start | bytes 6422528 | tf_op jit(solution)/shard_map/all_to_all | solution.py:596
  12.7 40.5 %collective-permute-start.1 = (bf16[640,1280]{1,0:T(8,128)(2,1)S(1)}, bf16[640,1280]{1,0:T(8,128)(2,1)S(1)}, u32[]{:S(2)}, u32[]{:S(2)}) collective-permute-start(bf16[640,1280]{1,0:T(8,128)(2,1)S(1)} %pad_maximum_fusion.w0), channel_id=1, source_target_pairs={{0,2},{2,4},{4,6},{6,0},{1,3},{3,5},{5,7},{7,1},{8,10},{10,12},{12... | collective-permute-start | bytes 4915208 | tf_op jit(solution)/shard_map/ppermute | solution.py:590
  14.7 39.2 %collective-permute-start.3 = (bf16[640,1280]{1,0:T(8,128)(2,1)S(1)}, bf16[640,1280]{1,0:T(8,128)(2,1)}, u32[]{:S(2)}, u32[]{:S(2)}) collective-permute-start(bf16[640,1280]{1,0:T(8,128)(2,1)S(1)} %pad_maximum_fusion.w0), channel_id=1, source_target_pairs={{16,1},{1,16},{0,17},{17,0},{18,3},{3,18},{2,19},{19,2},{20,5},{5,... | collective-permute-start | bytes 4915208 | tf_op jit(solution)/shard_map/ppermute | solution.py:590
  17.9 37.6 %collective-permute-start.2 = (bf16[640,1280]{1,0:T(8,128)(2,1)S(1)}, bf16[640,1280]{1,0:T(8,128)(2,1)}, u32[]{:S(2)}, u32[]{:S(2)}) collective-permute-start(bf16[640,1280]{1,0:T(8,128)(2,1)S(1)} %pad_maximum_fusion.w0), channel_id=1, source_target_pairs={{0,6},{2,0},{4,2},{6,4},{1,7},{3,1},{5,3},{7,5},{8,14},{10,8},{12,... | collective-permute-start | bytes 4915208 | tf_op jit(solution)/shard_map/ppermute | solution.py:590
  57.1 38.5 %all-to-all-start.1 = ((bf16[16,16,3584]{2,1,0:T(8,128)(2,1)}), bf16[16,16,3584]{2,1,0:T(8,128)(2,1)}, u32[]{:S(2)}, u32[]{:S(2)}) async-start(bf16[16,16,3584]{2,1,0:T(8,128)(2,1)} %bitcast.36), calls=%async_computation.1 | async-start | bytes 3670016 | tf_op jit(solution)/shard_map/all_to_all | solution.py:607
  61.8 41.1 %collective-permute-start.5 = (bf16[640,1280]{1,0:T(8,128)(2,1)}, bf16[640,1280]{1,0:T(8,128)(2,1)}, u32[]{:S(2)}, u32[]{:S(2)}) collective-permute-start(bf16[640,1280]{1,0:T(8,128)(2,1)} %copy-done.13), channel_id=1, source_target_pairs={{0,2},{2,4},{4,6},{6,0},{1,3},{3,5},{5,7},{7,1},{8,10},{10,12},{12... | collective-permute-start | bytes 4915208 | tf_op jit(solution)/shard_map/ppermute | solution.py:591
  63.6 41.5 %collective-permute-start.6 = (bf16[640,1280]{1,0:T(8,128)(2,1)}, bf16[640,1280]{1,0:T(8,128)(2,1)}, u32[]{:S(2)}, u32[]{:S(2)}) collective-permute-start(bf16[640,1280]{1,0:T(8,128)(2,1)} %copy-done.13), channel_id=1, source_target_pairs={{16,1},{1,16},{0,17},{17,0},{18,3},{3,18},{2,19},{19,2},{20,5},{5,... | collective-permute-start | bytes 4915208 | tf_op jit(solution)/shard_map/ppermute | solution.py:591
  66.4 48.1 %collective-permute-start.7 = (bf16[640,1280]{1,0:T(8,128)(2,1)}, bf16[640,1280]{1,0:T(8,128)(2,1)}, u32[]{:S(2)}, u32[]{:S(2)}) collective-permute-start(bf16[640,1280]{1,0:T(8,128)(2,1)} %collective-permute-done.3.rest_3_.o0), channel_id=1, source_target_pairs={{0,6},{2,0},{4,2},{6,4},{1,7},{3,1},{5,3},{7,5},{8,14},{10,8},{12,... | collective-permute-start | bytes 4915208 | tf_op jit(solution)/shard_map/ppermute | solution.py:591
  68.3 19.0 %collective-permute-start.8 = (f32[16,128]{1,0:T(8,128)S(1)}, f32[16,128]{1,0:T(8,128)S(1)}, u32[]{:S(2)}, u32[]{:S(2)}) collective-permute-start(f32[16,128]{1,0:T(8,128)S(1)} %shard_map.135), channel_id=1, source_target_pairs={{0,1},{1,0},{2,3},{3,2},{4,5},{5,4},{6,7},{7,6},{8,9},{9,8},{10,11... | collective-permute-start | bytes 24584 | tf_op jit(solution)/shard_map/ppermute | solution.py:618
  87.3 15.1 %collective-permute-start.11 = (f32[32,128]{1,0:T(8,128)S(1)}, f32[32,128]{1,0:T(8,128)S(1)}, u32[]{:S(2)}, u32[]{:S(2)}) collective-permute-start(f32[32,128]{1,0:T(8,128)S(1)} %pad_maximum_fusion.2.after.one), channel_id=1, source_target_pairs={{0,2},{2,4},{4,6},{6,0},{1,3},{3,5},{5,7},{7,1},{8,10},{10,12},{12... | collective-permute-start | bytes 49160 | tf_op jit(solution)/shard_map/ppermute | solution.py:625
  95.6 18.9 %collective-permute-start = (bf16[256,2560]{1,0:T(8,128)(2,1)}, bf16[256,2560]{1,0:T(8,128)(2,1)}, u32[]{:S(2)}, u32[]{:S(2)}) collective-permute-start(bf16[256,2560]{1,0:T(8,128)(2,1)} %shard_map.131.own_p.own_ref), channel_id=1, source_target_pairs={{0,8},{8,0},{1,9},{9,1},{2,10},{10,2},{3,11},{11,3},{4,12},{12,4},... | collective-permute-start | bytes 3932168 | tf_op jit(solution)/shard_map/ppermute | solution.py:609
  102.4 12.0 %collective-permute-start.4 = (bf16[256,2560]{1,0:T(8,128)(2,1)}, bf16[256,2560]{1,0:T(8,128)(2,1)}, u32[]{:S(2)}, u32[]{:S(2)}) collective-permute-start(bf16[256,2560]{1,0:T(8,128)(2,1)} %shard_map.134.own_r), channel_id=1, source_target_pairs={{0,8},{8,0},{1,9},{9,1},{2,10},{10,2},{3,11},{11,3},{4,12},{12,4},... | collective-permute-start | bytes 3932168 | tf_op jit(solution)/shard_map/ppermute | solution.py:627
  109.9 21.1 %collective-permute-start.10 = (bf16[320,1280]{1,0:T(8,128)(2,1)}, bf16[320,1280]{1,0:T(8,128)(2,1)S(1)}, u32[]{:S(2)}, u32[]{:S(2)}) collective-permute-start(bf16[320,1280]{1,0:T(8,128)(2,1)} %get-tuple-element.32), channel_id=1, source_target_pairs={{0,2},{2,4},{4,6},{6,0},{1,3},{3,5},{5,7},{7,1},{8,10},{10,12},{12... | collective-permute-start | bytes 2457608 | tf_op jit(solution)/shard_map/ppermute | solution.py:593
  109.9 21.5 %collective-permute-start.9 = (bf16[320,1280]{1,0:T(8,128)(2,1)}, bf16[320,1280]{1,0:T(8,128)(2,1)}, u32[]{:S(2)}, u32[]{:S(2)}) collective-permute-start(bf16[320,1280]{1,0:T(8,128)(2,1)} %get-tuple-element.31), channel_id=1, source_target_pairs={{16,1},{1,16},{0,17},{17,0},{18,3},{3,18},{2,19},{19,2},{20,5},{5,... | collective-permute-start | bytes 2457608 | tf_op jit(solution)/shard_map/ppermute | solution.py:593
  151.0 21.8 %collective-permute-start.21 = (bf16[8,80,640]{2,1,0:T(8,128)(2,1)}, bf16[8,80,640]{2,1,0:T(8,128)(2,1)S(1)}, u32[]{:S(2)}, u32[]{:S(2)}) collective-permute-start(bf16[8,80,640]{2,1,0:T(8,128)(2,1)} %get-tuple-element.46), channel_id=1, source_target_pairs={{0,32},{32,64},{64,96},{96,0},{1,33},{33,65},{65,97},{97,1},{2,34}... | collective-permute-start | bytes 2457608 | tf_op jit(solution)/shard_map/ppermute | solution.py:638
  151.4 23.8 %collective-permute-start.15 = (bf16[640,640]{1,0:T(8,128)(2,1)}, bf16[640,640]{1,0:T(8,128)(2,1)S(1)}, u32[]{:S(2)}, u32[]{:S(2)}) collective-permute-start(bf16[640,640]{1,0:T(8,128)(2,1)} %get-tuple-element.38), channel_id=1, source_target_pairs={{0,2},{2,4},{4,6},{6,0},{1,3},{3,5},{5,7},{7,1},{8,10},{10,12},{12... | collective-permute-start | bytes 2457608 | tf_op jit(solution)/shard_map/ppermute | solution.py:637
  151.7 39.2 %collective-permute-start.16 = (bf16[640,640]{1,0:T(8,128)(2,1)}, bf16[640,640]{1,0:T(8,128)(2,1)}, u32[]{:S(2)}, u32[]{:S(2)}) collective-permute-start(bf16[640,640]{1,0:T(8,128)(2,1)} %get-tuple-element.39), channel_id=1, source_target_pairs={{0,4},{2,6},{4,0},{6,2},{1,5},{3,7},{5,1},{7,3},{8,12},{10,14},{12... | collective-permute-start | bytes 2457608 | tf_op jit(solution)/shard_map/ppermute | solution.py:637
  155.1 36.1 %collective-permute-start.17 = (bf16[640,640]{1,0:T(8,128)(2,1)}, bf16[640,640]{1,0:T(8,128)(2,1)}, u32[]{:S(2)}, u32[]{:S(2)}) collective-permute-start(bf16[640,640]{1,0:T(8,128)(2,1)} %get-tuple-element.40), channel_id=1, source_target_pairs={{0,6},{2,0},{4,2},{6,4},{1,7},{3,1},{5,3},{7,5},{8,14},{10,8},{12,... | collective-permute-start | bytes 2457608 | tf_op jit(solution)/shard_map/ppermute | solution.py:637
  155.3 43.5 %collective-permute-start.23 = (bf16[8,80,640]{2,1,0:T(8,128)(2,1)}, bf16[8,80,640]{2,1,0:T(8,128)(2,1)S(1)}, u32[]{:S(2)}, u32[]{:S(2)}) collective-permute-start(bf16[8,80,640]{2,1,0:T(8,128)(2,1)} %get-tuple-element.48), channel_id=1, source_target_pairs={{0,96},{32,0},{64,32},{96,64},{1,97},{33,1},{65,33},{97,65},{2,98}... | collective-permute-start | bytes 2457608 | tf_op jit(solution)/shard_map/ppermute | solution.py:640
  173.7 25.1 %collective-permute-start.22 = (bf16[8,80,640]{2,1,0:T(8,128)(2,1)}, bf16[8,80,640]{2,1,0:T(8,128)(2,1)S(1)}, u32[]{:S(2)}, u32[]{:S(2)}) collective-permute-start(bf16[8,80,640]{2,1,0:T(8,128)(2,1)} %shard_map.142), channel_id=1, source_target_pairs={{0,64},{32,96},{64,0},{96,32},{1,65},{33,97},{65,1},{97,33},{2,66}... | collective-permute-start | bytes 2457608 | tf_op jit(solution)/shard_map/ppermute | solution.py:639
  193.1 10.8 %collective-permute-start.18 = (bf16[2,80,640]{2,1,0:T(8,128)(2,1)S(1)}, bf16[2,80,640]{2,1,0:T(8,128)(2,1)S(1)}, u32[]{:S(2)}, u32[]{:S(2)}) collective-permute-start(bf16[2,80,640]{2,1,0:T(8,128)(2,1)S(1)} %get-tuple-element.42), channel_id=1, source_target_pairs={{0,32},{32,64},{64,96},{96,0},{1,33},{33,65},{65,97},{97,1},{2,34}... | collective-permute-start | bytes 614408 | tf_op jit(solution)/shard_map/ppermute | solution.py:643
  195.5 10.2 %collective-permute-start.19 = (bf16[2,80,640]{2,1,0:T(8,128)(2,1)S(1)}, bf16[2,80,640]{2,1,0:T(8,128)(2,1)S(1)}, u32[]{:S(2)}, u32[]{:S(2)}) collective-permute-start(bf16[2,80,640]{2,1,0:T(8,128)(2,1)S(1)} %get-tuple-element.43), channel_id=1, source_target_pairs={{0,64},{32,96},{64,0},{96,32},{1,65},{33,97},{65,1},{97,33},{2,66}... | collective-permute-start | bytes 614408 | tf_op jit(solution)/shard_map/ppermute | solution.py:643
  200.2 12.3 %collective-permute-start.25 = (bf16[2,80,640]{2,1,0:T(8,128)(2,1)S(1)}, bf16[2,80,640]{2,1,0:T(8,128)(2,1)S(1)}, u32[]{:S(2)}, u32[]{:S(2)}) collective-permute-start(bf16[2,80,640]{2,1,0:T(8,128)(2,1)S(1)} %get-tuple-element.51), channel_id=1, source_target_pairs={{0,4},{2,6},{4,0},{6,2},{1,5},{3,7},{5,1},{7,3},{8,12},{10,14},{12... | collective-permute-start | bytes 614408 | tf_op jit(solution)/shard_map/ppermute | solution.py:644
  203.9 8.5 %collective-permute-start.26 = (bf16[2,80,640]{2,1,0:T(8,128)(2,1)S(1)}, bf16[2,80,640]{2,1,0:T(8,128)(2,1)S(1)}, u32[]{:S(2)}, u32[]{:S(2)}) collective-permute-start(bf16[2,80,640]{2,1,0:T(8,128)(2,1)S(1)} %get-tuple-element.52), channel_id=1, source_target_pairs={{0,6},{2,0},{4,2},{6,4},{1,7},{3,1},{5,3},{7,5},{8,14},{10,8},{12,... | collective-permute-start | bytes 614408 | tf_op jit(solution)/shard_map/ppermute | solution.py:644
  (31 other events, 289.6 us)

commit v5 on v4

--- a/solution.py
+++ b/solution.py
@@ -615,6 +615,7 @@
         out_shape=jax.ShapeDtypeStruct((SPAN, 128), f32),
         compiler_params=SMALL,
     )(rows_policy)
+    facts = hold(facts, (out_policy,))
     facts = jnp.concatenate([facts, send(facts, "xh", FLIP)], axis=0)
     advantages = pl.pallas_call(
         advantage_kernel,

time: 257 us -> 255 us (level)
  waiting for transfers between devices: 120 us -> 111 us
  starting transfers between devices: 62.9 us -> 68.1 us
    ppermute x1, waiting for transfers between devices: 17.8 us -> 10.3 us  [local(): facts = jnp.concatenate([facts, send(facts, 'xh', FLIP)], axis=0)]
    ppermute x3, waiting for transfers between devices: 0.01 us -> 4.74 us  [local(): send(facts, 'z', ring(d))]
    ppermute x3, starting transfers between devices: 4.25 us -> 7.85 us  [local(): second = [second[0]] + [send(second[d], 'z', ring(d)) for d in (1, 2, 3)]]
    ppermute x3, waiting for transfers between devices: 6.66 us -> 3.78 us  [local(): second = [second[0]] + [send(second[d], 'z', ring(d)) for d in (1, 2, 3)]]
    unnamed x32 -> x38, local copies, waits for them, and re-layouts: 4.9 us -> 6.25 us
where the time goes in v5:
time: 255 us
  waiting for transfers between devices  111 us (44%)
  starting transfers between devices  68.1 us (27%)
  Pallas kernels  65.2 us (26%)
  local copies, waits for them, and re-layouts  8.12 us (3%)
    ppermute x1, waiting for transfers between devices, local(): send(w0, 'z', ring(1))  29.8 us
    ppermute x3, waiting for transfers between devices, local(): first = [first[0]] + [send(first[d], 'z', ring(d)) for d in (1, 2, 3)]  16.8 us
    pallas_call x1, Pallas kernels, project_most(): pl.pallas_call(project_most_kernel, in_specs=[scalars()] + [in_place()] *...  14.6 us
    ppermute x1, waiting for transfers between devices, local(): near = send(second[1], 'y', ring(1))  14 us
    pallas_call x2, Pallas kernels, attend(): pl.pallas_call(attention_kernel, grid=(KV_HEADS,), in_specs=[scalars(), p...  13.8 us
    ppermute x1, waiting for transfers between devices, local(): facts = jnp.concatenate([facts, send(facts, 'xh', FLIP)], axis=0)  10.3 us
    pallas_call x1, Pallas kernels, gradient(): pl.pallas_call(gradient_kernel, grid_spec=pltpu.PrefetchScalarGridSpec(nu...  9.8 us
    pallas_call x2, Pallas kernels, pack(): pl.pallas_call(kernel, in_specs=[scalars()] * len(small) + [whole()] * le...  7.89 us
  transfers between devices with their start and end apart: 39, of which 23 were waited for; matrix products, arithmetic and copies ran while one was open for 1% of the time, Pallas kernels for 15%

profile of v5, /device:TPU:0, one launch (start us, length us, event | category | flops | bytes accessed | tf_op | source)
XLA Modules:
  0.0 254.7 jit_solution(15331148585639454184)
XLA Ops:
  0.6 4.6 %shard_map.130 = bf16[256,6272]{1,0:T(8,128)(2,1)} custom-call(f32[2]{0:T(128)} %rewards_ref.1, s32[2]{0:T(128)} %ids_ref.1, s32[1,2]{1,0:T(1,128)} %lengths_ref.5, s32[1,256]{1,0:T(1,128)} %slots_ref.3, bf16[256,2560]{1,0:T(8,128)(2,1)} %q_ref.2, bf16[256,1024]{1,0:T(8,128)(2,1)} %kv_ref.2, bf16[256,2560]{1,0:T(8,128)(2,1)} %target_ref.1), custom_call_target="tpu_custom_call" | custom-call | flops 1 | bytes 1 | tf_op jit(solution)/shard_map/pallas_call | solution.py:110
  5.2 5.6 %all-to-all-start = ((bf16[16,16,6272]{2,1,0:T(8,128)(2,1)}), bf16[16,16,6272]{2,1,0:T(8,128)(2,1)S(1)}, u32[]{:S(2)}, u32[]{:S(2)}) async-start(bf16[16,16,6272]{2,1,0:T(8,128)(2,1)} %bitcast.40), calls=%async_computation | async-start | bytes 6422528 | tf_op jit(solution)/shard_map/all_to_all | solution.py:596
  14.7 3.2 %collective-permute-start.3 = (bf16[640,1280]{1,0:T(8,128)(2,1)S(1)}, bf16[640,1280]{1,0:T(8,128)(2,1)}, u32[]{:S(2)}, u32[]{:S(2)}) collective-permute-start(bf16[640,1280]{1,0:T(8,128)(2,1)S(1)} %pad_maximum_fusion.w0), channel_id=1, source_target_pairs={{16,1},{1,16},{0,17},{17,0},{18,3},{3,18},{2,19},{19,2},{20,5},{5,... | collective-permute-start | bytes 4915208 | tf_op jit(solution)/shard_map/ppermute | solution.py:590
  20.1 3.3 %shard_map.132.rows_ref = bf16[256,3584]{1,0:T(8,128)(2,1)} custom-call(s32[1,256]{1,0:T(1,128)} %slots_ref.3, bf16[256,2560]{1,0:T(8,128)(2,1)} %q_ref.3, bf16[256,1024]{1,0:T(8,128)(2,1)} %kv_ref.3), custom_call_target="tpu_custom_call" | custom-call | flops 1 | bytes 1 | tf_op jit(solution)/shard_map/pallas_call | solution.py:110
  23.4 29.8 %collective-permute-done.1.rest_1_.sm = bf16[640,1280]{1,0:T(8,128)(2,1)S(1)} collective-permute-done((bf16[640,1280]{1,0:T(8,128)(2,1)S(1)}, bf16[640,1280]{1,0:T(8,128)(2,1)S(1)}, u32[]{:S(2)}, u32[]{:S(2)}) %collective-permute-start.1) | collective-permute-done | bytes 1638432 | tf_op jit(solution)/shard_map/ppermute | solution.py:590
  57.1 4.4 %all-to-all-start.1 = ((bf16[16,16,3584]{2,1,0:T(8,128)(2,1)}), bf16[16,16,3584]{2,1,0:T(8,128)(2,1)S(1)}, u32[]{:S(2)}, u32[]{:S(2)}) async-start(bf16[16,16,3584]{2,1,0:T(8,128)(2,1)} %bitcast.39), calls=%async_computation.1 | async-start | bytes 3670016 | tf_op jit(solution)/shard_map/all_to_all | solution.py:607
  63.3 2.8 %collective-permute-start.6 = (bf16[640,1280]{1,0:T(8,128)(2,1)}, bf16[640,1280]{1,0:T(8,128)(2,1)}, u32[]{:S(2)}, u32[]{:S(2)}) collective-permute-start(bf16[640,1280]{1,0:T(8,128)(2,1)} %copy-done.16), channel_id=1, source_target_pairs={{16,1},{1,16},{0,17},{17,0},{18,3},{3,18},{2,19},{19,2},{20,5},{5,... | collective-permute-start | bytes 4915208 | tf_op jit(solution)/shard_map/ppermute | solution.py:591
  67.9 7.0 %shard_map.131.rest_0_.own_p.own_ref = bf16[256,2560]{1,0:T(8,128)(2,1)} custom-call(s32[1,2]{1,0:T(1,128)} %lengths_ref.5, bf16[256,6272]{1,0:T(8,128)(2,1)} %bitcast.22, bf16[256,6272]{1,0:T(8,128)(2,1)} %bitcast.23, bf16[256,6272]{1,0:T(8,128)(2,1)} %bitcast.24), custom_call_target="tpu_custom_call" | custom-call | flops 1 | bytes 1 | tf_op jit(solution)/shard_map/pallas_call | solution.py:172
  76.8 10.3 %collective-permute-done.8 = f32[16,128]{1,0:T(8,128)S(1)} collective-permute-done((f32[16,128]{1,0:T(8,128)}, f32[16,128]{1,0:T(8,128)S(1)}, u32[]{:S(2)}, u32[]{:S(2)}) %collective-permute-start.8) | collective-permute-done | bytes 8224 | tf_op jit(solution)/shard_map/ppermute | solution.py:619
  90.4 6.8 %shard_map.134.own_r = bf16[256,2560]{1,0:T(8,128)(2,1)} custom-call(s32[1,2]{1,0:T(1,128)} %lengths_ref.5, bf16[256,3584]{1,0:T(8,128)(2,1)} %bitcast.36, bf16[256,3584]{1,0:T(8,128)(2,1)} %bitcast.37, bf16[256,3584]{1,0:T(8,128)(2,1)} %bitcast.38), custom_call_target="tpu_custom_call" | custom-call | flops 1 | bytes 1 | tf_op jit(solution)/shard_map/pallas_call | solution.py:172
  97.2 4.7 %collective-permute-done.11.two = f32[32,128]{1,0:T(8,128)S(1)} collective-permute-done((f32[32,128]{1,0:T(8,128)S(1)}, f32[32,128]{1,0:T(8,128)S(1)}, u32[]{:S(2)}, u32[]{:S(2)}) %collective-permute-start.11) | collective-permute-done | bytes 16416 | tf_op jit(solution)/shard_map/ppermute | solution.py:626
  112.9 14.6 %shard_map.137 = (f32[512,1280]{1,0:T(8,128)}, f32[512,1280]{1,0:T(8,128)}, bf16[512,384]{1,0:T(8,128)(2,1)}, bf16[512,384]{1,0:T(8,128)(2,1)}) custom-call(s32[5]{0:T(128)} %copy-done.10, bf16[256,2560]{1,0:T(8,128)(2,1)} %shard_map.131.rest_0_.own_p.own_ref, bf16[256,2560]{1,0:T(8,128)(2,1)} %collective-permute-done.other_p.other_ref, ...), custom_call_target="tpu_custom_call" | custom-call | flops 1 | bytes 1 | tf_op jit(solution)/shard_map/pallas_call | solution.py:274
  129.7 6.8 %shard_map.140 = (f32[512,1280]{1,0:T(8,128)}, f32[512,128]{1,0:T(8,128)}) custom-call(s32[5]{0:T(128)} %copy-done.10, bf16[512,384]{1,0:T(8,128)(2,1)} %get-tuple-element.29.rows_p, bf16[512,384]{1,0:T(8,128)(2,1)} %get-tuple-element.30.rows_r, bf16[320,1280]{1,0:T(8,128)(2,1)} %collective-permute-done.9.o2p, bf16[320,1280]{1,0:T(8,128)(2,1)} %copy-done.17, ...), custom_call_target="tpu_custom_call" | custom-call | flops 1677721600 | bytes 10485760 | tf_op jit(solution)/shard_map/pallas_call | solution.py:337
  139.0 9.8 %shard_map.141 = (bf16[640,640]{1,0:T(8,128)(2,1)}, bf16[640,640]{1,0:T(8,128)(2,1)}, bf16[640,640]{1,0:T(8,128)(2,1)}, bf16[640,640]{1,0:T(8,128)(2,1)}, bf16[8...) custom-call(s32[5]{0:T(128)} %copy-done.10, ...), custom_call_target="tpu_custom_call" | custom-call | flops 3355443200 | bytes 16777216 | tf_op jit(solution)/shard_map/pallas_call | solution.py:435
  151.5 2.7 %collective-permute-start.16 = (bf16[640,640]{1,0:T(8,128)(2,1)}, bf16[640,640]{1,0:T(8,128)(2,1)}, u32[]{:S(2)}, u32[]{:S(2)}) collective-permute-start(bf16[640,640]{1,0:T(8,128)(2,1)} %get-tuple-element.39), channel_id=1, source_target_pairs={{0,4},{2,6},{4,0},{6,2},{1,5},{3,7},{5,1},{7,3},{8,12},{10,14},{12... | collective-permute-start | bytes 2457608 | tf_op jit(solution)/shard_map/ppermute | solution.py:638
  156.7 14.0 %collective-permute-done.21.rest_0_ = bf16[8,80,640]{2,1,0:T(8,128)(2,1)S(1)} collective-permute-done((bf16[8,80,640]{2,1,0:T(8,128)(2,1)}, bf16[8,80,640]{2,1,0:T(8,128)(2,1)S(1)}, u32[]{:S(2)}, u32[]{:S(2)}) %collective-permute-start.21) | collective-permute-done | bytes 819232 | tf_op jit(solution)/shard_map/ppermute | solution.py:639
  173.5 16.6 %collective-permute-done.16 = bf16[640,640]{1,0:T(8,128)(2,1)} collective-permute-done((bf16[640,640]{1,0:T(8,128)(2,1)}, bf16[640,640]{1,0:T(8,128)(2,1)}, u32[]{:S(2)}, u32[]{:S(2)}) %collective-permute-start.16) | collective-permute-done | bytes 819232 | tf_op jit(solution)/shard_map/ppermute | solution.py:638
  200.0 2.8 %collective-permute-start.25 = (bf16[2,80,640]{2,1,0:T(8,128)(2,1)S(1)}, bf16[2,80,640]{2,1,0:T(8,128)(2,1)S(1)}, u32[]{:S(2)}, u32[]{:S(2)}) collective-permute-start(bf16[2,80,640]{2,1,0:T(8,128)(2,1)S(1)} %get-tuple-element.51), channel_id=1, source_target_pairs={{0,4},{2,6},{4,0},{6,2},{1,5},{3,7},{5,1},{7,3},{8,12},{10,14},{12... | collective-permute-start | bytes 614408 | tf_op jit(solution)/shard_map/ppermute | solution.py:645
  203.8 3.7 %collective-permute-start.26 = (bf16[2,80,640]{2,1,0:T(8,128)(2,1)S(1)}, bf16[2,80,640]{2,1,0:T(8,128)(2,1)S(1)}, u32[]{:S(2)}, u32[]{:S(2)}) collective-permute-start(bf16[2,80,640]{2,1,0:T(8,128)(2,1)S(1)} %get-tuple-element.52), channel_id=1, source_target_pairs={{0,6},{2,0},{4,2},{6,4},{1,7},{3,1},{5,3},{7,5},{8,14},{10,8},{12,... | collective-permute-start | bytes 614408 | tf_op jit(solution)/shard_map/ppermute | solution.py:645
  207.6 3.8 %collective-permute-done.25.refs_6_ = bf16[2,80,640]{2,1,0:T(8,128)(2,1)S(1)} collective-permute-done((bf16[2,80,640]{2,1,0:T(8,128)(2,1)S(1)}, bf16[2,80,640]{2,1,0:T(8,128)(2,1)S(1)}, u32[]{:S(2)}, u32[]{:S(2)}) %collective-permute-start.25) | collective-permute-done | bytes 204832 | tf_op jit(solution)/shard_map/ppermute | solution.py:645
  214.6 4.6 %collective-permute-done.27 = bf16[80,1280]{1,0:T(8,128)(2,1)S(1)} collective-permute-done((bf16[80,1280]{1,0:T(8,128)(2,1)S(1)}, bf16[80,1280]{1,0:T(8,128)(2,1)S(1)}, u32[]{:S(2)}, u32[]{:S(2)}) %collective-permute-start.27) | collective-permute-done | bytes 204832 | tf_op jit(solution)/shard_map/ppermute | solution.py:651
  219.3 5.7 %collective-permute-done.28 = bf16[80,1280]{1,0:T(8,128)(2,1)S(1)} collective-permute-done((bf16[80,1280]{1,0:T(8,128)(2,1)S(1)}, bf16[80,1280]{1,0:T(8,128)(2,1)S(1)}, u32[]{:S(2)}, u32[]{:S(2)}) %collective-permute-start.28) | collective-permute-done | bytes 204832 | tf_op jit(solution)/shard_map/ppermute | solution.py:652
  227.4 3.5 %collective-permute-done.29 = bf16[80,1280]{1,0:T(8,128)(2,1)S(1)} collective-permute-done((bf16[80,1280]{1,0:T(8,128)(2,1)S(1)}, bf16[80,1280]{1,0:T(8,128)(2,1)S(1)}, u32[]{:S(2)}, u32[]{:S(2)}) %collective-permute-start.29) | collective-permute-done | bytes 204832 | tf_op jit(solution)/shard_map/ppermute | solution.py:654
  250.3 4.2 %shard_map.147 = (f32[320,2560]{1,0:T(8,128)}, bf16[320,2560]{1,0:T(8,128)(2,1)}, f32[320,2560]{1,0:T(8,128)}) custom-call(s32[5]{0:T(128)S(1)} %copy-done.11, f32[8,128]{1,0:T(8,128)S(1)} %add_add_fusion.square_ref, bf16[4,80,1280]{2,1,0:T(8,128)(2,1)S(1)} %pad_maximum_fusion.1.mine_ref, bf16[4,80,1280]{2,1,0:T(8,128)(2,1)S(1)} %collective-permute-done.32.theirs_ref, ...), custom_call_target="tpu_custom_call" | custom-call | tf_op jit(solution)/shard_map/pallas_call | solution.py:548
  (119 shorter events, 78.5 us)
Async XLA Ops:
  5.2 50.3 %all-to-all-start = ((bf16[16,16,6272]{2,1,0:T(8,128)(2,1)}), bf16[16,16,6272]{2,1,0:T(8,128)(2,1)S(1)}, u32[]{:S(2)}, u32[]{:S(2)}) async-start(bf16[16,16,6272]{2,1,0:T(8,128)(2,1)} %bitcast.40), calls=%async_computation | async-start | bytes 6422528 | tf_op jit(solution)/shard_map/all_to_all | solution.py:596
  12.7 40.5 %collective-permute-start.1 = (bf16[640,1280]{1,0:T(8,128)(2,1)S(1)}, bf16[640,1280]{1,0:T(8,128)(2,1)S(1)}, u32[]{:S(2)}, u32[]{:S(2)}) collective-permute-start(bf16[640,1280]{1,0:T(8,128)(2,1)S(1)} %pad_maximum_fusion.w0), channel_id=1, source_target_pairs={{0,2},{2,4},{4,6},{6,0},{1,3},{3,5},{5,7},{7,1},{8,10},{10,12},{12... | collective-permute-start | bytes 4915208 | tf_op jit(solution)/shard_map/ppermute | solution.py:590
  14.7 39.2 %collective-permute-start.3 = (bf16[640,1280]{1,0:T(8,128)(2,1)S(1)}, bf16[640,1280]{1,0:T(8,128)(2,1)}, u32[]{:S(2)}, u32[]{:S(2)}) collective-permute-start(bf16[640,1280]{1,0:T(8,128)(2,1)S(1)} %pad_maximum_fusion.w0), channel_id=1, source_target_pairs={{16,1},{1,16},{0,17},{17,0},{18,3},{3,18},{2,19},{19,2},{20,5},{5,... | collective-permute-start | bytes 4915208 | tf_op jit(solution)/shard_map/ppermute | solution.py:590
  17.9 37.6 %collective-permute-start.2 = (bf16[640,1280]{1,0:T(8,128)(2,1)S(1)}, bf16[640,1280]{1,0:T(8,128)(2,1)}, u32[]{:S(2)}, u32[]{:S(2)}) collective-permute-start(bf16[640,1280]{1,0:T(8,128)(2,1)S(1)} %pad_maximum_fusion.w0), channel_id=1, source_target_pairs={{0,6},{2,0},{4,2},{6,4},{1,7},{3,1},{5,3},{7,5},{8,14},{10,8},{12,... | collective-permute-start | bytes 4915208 | tf_op jit(solution)/shard_map/ppermute | solution.py:590
  57.1 32.0 %all-to-all-start.1 = ((bf16[16,16,3584]{2,1,0:T(8,128)(2,1)}), bf16[16,16,3584]{2,1,0:T(8,128)(2,1)S(1)}, u32[]{:S(2)}, u32[]{:S(2)}) async-start(bf16[16,16,3584]{2,1,0:T(8,128)(2,1)} %bitcast.39), calls=%async_computation.1 | async-start | bytes 3670016 | tf_op jit(solution)/shard_map/all_to_all | solution.py:607
  61.5 40.5 %collective-permute-start.5 = (bf16[640,1280]{1,0:T(8,128)(2,1)}, bf16[640,1280]{1,0:T(8,128)(2,1)S(1)}, u32[]{:S(2)}, u32[]{:S(2)}) collective-permute-start(bf16[640,1280]{1,0:T(8,128)(2,1)} %copy-done.16), channel_id=1, source_target_pairs={{0,2},{2,4},{4,6},{6,0},{1,3},{3,5},{5,7},{7,1},{8,10},{10,12},{12... | collective-permute-start | bytes 4915208 | tf_op jit(solution)/shard_map/ppermute | solution.py:591
  63.3 40.4 %collective-permute-start.6 = (bf16[640,1280]{1,0:T(8,128)(2,1)}, bf16[640,1280]{1,0:T(8,128)(2,1)}, u32[]{:S(2)}, u32[]{:S(2)}) collective-permute-start(bf16[640,1280]{1,0:T(8,128)(2,1)} %copy-done.16), channel_id=1, source_target_pairs={{16,1},{1,16},{0,17},{17,0},{18,3},{3,18},{2,19},{19,2},{20,5},{5,... | collective-permute-start | bytes 4915208 | tf_op jit(solution)/shard_map/ppermute | solution.py:591
  66.1 46.8 %collective-permute-start.7 = (bf16[640,1280]{1,0:T(8,128)(2,1)}, bf16[640,1280]{1,0:T(8,128)(2,1)}, u32[]{:S(2)}, u32[]{:S(2)}) collective-permute-start(bf16[640,1280]{1,0:T(8,128)(2,1)} %collective-permute-done.3.rest_3_.o0), channel_id=1, source_target_pairs={{0,6},{2,0},{4,2},{6,4},{1,7},{3,1},{5,3},{7,5},{8,14},{10,8},{12,... | collective-permute-start | bytes 4915208 | tf_op jit(solution)/shard_map/ppermute | solution.py:591
  75.6 11.5 %collective-permute-start.8 = (f32[16,128]{1,0:T(8,128)}, f32[16,128]{1,0:T(8,128)S(1)}, u32[]{:S(2)}, u32[]{:S(2)}) collective-permute-start(f32[16,128]{1,0:T(8,128)} %shard_map.136), channel_id=1, source_target_pairs={{0,1},{1,0},{2,3},{3,2},{4,5},{5,4},{6,7},{7,6},{8,9},{9,8},{10,11... | collective-permute-start | bytes 24584 | tf_op jit(solution)/shard_map/ppermute | solution.py:619
  87.8 14.2 %collective-permute-start.11 = (f32[32,128]{1,0:T(8,128)S(1)}, f32[32,128]{1,0:T(8,128)S(1)}, u32[]{:S(2)}, u32[]{:S(2)}) collective-permute-start(f32[32,128]{1,0:T(8,128)S(1)} %pad_maximum_fusion.2.after.one), channel_id=1, source_target_pairs={{0,2},{2,4},{4,6},{6,0},{1,3},{3,5},{5,7},{7,1},{8,10},{10,12},{12... | collective-permute-start | bytes 49160 | tf_op jit(solution)/shard_map/ppermute | solution.py:626
  89.2 23.7 %collective-permute-start = (bf16[256,2560]{1,0:T(8,128)(2,1)}, bf16[256,2560]{1,0:T(8,128)(2,1)}, u32[]{:S(2)}, u32[]{:S(2)}) collective-permute-start(bf16[256,2560]{1,0:T(8,128)(2,1)} %shard_map.131.rest_0_.own_p.own_ref), channel_id=1, source_target_pairs={{0,8},{8,0},{1,9},{9,1},{2,10},{10,2},{3,11},{11,3},{4,12},{12,4},... | collective-permute-start | bytes 3932168 | tf_op jit(solution)/shard_map/ppermute | solution.py:609
  102.0 10.9 %collective-permute-start.4 = (bf16[256,2560]{1,0:T(8,128)(2,1)}, bf16[256,2560]{1,0:T(8,128)(2,1)}, u32[]{:S(2)}, u32[]{:S(2)}) collective-permute-start(bf16[256,2560]{1,0:T(8,128)(2,1)} %shard_map.134.own_r), channel_id=1, source_target_pairs={{0,8},{8,0},{1,9},{9,1},{2,10},{10,2},{3,11},{11,3},{4,12},{12,4},... | collective-permute-start | bytes 3932168 | tf_op jit(solution)/shard_map/ppermute | solution.py:628
  107.6 21.2 %collective-permute-start.10 = (bf16[320,1280]{1,0:T(8,128)(2,1)}, bf16[320,1280]{1,0:T(8,128)(2,1)S(1)}, u32[]{:S(2)}, u32[]{:S(2)}) collective-permute-start(bf16[320,1280]{1,0:T(8,128)(2,1)} %get-tuple-element.32), channel_id=1, source_target_pairs={{0,2},{2,4},{4,6},{6,0},{1,3},{3,5},{5,7},{7,1},{8,10},{10,12},{12... | collective-permute-start | bytes 2457608 | tf_op jit(solution)/shard_map/ppermute | solution.py:593
  108.4 21.3 %collective-permute-start.9 = (bf16[320,1280]{1,0:T(8,128)(2,1)}, bf16[320,1280]{1,0:T(8,128)(2,1)}, u32[]{:S(2)}, u32[]{:S(2)}) collective-permute-start(bf16[320,1280]{1,0:T(8,128)(2,1)} %get-tuple-element.31), channel_id=1, source_target_pairs={{16,1},{1,16},{0,17},{17,0},{18,3},{3,18},{2,19},{19,2},{20,5},{5,... | collective-permute-start | bytes 2457608 | tf_op jit(solution)/shard_map/ppermute | solution.py:593
  148.9 21.8 %collective-permute-start.21 = (bf16[8,80,640]{2,1,0:T(8,128)(2,1)}, bf16[8,80,640]{2,1,0:T(8,128)(2,1)S(1)}, u32[]{:S(2)}, u32[]{:S(2)}) collective-permute-start(bf16[8,80,640]{2,1,0:T(8,128)(2,1)} %get-tuple-element.46), channel_id=1, source_target_pairs={{0,32},{32,64},{64,96},{96,0},{1,33},{33,65},{65,97},{97,1},{2,34}... | collective-permute-start | bytes 2457608 | tf_op jit(solution)/shard_map/ppermute | solution.py:639
  150.6 22.9 %collective-permute-start.15 = (bf16[640,640]{1,0:T(8,128)(2,1)}, bf16[640,640]{1,0:T(8,128)(2,1)S(1)}, u32[]{:S(2)}, u32[]{:S(2)}) collective-permute-start(bf16[640,640]{1,0:T(8,128)(2,1)} %get-tuple-element.38), channel_id=1, source_target_pairs={{0,2},{2,4},{4,6},{6,0},{1,3},{3,5},{5,7},{7,1},{8,10},{10,12},{12... | collective-permute-start | bytes 2457608 | tf_op jit(solution)/shard_map/ppermute | solution.py:638
  151.5 38.5 %collective-permute-start.16 = (bf16[640,640]{1,0:T(8,128)(2,1)}, bf16[640,640]{1,0:T(8,128)(2,1)}, u32[]{:S(2)}, u32[]{:S(2)}) collective-permute-start(bf16[640,640]{1,0:T(8,128)(2,1)} %get-tuple-element.39), channel_id=1, source_target_pairs={{0,4},{2,6},{4,0},{6,2},{1,5},{3,7},{5,1},{7,3},{8,12},{10,14},{12... | collective-permute-start | bytes 2457608 | tf_op jit(solution)/shard_map/ppermute | solution.py:638
  154.2 36.1 %collective-permute-start.17 = (bf16[640,640]{1,0:T(8,128)(2,1)}, bf16[640,640]{1,0:T(8,128)(2,1)}, u32[]{:S(2)}, u32[]{:S(2)}) collective-permute-start(bf16[640,640]{1,0:T(8,128)(2,1)} %get-tuple-element.40), channel_id=1, source_target_pairs={{0,6},{2,0},{4,2},{6,4},{1,7},{3,1},{5,3},{7,5},{8,14},{10,8},{12,... | collective-permute-start | bytes 2457608 | tf_op jit(solution)/shard_map/ppermute | solution.py:638
  155.1 42.5 %collective-permute-start.23 = (bf16[8,80,640]{2,1,0:T(8,128)(2,1)}, bf16[8,80,640]{2,1,0:T(8,128)(2,1)S(1)}, u32[]{:S(2)}, u32[]{:S(2)}) collective-permute-start(bf16[8,80,640]{2,1,0:T(8,128)(2,1)} %get-tuple-element.48), channel_id=1, source_target_pairs={{0,96},{32,0},{64,32},{96,64},{1,97},{33,1},{65,33},{97,65},{2,98}... | collective-permute-start | bytes 2457608 | tf_op jit(solution)/shard_map/ppermute | solution.py:641
  171.5 26.1 %collective-permute-start.22 = (bf16[8,80,640]{2,1,0:T(8,128)(2,1)}, bf16[8,80,640]{2,1,0:T(8,128)(2,1)S(1)}, u32[]{:S(2)}, u32[]{:S(2)}) collective-permute-start(bf16[8,80,640]{2,1,0:T(8,128)(2,1)} %shard_map.143), channel_id=1, source_target_pairs={{0,64},{32,96},{64,0},{96,32},{1,65},{33,97},{65,1},{97,33},{2,66}... | collective-permute-start | bytes 2457608 | tf_op jit(solution)/shard_map/ppermute | solution.py:640
  192.2 11.6 %collective-permute-start.18 = (bf16[2,80,640]{2,1,0:T(8,128)(2,1)S(1)}, bf16[2,80,640]{2,1,0:T(8,128)(2,1)S(1)}, u32[]{:S(2)}, u32[]{:S(2)}) collective-permute-start(bf16[2,80,640]{2,1,0:T(8,128)(2,1)S(1)} %get-tuple-element.42), channel_id=1, source_target_pairs={{0,32},{32,64},{64,96},{96,0},{1,33},{33,65},{65,97},{97,1},{2,34}... | collective-permute-start | bytes 614408 | tf_op jit(solution)/shard_map/ppermute | solution.py:644
  193.8 13.8 %collective-permute-start.19 = (bf16[2,80,640]{2,1,0:T(8,128)(2,1)S(1)}, bf16[2,80,640]{2,1,0:T(8,128)(2,1)S(1)}, u32[]{:S(2)}, u32[]{:S(2)}) collective-permute-start(bf16[2,80,640]{2,1,0:T(8,128)(2,1)S(1)} %get-tuple-element.43), channel_id=1, source_target_pairs={{0,64},{32,96},{64,0},{96,32},{1,65},{33,97},{65,1},{97,33},{2,66}... | collective-permute-start | bytes 614408 | tf_op jit(solution)/shard_map/ppermute | solution.py:644
  195.4 12.2 %collective-permute-start.20 = (bf16[2,80,640]{2,1,0:T(8,128)(2,1)S(1)}, bf16[2,80,640]{2,1,0:T(8,128)(2,1)S(1)}, u32[]{:S(2)}, u32[]{:S(2)}) collective-permute-start(bf16[2,80,640]{2,1,0:T(8,128)(2,1)S(1)} %get-tuple-element.44), channel_id=1, source_target_pairs={{0,96},{32,0},{64,32},{96,64},{1,97},{33,1},{65,33},{97,65},{2,98}... | collective-permute-start | bytes 614408 | tf_op jit(solution)/shard_map/ppermute | solution.py:644
  200.0 11.4 %collective-permute-start.25 = (bf16[2,80,640]{2,1,0:T(8,128)(2,1)S(1)}, bf16[2,80,640]{2,1,0:T(8,128)(2,1)S(1)}, u32[]{:S(2)}, u32[]{:S(2)}) collective-permute-start(bf16[2,80,640]{2,1,0:T(8,128)(2,1)S(1)} %get-tuple-element.51), channel_id=1, source_target_pairs={{0,4},{2,6},{4,0},{6,2},{1,5},{3,7},{5,1},{7,3},{8,12},{10,14},{12... | collective-permute-start | bytes 614408 | tf_op jit(solution)/shard_map/ppermute | solution.py:645
  (34 other events, 289.1 us)

commit v6 on v5

--- a/solution.py
+++ b/solution.py
@@ -604,9 +604,6 @@
     packed = pack(
         functools.partial(pack_rows_kernel, Q_WIDTH), Q_WIDTH + 1024, (send_slot, q_reference, kv_reference)
     )
-    rows_reference = exchange(hold(packed, (rows_policy, sm, sp, o0)))
-    out_policy = attend(rows_policy, lengths, TARGET_AT + D_OUT)
-    other_policy = send(out_policy, "c", FLIP)
     facts = pl.pallas_call(
         facts_kernel,
         grid=(1,),
@@ -615,6 +612,9 @@
         out_shape=jax.ShapeDtypeStruct((SPAN, 128), f32),
         compiler_params=SMALL,
     )(rows_policy)
+    rows_reference = exchange(hold(packed, (facts, sm, sp, o0)))
+    out_policy = attend(rows_policy, lengths, TARGET_AT + D_OUT)
+    other_policy = send(out_policy, "c", FLIP)
     facts = hold(facts, (out_policy,))
     facts = jnp.concatenate([facts, send(facts, "xh", FLIP)], axis=0)
     advantages = pl.pallas_call(

time: 255 us -> 255 us (level)
    ppermute x1, waiting for transfers between devices: 29.8 us -> 3.16 us  [local(): send(w0, 'z', ring(1))]
    all_to_all x1, waiting for transfers between devices: 0.01 us -> 26.2 us  [local(): exchange(pack(pack_policy_kernel, FACTS_AT + 128, (send_slot, q_policy, k...]
    unnamed x38 -> x32, local copies, waits for them, and re-layouts: 6.25 us -> 4.17 us
  transfers between devices with their start and end apart: 39 -> 39, of which waited for: 23 -> 24; matrix products, arithmetic and copies ran while one was open for 1% -> 2% of each run, Pallas kernels for 15% -> 15%
where the time goes in v6:
time: 255 us; the launch traced here: 254 us
  waiting for transfers between devices  112 us (44%)
  starting transfers between devices  68.2 us (27%)
  Pallas kernels  65.1 us (26%)
  local copies, waits for them, and re-layouts  6.03 us (2%)
    all_to_all x1, waiting for transfers between devices, local(): exchange(pack(pack_policy_kernel, FACTS_AT + 128, (send_slot, q_policy, k...  26.2 us
    ppermute x3, waiting for transfers between devices, local(): first = [first[0]] + [send(first[d], 'z', ring(d)) for d in (1, 2, 3)]  16.8 us
    pallas_call x1, Pallas kernels, project_most(): pl.pallas_call(project_most_kernel, in_specs=[scalars()] + [in_place()] *...  14.6 us
    ppermute x1, waiting for transfers between devices, local(): near = send(second[1], 'y', ring(1))  14 us
    pallas_call x2, Pallas kernels, attend(): pl.pallas_call(attention_kernel, grid=(KV_HEADS,), in_specs=[scalars(), p...  13.7 us
    ppermute x1, waiting for transfers between devices, local(): facts = jnp.concatenate([facts, send(facts, 'xh', FLIP)], axis=0)  10.7 us
    pallas_call x1, Pallas kernels, gradient(): pl.pallas_call(gradient_kernel, grid_spec=pltpu.PrefetchScalarGridSpec(nu...  9.79 us
    pallas_call x2, Pallas kernels, pack(): pl.pallas_call(kernel, in_specs=[scalars()] * len(small) + [whole()] * le...  7.89 us
  transfers between devices with their start and end apart: 39, of which 24 were waited for; matrix products, arithmetic and copies ran while one was open for 2% of the time, Pallas kernels for 15%

profile of v6, /device:TPU:0, one launch (start us, length us, event | category | flops | bytes accessed | tf_op | source)
XLA Modules:
  0.0 254.2 jit_solution(776188415825821898)
XLA Ops:
  0.6 4.6 %shard_map.130 = bf16[256,6272]{1,0:T(8,128)(2,1)} custom-call(f32[2]{0:T(128)} %rewards_ref.1, s32[2]{0:T(128)} %ids_ref.1, s32[1,2]{1,0:T(1,128)} %lengths_ref.5, s32[1,256]{1,0:T(1,128)} %slots_ref.3, bf16[256,2560]{1,0:T(8,128)(2,1)} %q_ref.2, bf16[256,1024]{1,0:T(8,128)(2,1)} %kv_ref.2, bf16[256,2560]{1,0:T(8,128)(2,1)} %target_ref.1), custom_call_target="tpu_custom_call" | custom-call | flops 1 | bytes 1 | tf_op jit(solution)/shard_map/pallas_call | solution.py:110
  5.2 5.6 %all-to-all-start = ((bf16[16,16,6272]{2,1,0:T(8,128)(2,1)}), bf16[16,16,6272]{2,1,0:T(8,128)(2,1)S(1)}, u32[]{:S(2)}, u32[]{:S(2)}) async-start(bf16[16,16,6272]{2,1,0:T(8,128)(2,1)} %bitcast.39), calls=%async_computation | async-start | bytes 6422528 | tf_op jit(solution)/shard_map/all_to_all | solution.py:596
  15.8 3.2 %collective-permute-start.3 = (bf16[640,1280]{1,0:T(8,128)(2,1)}, bf16[640,1280]{1,0:T(8,128)(2,1)}, u32[]{:S(2)}, u32[]{:S(2)}) collective-permute-start(bf16[640,1280]{1,0:T(8,128)(2,1)} %pad_maximum_fusion.w0), channel_id=1, source_target_pairs={{16,1},{1,16},{0,17},{17,0},{18,3},{3,18},{2,19},{19,2},{20,5},{5,... | collective-permute-start | bytes 4915208 | tf_op jit(solution)/shard_map/ppermute | solution.py:590
  21.1 3.3 %shard_map.132.rows_ref = bf16[256,3584]{1,0:T(8,128)(2,1)} custom-call(s32[1,256]{1,0:T(1,128)} %slots_ref.3, bf16[256,2560]{1,0:T(8,128)(2,1)} %q_ref.3, bf16[256,1024]{1,0:T(8,128)(2,1)} %kv_ref.3), custom_call_target="tpu_custom_call" | custom-call | flops 1 | bytes 1 | tf_op jit(solution)/shard_map/pallas_call | solution.py:110
  24.4 26.2 %all-to-all-done = bf16[16,16,6272]{2,1,0:T(8,128)(2,1)S(1)} async-done(((bf16[16,16,6272]{2,1,0:T(8,128)(2,1)}), bf16[16,16,6272]{2,1,0:T(8,128)(2,1)S(1)}, u32[]{:S(2)}, u32[]{:S(2)}) %all-to-all-start) | async-done | bytes 3211296 | tf_op jit(solution)/shard_map/all_to_all | solution.py:596
  51.4 3.2 %collective-permute-done.1.rest_1_.sm = bf16[640,1280]{1,0:T(8,128)(2,1)} collective-permute-done((bf16[640,1280]{1,0:T(8,128)(2,1)}, bf16[640,1280]{1,0:T(8,128)(2,1)}, u32[]{:S(2)}, u32[]{:S(2)}) %collective-permute-start.1) | collective-permute-done | bytes 1638432 | tf_op jit(solution)/shard_map/ppermute | solution.py:590
  56.8 4.4 %all-to-all-start.1 = ((bf16[16,16,3584]{2,1,0:T(8,128)(2,1)}), bf16[16,16,3584]{2,1,0:T(8,128)(2,1)S(1)}, u32[]{:S(2)}, u32[]{:S(2)}) async-start(bf16[16,16,3584]{2,1,0:T(8,128)(2,1)} %bitcast.38), calls=%async_computation.1 | async-start | bytes 3670016 | tf_op jit(solution)/shard_map/all_to_all | solution.py:615
  62.9 2.8 %collective-permute-start.6 = (bf16[640,1280]{1,0:T(8,128)(2,1)}, bf16[640,1280]{1,0:T(8,128)(2,1)}, u32[]{:S(2)}, u32[]{:S(2)}) collective-permute-start(bf16[640,1280]{1,0:T(8,128)(2,1)} %collective-permute-done.1.rest_1_.sm), channel_id=1, source_target_pairs={{16,1},{1,16},{0,17},{17,0},{18,3},{3,18},{2,19},{19,2},{20,5},{5,... | collective-permute-start | bytes 4915208 | tf_op jit(solution)/shard_map/ppermute | solution.py:591
  67.0 6.8 %shard_map.131.rest_0_.own_p.own_ref = bf16[256,2560]{1,0:T(8,128)(2,1)} custom-call(s32[1,2]{1,0:T(1,128)} %lengths_ref.5, bf16[256,6272]{1,0:T(8,128)(2,1)} %bitcast.22, bf16[256,6272]{1,0:T(8,128)(2,1)} %bitcast.23, bf16[256,6272]{1,0:T(8,128)(2,1)} %bitcast.24), custom_call_target="tpu_custom_call" | custom-call | flops 1 | bytes 1 | tf_op jit(solution)/shard_map/pallas_call | solution.py:172
  75.5 10.7 %collective-permute-done.8 = f32[16,128]{1,0:T(8,128)S(1)} collective-permute-done((f32[16,128]{1,0:T(8,128)}, f32[16,128]{1,0:T(8,128)S(1)}, u32[]{:S(2)}, u32[]{:S(2)}) %collective-permute-start.8) | collective-permute-done | bytes 8224 | tf_op jit(solution)/shard_map/ppermute | solution.py:619
  90.0 6.8 %shard_map.135.own_r = bf16[256,2560]{1,0:T(8,128)(2,1)} custom-call(s32[1,2]{1,0:T(1,128)} %lengths_ref.5, bf16[256,3584]{1,0:T(8,128)(2,1)} %bitcast.35, bf16[256,3584]{1,0:T(8,128)(2,1)} %bitcast.36, bf16[256,3584]{1,0:T(8,128)(2,1)} %bitcast.37), custom_call_target="tpu_custom_call" | custom-call | flops 1 | bytes 1 | tf_op jit(solution)/shard_map/pallas_call | solution.py:172
  96.8 4.7 %collective-permute-done.11.two = f32[32,128]{1,0:T(8,128)S(1)} collective-permute-done((f32[32,128]{1,0:T(8,128)S(1)}, f32[32,128]{1,0:T(8,128)S(1)}, u32[]{:S(2)}, u32[]{:S(2)}) %collective-permute-start.11) | collective-permute-done | bytes 16416 | tf_op jit(solution)/shard_map/ppermute | solution.py:626
  112.5 14.6 %shard_map.137 = (f32[512,1280]{1,0:T(8,128)}, f32[512,1280]{1,0:T(8,128)}, bf16[512,384]{1,0:T(8,128)(2,1)}, bf16[512,384]{1,0:T(8,128)(2,1)}) custom-call(s32[5]{0:T(128)} %copy-done.9, bf16[256,2560]{1,0:T(8,128)(2,1)} %shard_map.131.rest_0_.own_p.own_ref, bf16[256,2560]{1,0:T(8,128)(2,1)} %collective-permute-done.other_p.other_ref, ...), custom_call_target="tpu_custom_call" | custom-call | flops 1 | bytes 1 | tf_op jit(solution)/shard_map/pallas_call | solution.py:274
  129.3 6.8 %shard_map.140 = (f32[512,1280]{1,0:T(8,128)}, f32[512,128]{1,0:T(8,128)}) custom-call(s32[5]{0:T(128)} %copy-done.9, bf16[512,384]{1,0:T(8,128)(2,1)} %get-tuple-element.29.rows_p, bf16[512,384]{1,0:T(8,128)(2,1)} %get-tuple-element.30.rows_r, bf16[320,1280]{1,0:T(8,128)(2,1)} %collective-permute-done.9.o2p, bf16[320,1280]{1,0:T(8,128)(2,1)} %copy-done.14, ...), custom_call_target="tpu_custom_call" | custom-call | flops 1677721600 | bytes 10485760 | tf_op jit(solution)/shard_map/pallas_call | solution.py:337
  138.6 9.8 %shard_map.141 = (bf16[640,640]{1,0:T(8,128)(2,1)}, bf16[640,640]{1,0:T(8,128)(2,1)}, bf16[640,640]{1,0:T(8,128)(2,1)}, bf16[640,640]{1,0:T(8,128)(2,1)}, bf16[8...) custom-call(s32[5]{0:T(128)} %copy-done.9, ...), custom_call_target="tpu_custom_call" | custom-call | flops 3355443200 | bytes 16777216 | tf_op jit(solution)/shard_map/pallas_call | solution.py:435
  156.1 14.0 %collective-permute-done.21.rest_0_ = bf16[8,80,640]{2,1,0:T(8,128)(2,1)S(1)} collective-permute-done((bf16[8,80,640]{2,1,0:T(8,128)(2,1)}, bf16[8,80,640]{2,1,0:T(8,128)(2,1)S(1)}, u32[]{:S(2)}, u32[]{:S(2)}) %collective-permute-start.21) | collective-permute-done | bytes 819232 | tf_op jit(solution)/shard_map/ppermute | solution.py:639
  173.0 16.6 %collective-permute-done.16 = bf16[640,640]{1,0:T(8,128)(2,1)} collective-permute-done((bf16[640,640]{1,0:T(8,128)(2,1)}, bf16[640,640]{1,0:T(8,128)(2,1)}, u32[]{:S(2)}, u32[]{:S(2)}) %collective-permute-start.16) | collective-permute-done | bytes 819232 | tf_op jit(solution)/shard_map/ppermute | solution.py:638
  199.4 2.9 %collective-permute-start.25 = (bf16[2,80,640]{2,1,0:T(8,128)(2,1)S(1)}, bf16[2,80,640]{2,1,0:T(8,128)(2,1)S(1)}, u32[]{:S(2)}, u32[]{:S(2)}) collective-permute-start(bf16[2,80,640]{2,1,0:T(8,128)(2,1)S(1)} %get-tuple-element.51), channel_id=1, source_target_pairs={{0,4},{2,6},{4,0},{6,2},{1,5},{3,7},{5,1},{7,3},{8,12},{10,14},{12... | collective-permute-start | bytes 614408 | tf_op jit(solution)/shard_map/ppermute | solution.py:645
  203.4 3.7 %collective-permute-start.26 = (bf16[2,80,640]{2,1,0:T(8,128)(2,1)S(1)}, bf16[2,80,640]{2,1,0:T(8,128)(2,1)S(1)}, u32[]{:S(2)}, u32[]{:S(2)}) collective-permute-start(bf16[2,80,640]{2,1,0:T(8,128)(2,1)S(1)} %get-tuple-element.52), channel_id=1, source_target_pairs={{0,6},{2,0},{4,2},{6,4},{1,7},{3,1},{5,3},{7,5},{8,14},{10,8},{12,... | collective-permute-start | bytes 614408 | tf_op jit(solution)/shard_map/ppermute | solution.py:645
  207.1 3.8 %collective-permute-done.25.refs_6_ = bf16[2,80,640]{2,1,0:T(8,128)(2,1)S(1)} collective-permute-done((bf16[2,80,640]{2,1,0:T(8,128)(2,1)S(1)}, bf16[2,80,640]{2,1,0:T(8,128)(2,1)S(1)}, u32[]{:S(2)}, u32[]{:S(2)}) %collective-permute-start.25) | collective-permute-done | bytes 204832 | tf_op jit(solution)/shard_map/ppermute | solution.py:645
  214.1 4.6 %collective-permute-done.27 = bf16[80,1280]{1,0:T(8,128)(2,1)S(1)} collective-permute-done((bf16[80,1280]{1,0:T(8,128)(2,1)S(1)}, bf16[80,1280]{1,0:T(8,128)(2,1)S(1)}, u32[]{:S(2)}, u32[]{:S(2)}) %collective-permute-start.27) | collective-permute-done | bytes 204832 | tf_op jit(solution)/shard_map/ppermute | solution.py:651
  218.9 5.7 %collective-permute-done.28 = bf16[80,1280]{1,0:T(8,128)(2,1)S(1)} collective-permute-done((bf16[80,1280]{1,0:T(8,128)(2,1)S(1)}, bf16[80,1280]{1,0:T(8,128)(2,1)S(1)}, u32[]{:S(2)}, u32[]{:S(2)}) %collective-permute-start.28) | collective-permute-done | bytes 204832 | tf_op jit(solution)/shard_map/ppermute | solution.py:652
  227.0 3.5 %collective-permute-done.29 = bf16[80,1280]{1,0:T(8,128)(2,1)S(1)} collective-permute-done((bf16[80,1280]{1,0:T(8,128)(2,1)S(1)}, bf16[80,1280]{1,0:T(8,128)(2,1)S(1)}, u32[]{:S(2)}, u32[]{:S(2)}) %collective-permute-start.29) | collective-permute-done | bytes 204832 | tf_op jit(solution)/shard_map/ppermute | solution.py:654
  249.8 4.2 %shard_map.147 = (f32[320,2560]{1,0:T(8,128)}, bf16[320,2560]{1,0:T(8,128)(2,1)}, f32[320,2560]{1,0:T(8,128)}) custom-call(s32[5]{0:T(128)S(1)} %copy-done.10, f32[8,128]{1,0:T(8,128)S(1)} %add_add_fusion.square_ref, bf16[4,80,1280]{2,1,0:T(8,128)(2,1)S(1)} %pad_maximum_fusion.1.mine_ref, bf16[4,80,1280]{2,1,0:T(8,128)(2,1)S(1)} %collective-permute-done.32.theirs_ref, ...), custom_call_target="tpu_custom_call" | custom-call | tf_op jit(solution)/shard_map/pallas_call | solution.py:548
  (113 shorter events, 80.8 us)
Async XLA Ops:
  5.2 45.4 %all-to-all-start = ((bf16[16,16,6272]{2,1,0:T(8,128)(2,1)}), bf16[16,16,6272]{2,1,0:T(8,128)(2,1)S(1)}, u32[]{:S(2)}, u32[]{:S(2)}) async-start(bf16[16,16,6272]{2,1,0:T(8,128)(2,1)} %bitcast.39), calls=%async_computation | async-start | bytes 6422528 | tf_op jit(solution)/shard_map/all_to_all | solution.py:596
  13.9 40.7 %collective-permute-start.1 = (bf16[640,1280]{1,0:T(8,128)(2,1)}, bf16[640,1280]{1,0:T(8,128)(2,1)}, u32[]{:S(2)}, u32[]{:S(2)}) collective-permute-start(bf16[640,1280]{1,0:T(8,128)(2,1)} %pad_maximum_fusion.w0), channel_id=1, source_target_pairs={{0,2},{2,4},{4,6},{6,0},{1,3},{3,5},{5,7},{7,1},{8,10},{10,12},{12... | collective-permute-start | bytes 4915208 | tf_op jit(solution)/shard_map/ppermute | solution.py:590
  15.8 39.4 %collective-permute-start.3 = (bf16[640,1280]{1,0:T(8,128)(2,1)}, bf16[640,1280]{1,0:T(8,128)(2,1)}, u32[]{:S(2)}, u32[]{:S(2)}) collective-permute-start(bf16[640,1280]{1,0:T(8,128)(2,1)} %pad_maximum_fusion.w0), channel_id=1, source_target_pairs={{16,1},{1,16},{0,17},{17,0},{18,3},{3,18},{2,19},{19,2},{20,5},{5,... | collective-permute-start | bytes 4915208 | tf_op jit(solution)/shard_map/ppermute | solution.py:590
  19.0 37.8 %collective-permute-start.2 = (bf16[640,1280]{1,0:T(8,128)(2,1)}, bf16[640,1280]{1,0:T(8,128)(2,1)}, u32[]{:S(2)}, u32[]{:S(2)}) collective-permute-start(bf16[640,1280]{1,0:T(8,128)(2,1)} %pad_maximum_fusion.w0), channel_id=1, source_target_pairs={{0,6},{2,0},{4,2},{6,4},{1,7},{3,1},{5,3},{7,5},{8,14},{10,8},{12,... | collective-permute-start | bytes 4915208 | tf_op jit(solution)/shard_map/ppermute | solution.py:590
  56.8 32.0 %all-to-all-start.1 = ((bf16[16,16,3584]{2,1,0:T(8,128)(2,1)}), bf16[16,16,3584]{2,1,0:T(8,128)(2,1)S(1)}, u32[]{:S(2)}, u32[]{:S(2)}) async-start(bf16[16,16,3584]{2,1,0:T(8,128)(2,1)} %bitcast.38), calls=%async_computation.1 | async-start | bytes 3670016 | tf_op jit(solution)/shard_map/all_to_all | solution.py:615
  61.1 40.3 %collective-permute-start.5 = (bf16[640,1280]{1,0:T(8,128)(2,1)}, bf16[640,1280]{1,0:T(8,128)(2,1)S(1)}, u32[]{:S(2)}, u32[]{:S(2)}) collective-permute-start(bf16[640,1280]{1,0:T(8,128)(2,1)} %collective-permute-done.1.rest_1_.sm), channel_id=1, source_target_pairs={{0,2},{2,4},{4,6},{6,0},{1,3},{3,5},{5,7},{7,1},{8,10},{10,12},{12... | collective-permute-start | bytes 4915208 | tf_op jit(solution)/shard_map/ppermute | solution.py:591
  62.9 40.4 %collective-permute-start.6 = (bf16[640,1280]{1,0:T(8,128)(2,1)}, bf16[640,1280]{1,0:T(8,128)(2,1)}, u32[]{:S(2)}, u32[]{:S(2)}) collective-permute-start(bf16[640,1280]{1,0:T(8,128)(2,1)} %collective-permute-done.1.rest_1_.sm), channel_id=1, source_target_pairs={{16,1},{1,16},{0,17},{17,0},{18,3},{3,18},{2,19},{19,2},{20,5},{5,... | collective-permute-start | bytes 4915208 | tf_op jit(solution)/shard_map/ppermute | solution.py:591
  65.7 46.8 %collective-permute-start.7 = (bf16[640,1280]{1,0:T(8,128)(2,1)}, bf16[640,1280]{1,0:T(8,128)(2,1)}, u32[]{:S(2)}, u32[]{:S(2)}) collective-permute-start(bf16[640,1280]{1,0:T(8,128)(2,1)} %collective-permute-done.3.rest_3_.o0), channel_id=1, source_target_pairs={{0,6},{2,0},{4,2},{6,4},{1,7},{3,1},{5,3},{7,5},{8,14},{10,8},{12,... | collective-permute-start | bytes 4915208 | tf_op jit(solution)/shard_map/ppermute | solution.py:591
  73.9 12.3 %collective-permute-start.8 = (f32[16,128]{1,0:T(8,128)}, f32[16,128]{1,0:T(8,128)S(1)}, u32[]{:S(2)}, u32[]{:S(2)}) collective-permute-start(f32[16,128]{1,0:T(8,128)} %shard_map.136), channel_id=1, source_target_pairs={{0,1},{1,0},{2,3},{3,2},{4,5},{5,4},{6,7},{7,6},{8,9},{9,8},{10,11... | collective-permute-start | bytes 24584 | tf_op jit(solution)/shard_map/ppermute | solution.py:619
  86.8 14.6 %collective-permute-start.11 = (f32[32,128]{1,0:T(8,128)S(1)}, f32[32,128]{1,0:T(8,128)S(1)}, u32[]{:S(2)}, u32[]{:S(2)}) collective-permute-start(f32[32,128]{1,0:T(8,128)S(1)} %pad_maximum_fusion.2.after.one), channel_id=1, source_target_pairs={{0,2},{2,4},{4,6},{6,0},{1,3},{3,5},{5,7},{7,1},{8,10},{10,12},{12... | collective-permute-start | bytes 49160 | tf_op jit(solution)/shard_map/ppermute | solution.py:626
  88.8 23.7 %collective-permute-start = (bf16[256,2560]{1,0:T(8,128)(2,1)}, bf16[256,2560]{1,0:T(8,128)(2,1)}, u32[]{:S(2)}, u32[]{:S(2)}) collective-permute-start(bf16[256,2560]{1,0:T(8,128)(2,1)} %shard_map.131.rest_0_.own_p.own_ref), channel_id=1, source_target_pairs={{0,8},{8,0},{1,9},{9,1},{2,10},{10,2},{3,11},{11,3},{4,12},{12,4},... | collective-permute-start | bytes 3932168 | tf_op jit(solution)/shard_map/ppermute | solution.py:617
  101.5 11.0 %collective-permute-start.4 = (bf16[256,2560]{1,0:T(8,128)(2,1)}, bf16[256,2560]{1,0:T(8,128)(2,1)}, u32[]{:S(2)}, u32[]{:S(2)}) collective-permute-start(bf16[256,2560]{1,0:T(8,128)(2,1)} %shard_map.135.own_r), channel_id=1, source_target_pairs={{0,8},{8,0},{1,9},{9,1},{2,10},{10,2},{3,11},{11,3},{4,12},{12,4},... | collective-permute-start | bytes 3932168 | tf_op jit(solution)/shard_map/ppermute | solution.py:628
  107.1 21.3 %collective-permute-start.10 = (bf16[320,1280]{1,0:T(8,128)(2,1)}, bf16[320,1280]{1,0:T(8,128)(2,1)S(1)}, u32[]{:S(2)}, u32[]{:S(2)}) collective-permute-start(bf16[320,1280]{1,0:T(8,128)(2,1)} %get-tuple-element.32), channel_id=1, source_target_pairs={{0,2},{2,4},{4,6},{6,0},{1,3},{3,5},{5,7},{7,1},{8,10},{10,12},{12... | collective-permute-start | bytes 2457608 | tf_op jit(solution)/shard_map/ppermute | solution.py:593
  107.9 21.3 %collective-permute-start.9 = (bf16[320,1280]{1,0:T(8,128)(2,1)}, bf16[320,1280]{1,0:T(8,128)(2,1)}, u32[]{:S(2)}, u32[]{:S(2)}) collective-permute-start(bf16[320,1280]{1,0:T(8,128)(2,1)} %get-tuple-element.31), channel_id=1, source_target_pairs={{16,1},{1,16},{0,17},{17,0},{18,3},{3,18},{2,19},{19,2},{20,5},{5,... | collective-permute-start | bytes 2457608 | tf_op jit(solution)/shard_map/ppermute | solution.py:593
  148.4 21.8 %collective-permute-start.21 = (bf16[8,80,640]{2,1,0:T(8,128)(2,1)}, bf16[8,80,640]{2,1,0:T(8,128)(2,1)S(1)}, u32[]{:S(2)}, u32[]{:S(2)}) collective-permute-start(bf16[8,80,640]{2,1,0:T(8,128)(2,1)} %get-tuple-element.46), channel_id=1, source_target_pairs={{0,32},{32,64},{64,96},{96,0},{1,33},{33,65},{65,97},{97,1},{2,34}... | collective-permute-start | bytes 2457608 | tf_op jit(solution)/shard_map/ppermute | solution.py:639
  150.1 22.9 %collective-permute-start.15 = (bf16[640,640]{1,0:T(8,128)(2,1)}, bf16[640,640]{1,0:T(8,128)(2,1)S(1)}, u32[]{:S(2)}, u32[]{:S(2)}) collective-permute-start(bf16[640,640]{1,0:T(8,128)(2,1)} %get-tuple-element.38), channel_id=1, source_target_pairs={{0,2},{2,4},{4,6},{6,0},{1,3},{3,5},{5,7},{7,1},{8,10},{10,12},{12... | collective-permute-start | bytes 2457608 | tf_op jit(solution)/shard_map/ppermute | solution.py:638
  151.0 38.6 %collective-permute-start.16 = (bf16[640,640]{1,0:T(8,128)(2,1)}, bf16[640,640]{1,0:T(8,128)(2,1)}, u32[]{:S(2)}, u32[]{:S(2)}) collective-permute-start(bf16[640,640]{1,0:T(8,128)(2,1)} %get-tuple-element.39), channel_id=1, source_target_pairs={{0,4},{2,6},{4,0},{6,2},{1,5},{3,7},{5,1},{7,3},{8,12},{10,14},{12... | collective-permute-start | bytes 2457608 | tf_op jit(solution)/shard_map/ppermute | solution.py:638
  153.8 36.0 %collective-permute-start.17 = (bf16[640,640]{1,0:T(8,128)(2,1)}, bf16[640,640]{1,0:T(8,128)(2,1)}, u32[]{:S(2)}, u32[]{:S(2)}) collective-permute-start(bf16[640,640]{1,0:T(8,128)(2,1)} %get-tuple-element.40), channel_id=1, source_target_pairs={{0,6},{2,0},{4,2},{6,4},{1,7},{3,1},{5,3},{7,5},{8,14},{10,8},{12,... | collective-permute-start | bytes 2457608 | tf_op jit(solution)/shard_map/ppermute | solution.py:638
  154.6 42.6 %collective-permute-start.23 = (bf16[8,80,640]{2,1,0:T(8,128)(2,1)}, bf16[8,80,640]{2,1,0:T(8,128)(2,1)S(1)}, u32[]{:S(2)}, u32[]{:S(2)}) collective-permute-start(bf16[8,80,640]{2,1,0:T(8,128)(2,1)} %get-tuple-element.48), channel_id=1, source_target_pairs={{0,96},{32,0},{64,32},{96,64},{1,97},{33,1},{65,33},{97,65},{2,98}... | collective-permute-start | bytes 2457608 | tf_op jit(solution)/shard_map/ppermute | solution.py:641
  171.1 26.1 %collective-permute-start.22 = (bf16[8,80,640]{2,1,0:T(8,128)(2,1)}, bf16[8,80,640]{2,1,0:T(8,128)(2,1)S(1)}, u32[]{:S(2)}, u32[]{:S(2)}) collective-permute-start(bf16[8,80,640]{2,1,0:T(8,128)(2,1)} %shard_map.143), channel_id=1, source_target_pairs={{0,64},{32,96},{64,0},{96,32},{1,65},{33,97},{65,1},{97,33},{2,66}... | collective-permute-start | bytes 2457608 | tf_op jit(solution)/shard_map/ppermute | solution.py:640
  191.8 11.6 %collective-permute-start.18 = (bf16[2,80,640]{2,1,0:T(8,128)(2,1)S(1)}, bf16[2,80,640]{2,1,0:T(8,128)(2,1)S(1)}, u32[]{:S(2)}, u32[]{:S(2)}) collective-permute-start(bf16[2,80,640]{2,1,0:T(8,128)(2,1)S(1)} %get-tuple-element.42), channel_id=1, source_target_pairs={{0,32},{32,64},{64,96},{96,0},{1,33},{33,65},{65,97},{97,1},{2,34}... | collective-permute-start | bytes 614408 | tf_op jit(solution)/shard_map/ppermute | solution.py:644
  193.3 13.8 %collective-permute-start.19 = (bf16[2,80,640]{2,1,0:T(8,128)(2,1)S(1)}, bf16[2,80,640]{2,1,0:T(8,128)(2,1)S(1)}, u32[]{:S(2)}, u32[]{:S(2)}) collective-permute-start(bf16[2,80,640]{2,1,0:T(8,128)(2,1)S(1)} %get-tuple-element.43), channel_id=1, source_target_pairs={{0,64},{32,96},{64,0},{96,32},{1,65},{33,97},{65,1},{97,33},{2,66}... | collective-permute-start | bytes 614408 | tf_op jit(solution)/shard_map/ppermute | solution.py:644
  194.9 12.2 %collective-permute-start.20 = (bf16[2,80,640]{2,1,0:T(8,128)(2,1)S(1)}, bf16[2,80,640]{2,1,0:T(8,128)(2,1)S(1)}, u32[]{:S(2)}, u32[]{:S(2)}) collective-permute-start(bf16[2,80,640]{2,1,0:T(8,128)(2,1)S(1)} %get-tuple-element.44), channel_id=1, source_target_pairs={{0,96},{32,0},{64,32},{96,64},{1,97},{33,1},{65,33},{97,65},{2,98}... | collective-permute-start | bytes 614408 | tf_op jit(solution)/shard_map/ppermute | solution.py:644
  199.4 11.4 %collective-permute-start.25 = (bf16[2,80,640]{2,1,0:T(8,128)(2,1)S(1)}, bf16[2,80,640]{2,1,0:T(8,128)(2,1)S(1)}, u32[]{:S(2)}, u32[]{:S(2)}) collective-permute-start(bf16[2,80,640]{2,1,0:T(8,128)(2,1)S(1)} %get-tuple-element.51), channel_id=1, source_target_pairs={{0,4},{2,6},{4,0},{6,2},{1,5},{3,7},{5,1},{7,3},{8,12},{10,14},{12... | collective-permute-start | bytes 614408 | tf_op jit(solution)/shard_map/ppermute | solution.py:645
  (31 other events, 275.3 us)
